TPU v7x, 128 devices: a whole 4x4x4 slice. The times are simulated.
128 devices in a mesh: dp: 16 (over y, x), expert: 8 (over z, core).
Axes of the slice: x: 4, y: 4, z: 4, core: 2. Of those that a mesh axis runs over, the one named last changes fastest.
Arguments:
- layer_input: bfloat16 [4096, 2048], P(('dp', 'expert')), may hold values from -6 to 6
- out_grad: bfloat16 [4096, 2048], P(('dp', 'expert')), may hold values from -3 to 3
- routes: int32 [4096, 8], P(('dp', 'expert')), may hold values from 0 to 15, all different within a row
- probs: bfloat16 [4096, 8], P(('dp', 'expert')), may hold values from 0.049804688 to 1
- gate_up: bfloat16 [2048, 2, 16, 768], P(None, None, 'expert'), may hold values from -0.125 to 0.125
- down_t: bfloat16 [2048, 16, 768], P(None, 'expert'), may hold values from -0.21875 to 0.21875
Outputs:
- grad_input: bfloat16 [4096, 2048], P(('dp', 'expert'))
- grad_prob: float32 [4096, 8], P(('dp', 'expert'))
- grad_weights: bfloat16 [2048, 3, 16, 768], P('dp', None, 'expert')
Inputs may be any that keep to these rules, and one draw needn't show every extreme that they name: `routes`: each row names 8 different experts.
All inputs are finite; a program needn't handle non-finite values. Where the computation divides by a largest or mean magnitude, that divisor is 1e-20 or more.
Results may differ from a plain program's by a relative error of at most 0.02.
Values may be sent and summed in bfloat16 or wider, within the bound.
No kernel may reach another device: no remote copies, remote signals or barrier semaphores. Data moves between devices by JAX's collectives and lax.ppermute only.
A program may use at most 256 MiB of HBM per device.

v0:
```python
import jax
import jax.numpy as jnp
from jax import lax
from jax.sharding import PartitionSpec as P

BLOCK = 128


def slot_ranks(flat_routes, experts):
    onehot = (flat_routes[:, None] == jnp.arange(experts, dtype=jnp.int32)[None, :]).astype(
        jnp.int32
    )
    before = jnp.cumsum(onehot, axis=0) - onehot
    return (jnp.sum(before * onehot, axis=1), onehot)


def expert_math(rows_x, rows_dy, rows_p, gate_up, down_t, block_width):
    weight_gate = gate_up[:, 0]
    weight_up = gate_up[:, 1]
    gate_pre = jnp.einsum("esd,def->esf", rows_x, weight_gate, preferred_element_type=jnp.float32)
    up_pre = jnp.einsum("esd,def->esf", rows_x, weight_up, preferred_element_type=jnp.float32)
    sigmoid_gate = jax.nn.sigmoid(gate_pre)
    activated = gate_pre * sigmoid_gate
    hidden = (activated * up_pre).astype(jnp.bfloat16)
    back_proj = jnp.einsum("esd,def->esf", rows_dy, down_t, preferred_element_type=jnp.float32)
    expert_out = jnp.einsum("esf,def->esd", hidden, down_t, preferred_element_type=jnp.float32)
    prob_grad = jnp.sum(rows_dy.astype(jnp.float32) * expert_out, axis=-1)
    weight_p = rows_p.astype(jnp.float32)[..., None]
    hidden_grad = weight_p * back_proj
    scaled = (weight_p * rows_dy.astype(jnp.float32)).astype(jnp.bfloat16)
    gate_grad = (
        hidden_grad * up_pre * sigmoid_gate * (1.0 + gate_pre * (1.0 - sigmoid_gate))
    ).astype(jnp.bfloat16)
    up_grad = (hidden_grad * activated).astype(jnp.bfloat16)
    slot_grad = jnp.einsum(
        "esf,def->esd", gate_grad, weight_gate, preferred_element_type=jnp.float32
    )
    slot_grad = slot_grad + jnp.einsum(
        "esf,def->esd", up_grad, weight_up, preferred_element_type=jnp.float32
    )
    local, span, width = slot_grad.shape
    blocks = slot_grad.reshape(local, span, width // block_width, block_width)
    block_scale = jnp.max(jnp.abs(blocks), axis=-1) + 1e-06
    packed = (blocks / block_scale[..., None]).astype(jnp.bfloat16).reshape(local, span, width)
    return (packed, block_scale, prob_grad, scaled, gate_grad, up_grad, hidden)


def stack_terms(cols_x, cols_scaled, gate_grad, up_grad, hidden):
    term_gate = jnp.einsum("esd,esf->def", cols_x, gate_grad, preferred_element_type=jnp.float32)
    term_up = jnp.einsum("esd,esf->def", cols_x, up_grad, preferred_element_type=jnp.float32)
    term_down = jnp.einsum("esd,esf->def", cols_scaled, hidden, preferred_element_type=jnp.float32)
    return jnp.stack([term_gate, term_up, term_down], axis=1)


def shards(layer_input, out_grad, routes, probs, gate_up, down_t):
    tokens, width = layer_input.shape
    top_k = routes.shape[1]
    local = gate_up.shape[2]
    groups = lax.axis_size("expert")
    experts = local * groups
    flat_routes = routes.reshape(-1)
    ranks, onehot = slot_ranks(flat_routes, experts)
    flat_probs = probs.reshape(-1)
    slots = flat_routes * tokens + ranks
    sentinel = tokens * top_k
    owner = (
        jnp.full((experts * tokens,), sentinel, jnp.int32)
        .at[slots]
        .set(jnp.arange(sentinel, dtype=jnp.int32))
    )
    source = owner // top_k
    padded_input = jnp.concatenate([layer_input, jnp.zeros((1, width), layer_input.dtype)], axis=0)
    padded_grad = jnp.concatenate([out_grad, jnp.zeros((1, width), out_grad.dtype)], axis=0)
    padded_probs = jnp.concatenate([flat_probs, jnp.zeros((1,), probs.dtype)], axis=0)
    send_input = padded_input[source].reshape(experts, tokens, width)
    send_grad = padded_grad[source].reshape(experts, tokens, width)
    send_probs = padded_probs[owner].reshape(experts, tokens)
    rows_x, rows_dy, rows_p = (
        lax.all_to_all(send_input, "expert", split_axis=0, concat_axis=1, tiled=True),
        lax.all_to_all(send_grad, "expert", split_axis=0, concat_axis=1, tiled=True),
        lax.all_to_all(send_probs, "expert", split_axis=0, concat_axis=1, tiled=True),
    )
    block_width = BLOCK
    packed, block_scale, prob_grad, scaled, gate_grad, up_grad, hidden = expert_math(
        rows_x, rows_dy, rows_p, gate_up, down_t, block_width
    )
    back_rows = lax.all_to_all(packed, "expert", split_axis=1, concat_axis=0, tiled=True)
    back_scale, back_prob = (
        lax.all_to_all(
            block_scale.astype(jnp.bfloat16), "expert", split_axis=1, concat_axis=0, tiled=True
        ).astype(block_scale.dtype),
        lax.all_to_all(
            prob_grad.astype(jnp.bfloat16), "expert", split_axis=1, concat_axis=0, tiled=True
        ).astype(prob_grad.dtype),
    )
    block_count = back_scale.shape[2]
    picked = back_rows.reshape(experts * tokens, width)[slots].astype(jnp.float32)
    scales = back_scale.reshape(experts * tokens, block_count)[slots]
    restored = (
        picked.reshape(tokens * top_k, block_count, width // block_count) * scales[:, :, None]
    ).reshape(tokens, top_k, width)
    grad_input = jnp.sum(restored, axis=1).astype(jnp.bfloat16)
    grad_prob = back_prob.reshape(experts * tokens)[slots].reshape(tokens, top_k)
    total = lax.psum_scatter(
        stack_terms(rows_x, scaled, gate_grad, up_grad, hidden).astype(jnp.bfloat16),
        "dp",
        scatter_dimension=0,
        tiled=True,
    )
    return (grad_input, grad_prob, total)


def solution(mesh):
    placed = (
        P(("dp", "expert"), None),
        P(("dp", "expert"), None),
        P(("dp", "expert"), None),
        P(("dp", "expert"), None),
        P(None, None, "expert", None),
        P(None, "expert", None),
    )
    return jax.shard_map(
        shards,
        mesh=mesh,
        in_specs=placed,
        out_specs=(
            P(("dp", "expert"), None),
            P(("dp", "expert"), None),
            P("dp", None, "expert", None),
        ),
        check_vma=False,
    )
```

profile of v0, /device:TPU:0, one launch (start us, length us, event | category | flops | bytes accessed | tf_op | source)
XLA Modules:
  0.0 270.0 jit_solution(540105077011287149)
XLA Ops:
  12.2 3.5 %gather_fusion = bf16[512]{0:T(512)(128)(2,1)S(1)} fusion(bf16[257]{0:T(512)(128)(2,1)S(1)} %pad_maximum_fusion.1, s32[1024]{0:T(1024)S(1)} %get-tuple-element.30), kind=kCustom, calls=%fused_computation | custom fusion | bytes 4096 | tf_op jit(solution)/shard_map/gather | solution.py:77
  16.4 5.4 %all-to-all-start = ((bf16[8,2,32]{2,1,0:T(2,128)(2,1)}), bf16[8,2,32]{2,1,0:T(2,128)(2,1)S(1)}, u32[]{:S(2)}, u32[]{:S(2)}) async-start(bf16[8,2,32]{2,1,0:T(2,128)(2,1)} %all_to_all.62), calls=%async_computation | async-start | bytes 8192 | tf_op jit(solution)/shard_map/all_to_all | solution.py:81
  22.7 3.3 %gather_fusion.1 = bf16[512,2048]{1,0:T(8,128)(2,1)} fusion(bf16[33,2048]{1,0:T(8,128)(2,1)S(1)} %concatenate.10, s32[1024]{0:T(1024)S(1)} %get-tuple-element.29), kind=kCustom, calls=%fused_computation.1 | custom fusion | bytes 4196352 | tf_op jit(solution)/shard_map/gather | solution.py:76
  27.0 4.0 %all-to-all-start.1 = ((bf16[16,32,2048]{2,1,0:T(8,128)(2,1)}), bf16[16,32,2048]{2,1,0:T(8,128)(2,1)S(1)}, u32[]{:S(2)}, u32[]{:S(2)}) async-start(bf16[16,32,2048]{2,1,0:T(8,128)(2,1)} %bitcast.4), calls=%async_computation.1 | async-start | bytes 4194304 | tf_op jit(solution)/shard_map/all_to_all | solution.py:80
  31.0 3.4 %gather_fusion.2 = bf16[512,2048]{1,0:T(8,128)(2,1)} fusion(bf16[33,2048]{1,0:T(8,128)(2,1)S(1)} %concatenate.11, s32[1024]{0:T(1024)S(1)} %get-tuple-element.29), kind=kCustom, calls=%fused_computation.2 | custom fusion | bytes 4196352 | tf_op jit(solution)/shard_map/gather | solution.py:75
  34.4 23.8 %all-to-all-done.1 = bf16[16,32,2048]{2,1,0:T(8,128)(2,1)S(1)} async-done(((bf16[16,32,2048]{2,1,0:T(8,128)(2,1)}), bf16[16,32,2048]{2,1,0:T(8,128)(2,1)S(1)}, u32[]{:S(2)}, u32[]{:S(2)}) %all-to-all-start.1) | async-done | bytes 2097184 | tf_op jit(solution)/shard_map/all_to_all | solution.py:80
  58.2 4.3 %all-to-all-start.2 = ((bf16[16,32,2048]{2,1,0:T(8,128)(2,1)}), bf16[16,32,2048]{2,1,0:T(8,128)(2,1)}, u32[]{:S(2)}, u32[]{:S(2)}) async-start(bf16[16,32,2048]{2,1,0:T(8,128)(2,1)} %bitcast.8), calls=%async_computation.2 | async-start | bytes 4194304 | tf_op jit(solution)/shard_map/all_to_all | solution.py:79
  62.8 11.6 %fusion.26 = (bf16[2048,1,2,768]{3,2,1,0:T(2,128)(2,1)}, bf16[2048,1,2,768]{3,2,1,0:T(2,128)(2,1)}) fusion(bf16[2048,2,2,768]{3,2,1,0:T(2,128)(2,1)} %param.10), kind=kLoop, calls=%fused_computation.66 | loop fusion | bytes 25165824 | tf_op jit(solution)/shard_map/slice | solution.py:19
  76.0 13.8 %all-to-all-done.2 = bf16[16,32,2048]{2,1,0:T(8,128)(2,1)} async-done(((bf16[16,32,2048]{2,1,0:T(8,128)(2,1)}), bf16[16,32,2048]{2,1,0:T(8,128)(2,1)}, u32[]{:S(2)}, u32[]{:S(2)}) %all-to-all-start.2) | async-done | bytes 2097184 | tf_op jit(solution)/shard_map/all_to_all | solution.py:79
  91.6 4.7 %fusion.6 = f32[2,256,768]{2,1,0:T(8,128)S(1)} fusion(bf16[2,256,2048]{2,1,0:T(8,128)(2,1)S(1)} %bitcast.109, bf16[2048,2,768]{2,1,0:T(2,128)(2,1)} %param.11), kind=kOutput, calls=%fused_computation.19 | convolution fusion | flops 1610612736 | bytes 9961472 | tf_op jit(solution)/shard_map/esd,def->esf/dot_general | solution.py:25
  98.3 3.0 %multiply_convert_fusion.2 = (bf16[2,256,768]{2,1,0:T(8,128)(2,1)S(1)}, bf16[2,256,768]{2,1,0:T(8,128)(2,1)S(1)}, bf16[2,256,768]{2,1,0:T(8,128)(2,1)S(1)}) fusion(f32[2,256,768]{2,1,0:T(8,128)S(1)} %fusion.1, f32[2,256,768]{2,1,0:T(8,128)S(1)} %fusion.6, f32[2,256]{1,0:T(2,128)S(1)} %reshape.116, bf16[2,256,2048]{2,1,0:T(8,128)(2,1)S(1)} %bitcast.102, ...), kind=kOutput, calls=%fused_computation.33 | convolution fusion | flops 1616904192 | bytes 13895680 | tf_op jit(solution)/shard_map/esd,def->esf/dot_general | solution.py:20
  101.3 1.9 convert_bitcast_fusion
  107.0 8.2 %pad_maximum_fusion = bf16[2048,3,2,768]{0,3,2,1:T(8,128)(2,1)} fusion(bf16[2048,1,2,768]{0,3,2,1:T(8,128)(2,1)S(1)} %convert_bitcast_fusion, bf16[2048,1,2,768]{0,3,2,1:T(8,128)(2,1)S(1)} %convert_bitcast_fusion.1, bf16[2048,1,2,768]{0,3,2,1:T(8,128)(2,1)S(1)} %convert_bitcast_fusion.2), kind=kLoop, calls=%fused_computation.7 | loop fusion | flops 18874368 | bytes 37748736 | tf_op jit(solution)/shard_map/stack | solution.py:52
  115.2 22.7 %copy.111 = bf16[2048,4608]{1,0:T(8,128)(2,1)} copy(bf16[2048,4608]{0,1:T(8,128)(2,1)} %bitcast.97) | data formatting | bytes 37748736
  137.9 4.9 %fusion = f32[2,256,2048]{2,1,0:T(8,128)S(1)} fusion(bf16[2,256,768]{2,1,0:T(8,128)(2,1)} %copy-done.5, bf16[2048,1,2,768]{3,2,1,0:T(2,128)(2,1)} %get-tuple-element.18), kind=kOutput, calls=%fused_computation.13 | convolution fusion | flops 1610612736 | bytes 11272192 | tf_op jit(solution)/shard_map/esf,def->esd/dot_general | solution.py:38
  142.8 6.9 %fusion.27 = (f32[2,256,2048]{2,1,0:T(8,128)S(1)}, f32[2,256,2048]{2,1,0:T(8,128)}) fusion(f32[2,256,2048]{2,1,0:T(8,128)S(1)} %fusion, bf16[2,256,768]{2,1,0:T(8,128)(2,1)S(1)} %get-tuple-element.20, bf16[2048,1,2,768]{3,2,1,0:T(2,128)(2,1)} %get-tuple-element.19), kind=kOutput, calls=%fused_computation.67 | convolution fusion | flops 1612709888 | bytes 19660800 | tf_op jit(solution)/shard_map/esf,def->esd/dot_general | solution.py:35
  151.9 4.8 %fusion.8 = bf16[2,256]{1,0:T(2,128)(2,1)S(1)} fusion(bf16[2,256,2048]{2,1,0:T(8,128)(2,1)S(1)} %bitcast.111, bf16[2,256,768]{2,1,0:T(8,128)(2,1)S(1)} %copy-done.4, bf16[2048,2,768]{2,1,0:T(2,128)(2,1)} %param.11), kind=kOutput, calls=%fused_computation.23 | convolution fusion | flops 1613757952 | bytes 9176064 | tf_op jit(solution)/shard_map/esf,def->esd/dot_general | solution.py:26
  157.4 3.3 %all-to-all-start.5 = ((bf16[2,8,32]{2,0,1:T(2,128)(2,1)}), bf16[2,8,32]{2,0,1:T(2,128)(2,1)S(1)}, u32[]{:S(2)}, u32[]{:S(2)}) async-start(bf16[2,8,32]{2,0,1:T(2,128)(2,1)} %copy.100), calls=%async_computation.5 | async-start | bytes 8192 | tf_op jit(solution)/shard_map/all_to_all | solution.py:92
  161.8 2.7 div.31
  164.4 5.1 %div.32 = f32[2,256,2048]{2,1,0:T(8,128)} reshape(f32[2,256,16,128]{3,2,1,0:T(8,128)} %div.31) | data formatting | bytes 8388608 | tf_op jit(solution)/shard_map/div | solution.py:44
  169.5 4.7 %all-to-all-start.4 = ((bf16[8,2,512]{2,1,0:T(2,128)(2,1)}), bf16[8,2,512]{2,1,0:T(2,128)(2,1)S(1)}, u32[]{:S(2)}, u32[]{:S(2)}) async-start(bf16[8,2,512]{2,1,0:T(2,128)(2,1)} %reshape.185), calls=%async_computation.4 | async-start | bytes 32768 | tf_op jit(solution)/shard_map/all_to_all | solution.py:89
  174.2 4.4 %divide_convert_fusion = bf16[2,256,2048]{2,1,0:T(8,128)(2,1)S(1)} fusion(f32[2,256,2048]{2,1,0:T(8,128)} %get-tuple-element.28, f32[2,256,2048]{2,1,0:T(8,128)} %div.32), kind=kLoop, calls=%fused_computation.26 | loop fusion | flops 2097152 | bytes 10485760 | tf_op jit(solution)/shard_map/convert_element_type | solution.py:44
  178.6 3.5 %copy.94 = bf16[2,256,2048]{2,0,1:T(2,128)(2,1)} copy(bf16[2,256,2048]{2,1,0:T(8,128)(2,1)S(1)} %divide_convert_fusion) | data formatting | bytes 4194304 | tf_op jit(solution)/shard_map/convert_element_type | solution.py:44
  182.1 4.8 %all-to-all-start.3 = ((bf16[2,256,2048]{2,0,1:T(2,128)(2,1)}), bf16[2,256,2048]{2,0,1:T(2,128)(2,1)S(1)}, u32[]{:S(2)}, u32[]{:S(2)}) async-start(bf16[2,256,2048]{2,0,1:T(2,128)(2,1)} %copy.94), calls=%async_computation.3 | async-start | bytes 4194304 | tf_op jit(solution)/shard_map/all_to_all | solution.py:87
  187.0 1.9 gather_fusion.5
  190.9 2.0 mul.82
  192.9 2.8 %mul.83 = f32[32,8,2048]{2,1,0:T(8,128)} reshape(f32[256,16,128]{2,1,0:T(8,128)} %mul.82) | data formatting | bytes 4194304 | tf_op jit(solution)/shard_map/mul | solution.py:100
  195.6 18.5 %all-to-all-done.3 = bf16[2,256,2048]{2,0,1:T(2,128)(2,1)S(1)} async-done(((bf16[2,256,2048]{2,0,1:T(2,128)(2,1)}), bf16[2,256,2048]{2,0,1:T(2,128)(2,1)S(1)}, u32[]{:S(2)}, u32[]{:S(2)}) %all-to-all-start.3) | async-done | bytes 2097184 | tf_op jit(solution)/shard_map/all_to_all | solution.py:87
  215.4 2.5 copy.95
  219.3 3.1 %fusion.14 = bf16[32,2048]{1,0:T(8,128)(2,1)} fusion(f32[32,8,2048]{2,1,0:T(8,128)} %mul.83, bf16[256,2048]{1,0:T(8,128)(2,1)S(1)} %gather_fusion.3), kind=kLoop, calls=%fused_computation.29 | loop fusion | flops 1507328 | bytes 3276800 | tf_op jit(solution)/shard_map/reduce_sum | solution.py:102
  222.4 36.3 %reduce-scatter.4.cloned.1.call-done = bf16[128,4608]{1,0:T(8,128)(2,1)} async-done(((bf16[2048,4608]{1,0:T(8,128)(2,1)}), bf16[128,4608]{1,0:T(8,128)(2,1)}) %reduce-scatter.4.cloned.1.call-update) | async-done | bytes 1179664
  260.3 2.8 %copy.105 = bf16[128,3,2,768]{3,2,1,0:T(2,128)(2,1)} copy(bf16[128,3,2,768]{0,3,2,1:T(8,128)(2,1)S(1)} %bitcast.113) | data formatting | bytes 2359296
  (76 shorter events, 27.1 us)
Async XLA Ops:
  16.4 10.6 %all-to-all-start = ((bf16[8,2,32]{2,1,0:T(2,128)(2,1)}), bf16[8,2,32]{2,1,0:T(2,128)(2,1)S(1)}, u32[]{:S(2)}, u32[]{:S(2)}) async-start(bf16[8,2,32]{2,1,0:T(2,128)(2,1)} %all_to_all.62), calls=%async_computation | async-start | bytes 8192 | tf_op jit(solution)/shard_map/all_to_all | solution.py:81
  26.0 4.9 %copy-start.6 = (bf16[32,2048]{1,0:T(8,128)(2,1)S(1)}, bf16[32,2048]{1,0:T(8,128)(2,1)}, u32[]{:S(2)}) copy-start(bf16[32,2048]{1,0:T(8,128)(2,1)} %param.6) | copy-start | bytes 393220
  27.0 31.2 %all-to-all-start.1 = ((bf16[16,32,2048]{2,1,0:T(8,128)(2,1)}), bf16[16,32,2048]{2,1,0:T(8,128)(2,1)S(1)}, u32[]{:S(2)}, u32[]{:S(2)}) async-start(bf16[16,32,2048]{2,1,0:T(8,128)(2,1)} %bitcast.4), calls=%async_computation.1 | async-start | bytes 4194304 | tf_op jit(solution)/shard_map/all_to_all | solution.py:80
  58.2 31.6 %all-to-all-start.2 = ((bf16[16,32,2048]{2,1,0:T(8,128)(2,1)}), bf16[16,32,2048]{2,1,0:T(8,128)(2,1)}, u32[]{:S(2)}, u32[]{:S(2)}) async-start(bf16[16,32,2048]{2,1,0:T(8,128)(2,1)} %bitcast.8), calls=%async_computation.2 | async-start | bytes 4194304 | tf_op jit(solution)/shard_map/all_to_all | solution.py:79
  62.5 196.1 %reduce-scatter.4.cloned.1.call-start = ((), (), s32[]{:S(2)}) async-start(), calls=%async_computation.7 | async-start | bytes 20054016
  76.0 15.6 %copy-start.1 = (bf16[2,8,32,2048]{3,2,1,0:T(8,128)(2,1)S(1)}, bf16[2,8,32,2048]{3,2,1,0:T(8,128)(2,1)}, u32[]{:S(2)}) copy-start(bf16[2,8,32,2048]{3,2,1,0:T(8,128)(2,1)} %copy.87) | copy-start | bytes 6291460
  91.6 4.8 %copy-start.2 = (bf16[2048,1,2,768]{3,2,1,0:T(2,128)(2,1)S(1)}, bf16[2048,1,2,768]{3,2,1,0:T(2,128)(2,1)}, u32[]{:S(2)}) copy-start(bf16[2048,1,2,768]{3,2,1,0:T(2,128)(2,1)} %get-tuple-element.18) | copy-start | bytes 18874372
  91.6 6.6 %slice-start = ((s8[6291456]{0:T(1024)(128)(4,1)}), s8[4194304]{0:T(1024)(128)(4,1)S(1)}, s32[]{:S(2)}) async-start(s8[6291456]{0:T(1024)(128)(4,1)} %bitcast.99), calls=%async_computation.8 | async-start | bytes 8388608
  96.3 1.9 slice-start.1
  101.3 2.0 copy-start.3
  101.3 3.8 %copy-start.5 = (bf16[2,256,768]{2,1,0:T(8,128)(2,1)}, bf16[2,256,768]{2,1,0:T(8,128)(2,1)S(1)}, u32[]{:S(2)}) copy-start(bf16[2,256,768]{2,1,0:T(8,128)(2,1)S(1)} %get-tuple-element.21) | copy-start | bytes 2359300
  150.6 1.3 copy-start.4
  157.4 12.1 %all-to-all-start.5 = ((bf16[2,8,32]{2,0,1:T(2,128)(2,1)}), bf16[2,8,32]{2,0,1:T(2,128)(2,1)S(1)}, u32[]{:S(2)}, u32[]{:S(2)}) async-start(bf16[2,8,32]{2,0,1:T(2,128)(2,1)} %copy.100), calls=%async_computation.5 | async-start | bytes 8192 | tf_op jit(solution)/shard_map/all_to_all | solution.py:92
  169.5 12.6 %all-to-all-start.4 = ((bf16[8,2,512]{2,1,0:T(2,128)(2,1)}), bf16[8,2,512]{2,1,0:T(2,128)(2,1)S(1)}, u32[]{:S(2)}, u32[]{:S(2)}) async-start(bf16[8,2,512]{2,1,0:T(2,128)(2,1)} %reshape.185), calls=%async_computation.4 | async-start | bytes 32768 | tf_op jit(solution)/shard_map/all_to_all | solution.py:89
  182.1 32.0 %all-to-all-start.3 = ((bf16[2,256,2048]{2,0,1:T(2,128)(2,1)}), bf16[2,256,2048]{2,0,1:T(2,128)(2,1)S(1)}, u32[]{:S(2)}, u32[]{:S(2)}) async-start(bf16[2,256,2048]{2,0,1:T(2,128)(2,1)} %copy.94), calls=%async_computation.3 | async-start | bytes 4194304 | tf_op jit(solution)/shard_map/all_to_all | solution.py:87
  214.1 1.3 copy-start
Sparse Core Ops, SparseCore 0:
  138.0 120.5 reduce-scatter.3
where the time goes:
time: 272 us; the launch traced here: 270 us
  waiting for transfers between devices  93.3 us (34%)
  local copies, waits for them, and re-layouts  85.3 us (31%)
  matrix products  31.9 us (12%)
  starting transfers between devices  26.8 us (10%)
  other arithmetic  18.3 us (7%)
  between operations  14.4 us (5%)
    unnamed x2, waiting for transfers between devices  36.3 us
    unnamed x27, local copies, waits for them, and re-layouts  32.5 us
    all_to_all x1, waiting for transfers between devices, shards(): lax.all_to_all(send_grad, 'expert', split_axis=0, concat_axis=1, tiled=True)  23.8 us
    all_to_all x1, waiting for transfers between devices, shards(): lax.all_to_all(packed, 'expert', split_axis=1, concat_axis=0, tiled=True)  18.5 us
    all_to_all x1, waiting for transfers between devices, shards(): lax.all_to_all(send_input, 'expert', split_axis=0, concat_axis=1, tiled=T...  13.8 us
    slice x1, local copies, waits for them, and re-layouts, expert_math(): weight_up = gate_up[:, 1]  11.6 us
    another operation x1, other arithmetic, stack_terms(): return jnp.stack([term_gate, term_up, term_down], axis=1)  8.19 us
    div x2, local copies, waits for them, and re-layouts, expert_math(): blocks / block_scale[..., None]  7.74 us
  transfers between devices with their start and end apart: 7, of which 5 were waited for; matrix products, arithmetic and copies ran while one was open for 27% of the time, Pallas kernels for 0%

commit v1 on v0

v1 whole, which is shorter than its diff:
```python
import functools

import jax
import jax.numpy as jnp
import numpy as np
from jax import lax
from jax.experimental import pallas as pl
from jax.experimental.pallas import tpu as pltpu
from jax.sharding import Mesh, PartitionSpec as P

F32 = jnp.float32
BF16 = jnp.bfloat16
LANES = 128
SIDE = 4
VMEM = 48 << 20

XOR = {k: [(j, j ^ k) for j in range(SIDE)] for k in (1, 2, 3)}
RIGHT = [(j, (j + 1) % SIDE) for j in range(SIDE)]
LEFT = [(j, (j - 1) % SIDE) for j in range(SIDE)]
SWAP = [(0, 1), (1, 0)]


def forward_kernel(width, mine_ref, other_ref, sel_ref, gate_ref, up_ref, down_ref, h_ref, gp_ref, rows_ref):
    step = pl.program_id(0)
    half = mine_ref.shape[0]

    @pl.when(step == 0)
    def _():
        rows_ref[:half] = mine_ref[...]
        rows_ref[half:] = other_ref[...]

    block = 256
    for start in range(0, 2 * half, block):
        rows = pl.ds(start, block)
        x = rows_ref[rows, :width]
        dy = rows_ref[rows, width : 2 * width]
        p = jnp.sum(rows_ref[rows, 2 * width :].astype(F32) * sel_ref[...], axis=-1, keepdims=True)
        gate = jnp.dot(x, gate_ref[...], preferred_element_type=F32)
        up = jnp.dot(x, up_ref[...], preferred_element_type=F32)
        back = jnp.dot(dy, down_ref[...], preferred_element_type=F32)
        sig = 1.0 / (1.0 + jnp.exp(-gate))
        act = gate * sig
        hidden = act * up
        hidden_grad = p * back
        h_ref[0, rows] = (hidden_grad * up * (sig * (1.0 + gate * (1.0 - sig)))).astype(BF16)
        h_ref[1, rows] = (hidden_grad * act).astype(BF16)
        h_ref[2, rows] = (p * hidden).astype(BF16)
        term = jnp.sum(hidden * back, axis=-1, keepdims=True) * sel_ref[...]

        @pl.when(step == 0)
        def _():
            gp_ref[rows] = term

        @pl.when(step != 0)
        def _():
            gp_ref[rows] = gp_ref[rows] + term


def forward(mine, other, sel, gate_up, down):
    half, columns = mine.shape
    width, hidden = down.shape
    rows = 2 * half
    tile = 256
    return pl.pallas_call(
        functools.partial(forward_kernel, width),
        name="forward",
        grid=(hidden // tile,),
        in_specs=[
            pl.BlockSpec((half, columns), lambda j: (0, 0)),
            pl.BlockSpec((half, columns), lambda j: (0, 0)),
            pl.BlockSpec((1, LANES), lambda j: (0, 0)),
            pl.BlockSpec((None, width, tile), lambda j: (0, 0, j)),
            pl.BlockSpec((None, width, tile), lambda j: (1, 0, j)),
            pl.BlockSpec((width, tile), lambda j: (0, j)),
        ],
        out_specs=[
            pl.BlockSpec((3, rows, tile), lambda j: (0, 0, j)),
            pl.BlockSpec((rows, LANES), lambda j: (0, 0)),
        ],
        out_shape=[
            jax.ShapeDtypeStruct((3, rows, hidden), BF16),
            jax.ShapeDtypeStruct((rows, LANES), F32),
        ],
        scratch_shapes=[pltpu.VMEM((rows, columns), BF16)],
        compiler_params=pltpu.CompilerParams(vmem_limit_bytes=VMEM),
        cost_estimate=pl.CostEstimate(
            flops=6 * rows * width * hidden, bytes_accessed=6 * width * hidden, transcendentals=0
        ),
    )(mine, other, sel, gate_up, gate_up, down)


def weight_kernel(pieces, spans, cols_ref, *refs):
    col_refs = refs[: 4 * pieces]
    h_refs = refs[4 * pieces : 4 * pieces + pieces // 2]
    out_ref, x_ref, dy_ref = refs[4 * pieces + pieces // 2 :]
    at = 0
    for piece, span in enumerate(spans):
        x_other, x_own, dy_other, dy_own = col_refs[4 * piece : 4 * piece + 4]
        rows = pl.ds(at, span)
        x_ref[rows, :LANES] = x_other[...]
        x_ref[rows, LANES:] = x_own[...]
        dy_ref[rows, :LANES] = dy_other[...]
        dy_ref[rows, LANES:] = dy_own[...]
        at += span
    contract = (((0,), (0,)), ((), ()))
    for kind, source in enumerate((x_ref, x_ref, dy_ref)):
        total = None
        at = 0
        for chunk in range(pieces // 2):
            span = 2 * spans[2 * chunk]
            term = lax.dot_general(
                source[at : at + span], h_refs[chunk][kind], contract, preferred_element_type=F32
            )
            total = term if total is None else total + term
            at += span
        out_ref[0, kind] = total[:LANES].astype(BF16)
        out_ref[1, kind] = total[LANES:].astype(BF16)


def weight_terms(cols, chunks, hs):
    steps = cols.shape[0] // 4
    hidden = hs[0].shape[2]
    arrays, specs, spans = [], [], []
    for pair in chunks:
        for rows in pair:
            spans.append(rows.shape[0])
            for which in range(4):
                arrays.append(rows)
                specs.append(
                    pl.BlockSpec(
                        (rows.shape[0], LANES), lambda j, cols, which=which: (0, cols[4 * j + which])
                    )
                )
    for h in hs:
        arrays.append(h)
        specs.append(pl.BlockSpec(h.shape, lambda j, cols: (0, 0, 0)))
    tokens = sum(spans)
    return pl.pallas_call(
        functools.partial(weight_kernel, len(spans), tuple(spans)),
        name="weight_terms",
        grid_spec=pltpu.PrefetchScalarGridSpec(
            num_scalar_prefetch=1,
            grid=(steps,),
            in_specs=specs,
            out_specs=pl.BlockSpec((None, 2, 3, LANES, hidden), lambda j, cols: (j, 0, 0, 0, 0)),
            scratch_shapes=[pltpu.VMEM((tokens, 2 * LANES), BF16), pltpu.VMEM((tokens, 2 * LANES), BF16)],
        ),
        out_shape=jax.ShapeDtypeStruct((steps, 2, 3, LANES, hidden), BF16),
        compiler_params=pltpu.CompilerParams(vmem_limit_bytes=VMEM),
        cost_estimate=pl.CostEstimate(
            flops=12 * steps * tokens * LANES * hidden,
            bytes_accessed=6 * tokens * hidden,
            transcendentals=0,
        ),
    )(cols, *arrays)


def slot_rows(sub, side):
    order = []
    for z in range(SIDE):
        for x in range(2):
            if z == 0:
                order.append((0, x * sub))
            elif z < 3:
                order.append((1, (z - 1) * SIDE * sub + x * sub))
            else:
                order.append((2, x * sub))
            order.append((0, SIDE * sub + z * sub) if x == 0 else (1, 2 * SIDE * sub + z * sub))
    return order


def slot_kernel(sub, width, h1, h2, h3, g1, g2, g3, gate_ref, up_ref, mine_ref, other_ref, rows_ref):
    step = pl.program_id(0)
    hs, gs = (h1, h2, h3), (g1, g2, g3)
    half = rows_ref.shape[1] // 2

    @pl.when(step == 0)
    def _():
        for core, out in enumerate((mine_ref, other_ref)):
            for n, (chunk, first) in enumerate(slot_rows(sub, SIDE)):
                at = first + core * (hs[chunk].shape[1] // 2)
                for kind in range(2):
                    rows_ref[kind, core * half + n * sub : core * half + (n + 1) * sub] = hs[chunk][
                        kind, at : at + sub
                    ]
                out[n * sub : (n + 1) * sub, width:] = gs[chunk][at : at + sub].astype(BF16)

    contract = (((1,), (1,)), ((), ()))
    tile = gate_ref.shape[0]
    cols = pl.ds(pl.multiple_of(step * tile, tile), tile)
    for core, out in enumerate((mine_ref, other_ref)):
        rows = slice(core * half, (core + 1) * half)
        total = lax.dot_general(rows_ref[0, rows], gate_ref[...], contract, preferred_element_type=F32)
        total += lax.dot_general(rows_ref[1, rows], up_ref[...], contract, preferred_element_type=F32)
        out[:, cols] = total.astype(BF16)


def slot_terms(hs, gps, gate_up, sub):
    _, width, hidden = gate_up.shape
    tile = 512
    half = 16 * sub
    out = jax.ShapeDtypeStruct((half, width + LANES), BF16)
    specs = [pl.BlockSpec((2,) + h.shape[1:], lambda j: (0, 0, 0)) for h in hs]
    specs += [pl.BlockSpec(g.shape, lambda j: (0, 0)) for g in gps]
    specs += [pl.BlockSpec((None, tile, hidden), lambda j, k=k: (k, j, 0)) for k in range(2)]
    return pl.pallas_call(
        functools.partial(slot_kernel, sub, width),
        name="slot_terms",
        grid=(width // tile,),
        in_specs=specs,
        out_specs=[pl.BlockSpec(out.shape, lambda j: (0, 0))] * 2,
        out_shape=[out, out],
        scratch_shapes=[pltpu.VMEM((2, 2 * half, hidden), BF16)],
        compiler_params=pltpu.CompilerParams(vmem_limit_bytes=VMEM),
        cost_estimate=pl.CostEstimate(
            flops=8 * half * width * hidden, bytes_accessed=4 * width * hidden, transcendentals=0
        ),
    )(*hs, *gps, gate_up, gate_up)


def add(a, b):
    return (a.astype(F32) + b.astype(F32)).astype(BF16)


def shards(layer_input, out_grad, routes, probs, gate_up, down_t):
    tokens, width = layer_input.shape
    sub = tokens // 2
    x, y = lax.axis_index("x"), lax.axis_index("y")
    z, core = lax.axis_index("z"), lax.axis_index("core")
    expert = x % 2
    lane = lax.broadcasted_iota(jnp.int32, (1, LANES), 1)
    sel = (lane == (z * 2 + core) * 2 + expert).astype(F32)

    hot = routes[:, :, None] == lax.broadcasted_iota(jnp.int32, (1, 1, LANES), 2)
    dense = jnp.sum(jnp.where(hot, probs.astype(F32)[:, :, None], 0.0), axis=1).astype(BF16)
    row = jnp.concatenate([layer_input, out_grad, dense], axis=1)

    first, second = row[:sub], row[sub:]
    near = [1, 3, 2]
    first_x = [first] + [lax.ppermute(first, "x", XOR[k]) for k in near]
    second_z = [second] + [lax.ppermute(second, "z", XOR[k]) for k in near]
    first_x = jnp.concatenate(first_x, axis=0)
    second_z = jnp.concatenate(second_z, axis=0)
    first_z = [lax.ppermute(first_x, "z", XOR[k]) for k in near]
    second_x = [lax.ppermute(second_z, "x", XOR[k]) for k in near]

    mine = [
        jnp.concatenate([first_x, second_z], axis=0),
        jnp.concatenate(first_z[:2] + second_x[:2], axis=0),
        jnp.concatenate([first_z[2], second_x[2]], axis=0),
    ]
    chunks = [(m, lax.ppermute(m, "core", SWAP)) for m in mine]

    gate_up = jnp.transpose(lax.dynamic_index_in_dim(gate_up, expert, 2, keepdims=False), (1, 0, 2))
    down = lax.dynamic_index_in_dim(down_t, expert, 1, keepdims=False)

    hs, gps = [], []
    for m, o in chunks:
        h, gp = forward(m, o, sel, gate_up, down)
        hs.append(h)
        gps.append(gp)

    blocks = width // LANES
    cols = []
    for r in (2, 3, 1, 0):
        base = SIDE * ((y + r) % SIDE)
        other, own = base + (x ^ 1), base + x
        cols += [other, own, blocks + other, blocks + own]
    cols = jnp.stack(cols).astype(jnp.int32)
    far = weight_terms(cols[:8], chunks, hs)
    close = weight_terms(cols[8:], chunks, hs)

    a_right = lax.ppermute(far[0, 0], "y", RIGHT)
    a_left = lax.ppermute(far[1, 0], "y", LEFT)
    b_left = lax.ppermute(far[0, 1], "y", LEFT)
    b_right = lax.ppermute(close[0, 1], "y", RIGHT)
    a_right = lax.ppermute(add(close[0, 0], a_right), "y", RIGHT)
    b_left = lax.ppermute(add(far[1, 1], b_left), "y", LEFT)
    swap = (close[1, 0].astype(F32) + a_right.astype(F32) + a_left.astype(F32)).astype(BF16)
    swap = lax.ppermute(swap, "x", XOR[1])
    kept = (close[1, 1].astype(F32) + b_right.astype(F32) + b_left.astype(F32)).astype(BF16)
    even, odd = jnp.where(expert == 0, kept, swap), jnp.where(expert == 0, swap, kept)
    grad_weights = jnp.transpose(jnp.stack([even, odd], axis=0), (2, 1, 0, 3))

    part, away = slot_terms(hs, gps, gate_up, sub)
    part = add(part, lax.ppermute(away, "core", SWAP))
    part = part.reshape((SIDE, 2, tokens, part.shape[1]))
    total = part[0].astype(F32)
    for n, k in enumerate(near):
        total = total + lax.ppermute(part[n + 1], "z", XOR[k]).astype(F32)
    total = total.astype(BF16)
    rows = total[0].astype(F32) + lax.ppermute(total[1], "x", XOR[1]).astype(F32)
    grad_input = rows[:, :width].astype(BF16)
    grad_prob = jnp.sum(jnp.where(hot, rows[:, None, width:], 0.0), axis=2)
    return (grad_input, grad_prob, grad_weights)


def solution(mesh):
    grid = Mesh(mesh.devices.reshape(4, 4, 4, 2), ("y", "x", "z", "core"))
    every = P(("y", "x", "z", "core"), None)
    return jax.shard_map(
        shards,
        mesh=grid,
        in_specs=(every, every, every, every, P(None, None, ("z", "core"), None), P(None, ("z", "core"), None)),
        out_specs=(every, every, P(("y", "x"), None, ("z", "core"), None)),
        check_vma=False,
    )
```

time: 272 us -> 204 us (0.75)
  Pallas kernels: 0 us -> 49.8 us
  local copies, waits for them, and re-layouts: 85.3 us -> 49.6 us
  waiting for transfers between devices: 93.3 us -> 60.5 us
  matrix products: 31.9 us -> 0 us
  between operations: 14.4 us -> 0.93 us
  other arithmetic: 18.3 us -> 5.13 us
  starting transfers between devices: 26.8 us -> 37.9 us
    ppermute x0 -> x27, waiting for transfers between devices: none -> 60.5 us  [the longest x1 23.9 us: shards(): a_right = lax.ppermute(add(close[0, 0], a_right), 'y', RIGHT)]
    all_to_all x6 -> x0, waiting for transfers between devices: 57 us -> none  [the longest x1 23.8 us: shards(): lax.all_to_all(send_grad, 'expert', split_axis=0, concat_axis=1, tiled=True)]
    pallas_call x0 -> x6, Pallas kernels: none -> 49.8 us  [the longest x3 27.1 us: forward(): pl.pallas_call(functools.partial(forward_kernel, width), name='forward',...]
    ppermute x0 -> x27, starting transfers between devices: none -> 37.9 us  [the longest x3 8.36 us: shards(): second_x = [lax.ppermute(second_z, 'x', XOR[k]) for k in near]]
    unnamed x2 -> x0, waiting for transfers between devices: 36.3 us -> none
    dot_general x9 -> x0, matrix products: 31.9 us -> none  [the longest x1 6.86 us: expert_math(): jnp.einsum('esf,def->esd', gate_grad, weight_gate, preferred_element_type...]
    dynamic_slice x0 -> x3, local copies, waits for them, and re-layouts: none -> 31.7 us  [the longest x2 23.9 us: shards(): lax.dynamic_index_in_dim(gate_up, expert, 2, keepdims=False)]
    all_to_all x6 -> x0, starting transfers between devices: 26.5 us -> none  [the longest x1 5.4 us: shards(): lax.all_to_all(send_probs, 'expert', split_axis=0, concat_axis=1, tiled=T...]
  transfers between devices with their start and end apart: 7 -> 27, of which waited for: 5 -> 8; matrix products, arithmetic and copies ran while one was open for 27% -> 23% of each run, Pallas kernels for 0% -> 15%
where the time goes in v1:
time: 204 us
  waiting for transfers between devices  60.5 us (30%)
  Pallas kernels  49.8 us (24%)
  local copies, waits for them, and re-layouts  49.6 us (24%)
  starting transfers between devices  37.9 us (19%)
  other arithmetic  5.13 us (3%)
    pallas_call x3, Pallas kernels, forward(): pl.pallas_call(functools.partial(forward_kernel, width), name='forward',...  27.1 us
    ppermute x1, waiting for transfers between devices, shards(): a_right = lax.ppermute(add(close[0, 0], a_right), 'y', RIGHT)  23.9 us
    dynamic_slice x2, local copies, waits for them, and re-layouts, shards(): lax.dynamic_index_in_dim(gate_up, expert, 2, keepdims=False)  23.9 us
    pallas_call x2, Pallas kernels, weight_terms(): pl.pallas_call(functools.partial(weight_kernel, len(spans), tuple(spans))...  15.1 us
    ppermute x1, waiting for transfers between devices, shards(): swap = lax.ppermute(swap, 'x', XOR[1])  12.9 us
    unnamed x24, local copies, waits for them, and re-layouts  11.3 us
    ppermute x1, waiting for transfers between devices, shards(): b_left = lax.ppermute(far[0, 1], 'y', LEFT)  9.05 us
    ppermute x3, starting transfers between devices, shards(): second_x = [lax.ppermute(second_z, 'x', XOR[k]) for k in near]  8.36 us
  transfers between devices with their start and end apart: 27, of which 8 were waited for; matrix products, arithmetic and copies ran while one was open for 23% of the time, Pallas kernels for 15%

profile of v1, /device:TPU:0, one launch (start us, length us, event | category | flops | bytes accessed | tf_op | source)
XLA Modules:
  0.0 203.8 jit_solution(12898102799578888388)
XLA Ops:
  4.0 1.6 collective-permute-start
  5.6 2.1 %collective-permute-start.1 = (bf16[16,4224]{1,0:T(8,128)(2,1)S(1)}, bf16[16,4224]{1,0:T(8,128)(2,1)S(1)}, u32[]{:S(2)}, u32[]{:S(2)}) collective-permute-start(bf16[16,4224]{1,0:T(8,128)(2,1)S(1)} %get-tuple-element.39), channel_id=1, source_target_pairs={{0,24},{8,16},{16,8},{24,0},{1,25},{9,17},{17,9},{25,1},{2,26},{10... | collective-permute-start | bytes 405512 | tf_op jit(solution)/shard_map/ppermute | solution.py:240
  8.3 1.9 collective-permute-start.3
  10.2 2.5 %collective-permute-start.4 = (bf16[16,4224]{1,0:T(8,128)(2,1)S(1)}, bf16[16,4224]{1,0:T(8,128)(2,1)S(1)}, u32[]{:S(2)}, u32[]{:S(2)}) collective-permute-start(bf16[16,4224]{1,0:T(8,128)(2,1)S(1)} %get-tuple-element.37), channel_id=1, source_target_pairs={{0,6},{2,4},{4,2},{6,0},{1,7},{3,5},{5,3},{7,1},{8,14},{10,12},{12... | collective-permute-start | bytes 405512 | tf_op jit(solution)/shard_map/ppermute | solution.py:241
  14.8 2.0 collective-permute-start.7
  16.8 2.5 %collective-permute-start.8 = (bf16[64,4224]{1,0:T(8,128)(2,1)S(1)}, bf16[64,4224]{1,0:T(8,128)(2,1)S(1)}, u32[]{:S(2)}, u32[]{:S(2)}) collective-permute-start(bf16[64,4224]{1,0:T(8,128)(2,1)S(1)} %pad_maximum_fusion), channel_id=1, source_target_pairs={{0,6},{2,4},{4,2},{6,0},{1,7},{3,5},{5,3},{7,1},{8,14},{10,12},{12... | collective-permute-start | bytes 1622024 | tf_op jit(solution)/shard_map/ppermute | solution.py:244
  19.8 2.8 %collective-permute-start.9 = (bf16[64,4224]{1,0:T(8,128)(2,1)S(1)}, bf16[64,4224]{1,0:T(8,128)(2,1)S(1)}, u32[]{:S(2)}, u32[]{:S(2)}) collective-permute-start(bf16[64,4224]{1,0:T(8,128)(2,1)S(1)} %pad_maximum_fusion.1), channel_id=1, source_target_pairs={{0,8},{8,0},{16,24},{24,16},{1,9},{9,1},{17,25},{25,17},{2,10},{10... | collective-permute-start | bytes 1622024 | tf_op jit(solution)/shard_map/ppermute | solution.py:245
  22.6 2.1 %collective-permute-start.10 = (bf16[64,4224]{1,0:T(8,128)(2,1)S(1)}, bf16[64,4224]{1,0:T(8,128)(2,1)S(1)}, u32[]{:S(2)}, u32[]{:S(2)}) collective-permute-start(bf16[64,4224]{1,0:T(8,128)(2,1)S(1)} %pad_maximum_fusion.1), channel_id=1, source_target_pairs={{0,24},{8,16},{16,8},{24,0},{1,25},{9,17},{17,9},{25,1},{2,26},{10... | collective-permute-start | bytes 1622024 | tf_op jit(solution)/shard_map/ppermute | solution.py:245
  30.1 3.4 %collective-permute-start.13 = (bf16[64,4224]{1,0:T(8,128)(2,1)S(1)}, bf16[64,4224]{1,0:T(8,128)(2,1)S(1)}, u32[]{:S(2)}, u32[]{:S(2)}) collective-permute-start(bf16[64,4224]{1,0:T(8,128)(2,1)S(1)} %pad_maximum_fusion.1), channel_id=1, source_target_pairs={{0,16},{8,24},{16,0},{24,8},{1,17},{9,25},{17,1},{25,9},{2,18},{10... | collective-permute-start | bytes 1622024 | tf_op jit(solution)/shard_map/ppermute | solution.py:245
  33.6 7.5 %collective-permute-done.8 = bf16[64,4224]{1,0:T(8,128)(2,1)S(1)} collective-permute-done((bf16[64,4224]{1,0:T(8,128)(2,1)S(1)}, bf16[64,4224]{1,0:T(8,128)(2,1)S(1)}, u32[]{:S(2)}, u32[]{:S(2)}) %collective-permute-start.8) | collective-permute-done | bytes 540704 | tf_op jit(solution)/shard_map/ppermute | solution.py:244
  41.1 5.0 %collective-permute-done.10 = bf16[64,4224]{1,0:T(8,128)(2,1)S(1)} collective-permute-done((bf16[64,4224]{1,0:T(8,128)(2,1)S(1)}, bf16[64,4224]{1,0:T(8,128)(2,1)S(1)}, u32[]{:S(2)}, u32[]{:S(2)}) %collective-permute-start.10) | collective-permute-done | bytes 540704 | tf_op jit(solution)/shard_map/ppermute | solution.py:245
  47.1 15.7 %constant_dynamic-slice_fusion.1 = bf16[2048,2,1,768]{3,2,1,0:T(2,128)(2,1)} fusion(bf16[2048,2,2,768]{3,2,1,0:T(2,128)(2,1)} %param.10, s32[]{:T(128)S(6)} %select_n.51), kind=kLoop, calls=%fused_computation.54 | loop fusion | bytes 12582916 | tf_op jit(solution)/shard_map/jit(dynamic_index_in_dim)/dynamic_slice | solution.py:254
  62.8 8.2 %copy.27 = bf16[2048,2,1,768]{3,0,1,2:T(8,128)(2,1)} copy(bf16[2048,2,1,768]{3,2,1,0:T(2,128)(2,1)} %constant_dynamic-slice_fusion.1) | data formatting | bytes 12582912 | tf_op jit(solution)/shard_map/jit(dynamic_index_in_dim)/dynamic_slice | solution.py:254
  71.0 7.8 %constant_dynamic-slice_fusion = bf16[2048,1,768]{2,1,0:T(2,128)(2,1)S(1)} fusion(bf16[2048,2,768]{2,1,0:T(2,128)(2,1)} %param.11, s32[]{:T(128)S(6)} %select_n.51), kind=kLoop, calls=%fused_computation.53 | loop fusion | bytes 6291460 | tf_op jit(solution)/shard_map/jit(dynamic_index_in_dim)/dynamic_slice | solution.py:255
  78.9 2.2 %copy.28 = bf16[2048,1,768]{2,0,1:T(8,128)(2,1)} copy(bf16[2048,1,768]{2,1,0:T(2,128)(2,1)S(1)} %constant_dynamic-slice_fusion) | data formatting | bytes 6291456
  81.0 7.2 %forward.3 = (bf16[3,256,768]{2,1,0:T(8,128)(2,1)S(1)}, f32[256,128]{1,0:T(8,128)S(1)}) custom-call(bf16[128,4224]{1,0:T(8,128)(2,1)} %constant_dynamic-update-slice_fusion.mine_ref.refs_0_.refs_1_.refs_2_.refs_3_, bf16[128,4224]{1,0:T(8,128)(2,1)} %collective-permute-done.6.other_ref.refs_4_.refs_5_.refs_6_.refs_7_, ...), custom_call_target="tpu_custom_call" | custom-call | flops 2415919104 | bytes 9437184 | tf_op jit(solution)/shard_map/forward/pallas_call | solution.py:64
  88.3 7.3 %forward.5 = (bf16[3,256,768]{2,1,0:T(8,128)(2,1)S(1)}, f32[256,128]{1,0:T(8,128)S(1)}) custom-call(bf16[128,4224]{1,0:T(8,128)(2,1)S(1)} %constant_dynamic-update-slice_fusion.12.mine_ref.refs_16_.refs_17_.refs_18_.refs_19_, bf16[128,4224]{1,0:T(8,128)(2,1)} %collective-permute-done.14.other_ref.refs_20_.refs_21_.refs_22_.refs_23_, ...), custom_call_target="tpu_custom_call" | custom-call | flops 2415919104 | bytes 9437184 | tf_op jit(solution)/shard_map/forward/pallas_call | solution.py:64
  95.6 12.7 %forward.4 = (bf16[3,512,768]{2,1,0:T(8,128)(2,1)}, f32[512,128]{1,0:T(8,128)S(1)}) custom-call(bf16[256,4224]{1,0:T(8,128)(2,1)S(1)} %constant_dynamic-update-slice_fusion.8.mine_ref.refs_8_.refs_9_.refs_10_.refs_11_, bf16[256,4224]{1,0:T(8,128)(2,1)} %collective-permute-done.11.other_ref.refs_12_.refs_13_.refs_14_.refs_15_, ...), custom_call_target="tpu_custom_call" | custom-call | flops 4831838208 | bytes 9437184 | tf_op jit(solution)/shard_map/forward/pallas_call | solution.py:64
  108.2 7.5 %slot_terms.1 = (bf16[256,2176]{1,0:T(8,128)(2,1)S(1)}, bf16[256,2176]{1,0:T(8,128)(2,1)}) custom-call(bf16[3,256,768]{2,1,0:T(8,128)(2,1)S(1)} %get-tuple-element.11.h1.refs_24_, bf16[3,512,768]{2,1,0:T(8,128)(2,1)} %get-tuple-element.12.h2.refs_25_, bf16[3,256,768]{2,1,0:T(8,128)(2,1)S(1)} %get-tuple-element.13.h3.refs_26_, ...), custom_call_target="tpu_custom_call" | custom-call | flops 3221225472 | bytes 6291456 | tf_op jit(solution)/shard_map/slot_terms/pallas_call | solution.py:206
  117.3 7.5 %weight_terms.3 = bf16[2,2,3,128,768]{4,3,2,1,0:T(8,128)(2,1)} custom-call(s32[8]{0:T(128)S(1)} %stack.79.cols_ref, bf16[128,4224]{1,0:T(8,128)(2,1)} %constant_dynamic-update-slice_fusion.mine_ref.refs_0_.refs_1_.refs_2_.refs_3_, bf16[128,4224]{1,0:T(8,128)(2,1)} %constant_dynamic-update-slice_fusion.mine_ref.refs_0_.refs_1_.refs_2_.refs_3_, ...), custom_call_target="tpu_custom_call" | custom-call | flops 2415919104 | bytes 4718592 | tf_op jit(solution)/shard_map/weight_terms/pallas_call | solution.py:138
  126.3 3.1 %collective-permute-start.25 = (bf16[3,128,768]{2,1,0:T(8,128)(2,1)S(1)}, bf16[3,128,768]{2,1,0:T(8,128)(2,1)S(1)}, u32[]{:S(2)}, u32[]{:S(2)}) collective-permute-start(bf16[3,128,768]{2,1,0:T(8,128)(2,1)S(1)} %get-tuple-element.31), channel_id=1, source_target_pairs={{0,96},{32,0},{64,32},{96,64},{1,97},{33,1},{65,33},{97,65},{2,98}... | collective-permute-start | bytes 1769480 | tf_op jit(solution)/shard_map/ppermute | solution.py:274
  129.4 3.2 %collective-permute-start.21 = (bf16[3,128,768]{2,1,0:T(8,128)(2,1)S(1)}, bf16[3,128,768]{2,1,0:T(8,128)(2,1)S(1)}, u32[]{:S(2)}, u32[]{:S(2)}) collective-permute-start(bf16[3,128,768]{2,1,0:T(8,128)(2,1)S(1)} %get-tuple-element.30), channel_id=1, source_target_pairs={{0,96},{32,0},{64,32},{96,64},{1,97},{33,1},{65,33},{97,65},{2,98}... | collective-permute-start | bytes 1769480 | tf_op jit(solution)/shard_map/ppermute | solution.py:275
  132.7 7.5 %weight_terms.2 = bf16[2,2,3,128,768]{4,3,2,1,0:T(8,128)(2,1)} custom-call(s32[8]{0:T(128)S(1)} %stack.70.cols_ref, bf16[128,4224]{1,0:T(8,128)(2,1)} %constant_dynamic-update-slice_fusion.mine_ref.refs_0_.refs_1_.refs_2_.refs_3_, bf16[128,4224]{1,0:T(8,128)(2,1)} %constant_dynamic-update-slice_fusion.mine_ref.refs_0_.refs_1_.refs_2_.refs_3_, ...), custom_call_target="tpu_custom_call" | custom-call | flops 2415919104 | bytes 4718592 | tf_op jit(solution)/shard_map/weight_terms/pallas_call | solution.py:138
  140.2 1.9 slice_bitcast_fusion.6
  143.1 2.2 %collective-permute-start.17 = (bf16[2,32,2176]{2,1,0:T(8,128)(2,1)S(1)}, bf16[2,32,2176]{2,1,0:T(8,128)(2,1)S(1)}, u32[]{:S(2)}, u32[]{:S(2)}) collective-permute-start(bf16[2,32,2176]{2,1,0:T(8,128)(2,1)S(1)} %bitcast.87), channel_id=1, source_target_pairs={{0,6},{2,4},{4,2},{6,0},{1,7},{3,5},{5,3},{7,1},{8,14},{10,12},{12... | collective-permute-start | bytes 835592 | tf_op jit(solution)/shard_map/ppermute | solution.py:290
  146.3 9.1 %collective-permute-done.21 = bf16[3,128,768]{2,1,0:T(8,128)(2,1)S(1)} collective-permute-done((bf16[3,128,768]{2,1,0:T(8,128)(2,1)S(1)}, bf16[3,128,768]{2,1,0:T(8,128)(2,1)S(1)}, u32[]{:S(2)}, u32[]{:S(2)}) %collective-permute-start.21) | collective-permute-done | bytes 589856 | tf_op jit(solution)/shard_map/ppermute | solution.py:275
  157.6 1.7 collective-permute-start.24
  159.2 1.6 collective-permute-start.22
  161.1 23.9 %collective-permute-done.24 = bf16[3,128,768]{2,1,0:T(8,128)(2,1)S(1)} collective-permute-done((bf16[3,128,768]{2,1,0:T(8,128)(2,1)S(1)}, bf16[3,128,768]{2,1,0:T(8,128)(2,1)S(1)}, u32[]{:S(2)}, u32[]{:S(2)}) %collective-permute-start.24) | collective-permute-done | bytes 589856 | tf_op jit(solution)/shard_map/ppermute | solution.py:277
  187.0 12.9 %collective-permute-done.26 = bf16[3,128,768]{2,1,0:T(8,128)(2,1)} collective-permute-done((bf16[3,128,768]{2,1,0:T(8,128)(2,1)S(1)}, bf16[3,128,768]{2,1,0:T(8,128)(2,1)}, u32[]{:S(2)}, u32[]{:S(2)}) %collective-permute-start.26) | collective-permute-done | bytes 589856 | tf_op jit(solution)/shard_map/ppermute | solution.py:280
  199.9 1.6 select_bitcast_fusion.1
  201.6 2.2 %copy.23 = bf16[128,3,2,768]{3,2,1,0:T(2,128)(2,1)} copy(bf16[128,3,2,768]{3,0,1,2:T(8,128)(2,1)S(1)} %maximum_bitcast_fusion) | data formatting | bytes 2359296
  (82 shorter events, 22.3 us)
Async XLA Ops:
  4.0 8.8 %collective-permute-start = (bf16[16,4224]{1,0:T(8,128)(2,1)S(1)}, bf16[16,4224]{1,0:T(8,128)(2,1)S(1)}, u32[]{:S(2)}, u32[]{:S(2)}) collective-permute-start(bf16[16,4224]{1,0:T(8,128)(2,1)S(1)} %get-tuple-element.39), channel_id=1, source_target_pairs={{0,8},{8,0},{16,24},{24,16},{1,9},{9,1},{17,25},{25,17},{2,10},{10... | collective-permute-start | bytes 405512 | tf_op jit(solution)/shard_map/ppermute | solution.py:240
  5.6 9.2 %collective-permute-start.1 = (bf16[16,4224]{1,0:T(8,128)(2,1)S(1)}, bf16[16,4224]{1,0:T(8,128)(2,1)S(1)}, u32[]{:S(2)}, u32[]{:S(2)}) collective-permute-start(bf16[16,4224]{1,0:T(8,128)(2,1)S(1)} %get-tuple-element.39), channel_id=1, source_target_pairs={{0,24},{8,16},{16,8},{24,0},{1,25},{9,17},{17,9},{25,1},{2,26},{10... | collective-permute-start | bytes 405512 | tf_op jit(solution)/shard_map/ppermute | solution.py:240
  7.7 7.1 %collective-permute-start.2 = (bf16[16,4224]{1,0:T(8,128)(2,1)S(1)}, bf16[16,4224]{1,0:T(8,128)(2,1)S(1)}, u32[]{:S(2)}, u32[]{:S(2)}) collective-permute-start(bf16[16,4224]{1,0:T(8,128)(2,1)S(1)} %get-tuple-element.39), channel_id=1, source_target_pairs={{0,16},{8,24},{16,0},{24,8},{1,17},{9,25},{17,1},{25,9},{2,18},{10... | collective-permute-start | bytes 405512 | tf_op jit(solution)/shard_map/ppermute | solution.py:240
  8.3 11.0 %collective-permute-start.3 = (bf16[16,4224]{1,0:T(8,128)(2,1)S(1)}, bf16[16,4224]{1,0:T(8,128)(2,1)S(1)}, u32[]{:S(2)}, u32[]{:S(2)}) collective-permute-start(bf16[16,4224]{1,0:T(8,128)(2,1)S(1)} %get-tuple-element.37), channel_id=1, source_target_pairs={{0,2},{2,0},{4,6},{6,4},{1,3},{3,1},{5,7},{7,5},{8,10},{10,8},{12,... | collective-permute-start | bytes 405512 | tf_op jit(solution)/shard_map/ppermute | solution.py:241
  10.2 9.1 %collective-permute-start.4 = (bf16[16,4224]{1,0:T(8,128)(2,1)S(1)}, bf16[16,4224]{1,0:T(8,128)(2,1)S(1)}, u32[]{:S(2)}, u32[]{:S(2)}) collective-permute-start(bf16[16,4224]{1,0:T(8,128)(2,1)S(1)} %get-tuple-element.37), channel_id=1, source_target_pairs={{0,6},{2,4},{4,2},{6,0},{1,7},{3,5},{5,3},{7,1},{8,14},{10,12},{12... | collective-permute-start | bytes 405512 | tf_op jit(solution)/shard_map/ppermute | solution.py:241
  12.7 7.0 %collective-permute-start.5 = (bf16[16,4224]{1,0:T(8,128)(2,1)S(1)}, bf16[16,4224]{1,0:T(8,128)(2,1)S(1)}, u32[]{:S(2)}, u32[]{:S(2)}) collective-permute-start(bf16[16,4224]{1,0:T(8,128)(2,1)S(1)} %get-tuple-element.37), channel_id=1, source_target_pairs={{0,4},{2,6},{4,0},{6,2},{1,5},{3,7},{5,1},{7,3},{8,12},{10,14},{12... | collective-permute-start | bytes 405512 | tf_op jit(solution)/shard_map/ppermute | solution.py:241
  14.8 15.3 %collective-permute-start.7 = (bf16[64,4224]{1,0:T(8,128)(2,1)S(1)}, bf16[64,4224]{1,0:T(8,128)(2,1)S(1)}, u32[]{:S(2)}, u32[]{:S(2)}) collective-permute-start(bf16[64,4224]{1,0:T(8,128)(2,1)S(1)} %pad_maximum_fusion), channel_id=1, source_target_pairs={{0,2},{2,0},{4,6},{6,4},{1,3},{3,1},{5,7},{7,5},{8,10},{10,8},{12,... | collective-permute-start | bytes 1622024 | tf_op jit(solution)/shard_map/ppermute | solution.py:244
  16.8 24.3 %collective-permute-start.8 = (bf16[64,4224]{1,0:T(8,128)(2,1)S(1)}, bf16[64,4224]{1,0:T(8,128)(2,1)S(1)}, u32[]{:S(2)}, u32[]{:S(2)}) collective-permute-start(bf16[64,4224]{1,0:T(8,128)(2,1)S(1)} %pad_maximum_fusion), channel_id=1, source_target_pairs={{0,6},{2,4},{4,2},{6,0},{1,7},{3,5},{5,3},{7,1},{8,14},{10,12},{12... | collective-permute-start | bytes 1622024 | tf_op jit(solution)/shard_map/ppermute | solution.py:244
  19.8 21.3 %collective-permute-start.9 = (bf16[64,4224]{1,0:T(8,128)(2,1)S(1)}, bf16[64,4224]{1,0:T(8,128)(2,1)S(1)}, u32[]{:S(2)}, u32[]{:S(2)}) collective-permute-start(bf16[64,4224]{1,0:T(8,128)(2,1)S(1)} %pad_maximum_fusion.1), channel_id=1, source_target_pairs={{0,8},{8,0},{16,24},{24,16},{1,9},{9,1},{17,25},{25,17},{2,10},{10... | collective-permute-start | bytes 1622024 | tf_op jit(solution)/shard_map/ppermute | solution.py:245
  22.6 23.5 %collective-permute-start.10 = (bf16[64,4224]{1,0:T(8,128)(2,1)S(1)}, bf16[64,4224]{1,0:T(8,128)(2,1)S(1)}, u32[]{:S(2)}, u32[]{:S(2)}) collective-permute-start(bf16[64,4224]{1,0:T(8,128)(2,1)S(1)} %pad_maximum_fusion.1), channel_id=1, source_target_pairs={{0,24},{8,16},{16,8},{24,0},{1,25},{9,17},{17,9},{25,1},{2,26},{10... | collective-permute-start | bytes 1622024 | tf_op jit(solution)/shard_map/ppermute | solution.py:245
  24.7 21.6 %collective-permute-start.12 = (bf16[64,4224]{1,0:T(8,128)(2,1)S(1)}, bf16[64,4224]{1,0:T(8,128)(2,1)S(1)}, u32[]{:S(2)}, u32[]{:S(2)}) collective-permute-start(bf16[64,4224]{1,0:T(8,128)(2,1)S(1)} %pad_maximum_fusion), channel_id=1, source_target_pairs={{0,4},{2,6},{4,0},{6,2},{1,5},{3,7},{5,1},{7,3},{8,12},{10,14},{12... | collective-permute-start | bytes 1622024 | tf_op jit(solution)/shard_map/ppermute | solution.py:244
  30.1 16.3 %collective-permute-start.13 = (bf16[64,4224]{1,0:T(8,128)(2,1)S(1)}, bf16[64,4224]{1,0:T(8,128)(2,1)S(1)}, u32[]{:S(2)}, u32[]{:S(2)}) collective-permute-start(bf16[64,4224]{1,0:T(8,128)(2,1)S(1)} %pad_maximum_fusion.1), channel_id=1, source_target_pairs={{0,16},{8,24},{16,0},{24,8},{1,17},{9,25},{17,1},{25,9},{2,18},{10... | collective-permute-start | bytes 1622024 | tf_op jit(solution)/shard_map/ppermute | solution.py:245
  41.0 40.0 %collective-permute-start.6 = (bf16[128,4224]{1,0:T(8,128)(2,1)}, bf16[128,4224]{1,0:T(8,128)(2,1)}, u32[]{:S(2)}, u32[]{:S(2)}) collective-permute-start(bf16[128,4224]{1,0:T(8,128)(2,1)} %constant_dynamic-update-slice_fusion.mine_ref.refs_0_.refs_1_.refs_2_.refs_3_), channel_id=1, source_target_pairs={{0,1},{1,0},{2,3},{3,2},{4,5},{5,4},{6,7},{7,6},{8,9},{9,8},{10,11... | collective-permute-start | bytes 3244040 | tf_op jit(solution)/shard_map/ppermute | solution.py:252
  46.2 49.4 %copy-start = (bf16[256,4224]{1,0:T(8,128)(2,1)}, bf16[256,4224]{1,0:T(8,128)(2,1)S(1)}, u32[]{:S(2)}) copy-start(bf16[256,4224]{1,0:T(8,128)(2,1)S(1)} %constant_dynamic-update-slice_fusion.8.mine_ref.refs_8_.refs_9_.refs_10_.refs_11_) | copy-start | bytes 6488068
  46.2 49.4 %collective-permute-start.11 = (bf16[256,4224]{1,0:T(8,128)(2,1)S(1)}, bf16[256,4224]{1,0:T(8,128)(2,1)}, u32[]{:S(2)}, u32[]{:S(2)}) collective-permute-start(bf16[256,4224]{1,0:T(8,128)(2,1)S(1)} %constant_dynamic-update-slice_fusion.8.mine_ref.refs_8_.refs_9_.refs_10_.refs_11_), channel_id=1, source_target_pairs={{0,1},{1,0},{2,3},{3,2},{4,5},{5,4},{6,7},{7,6},{8,9},{9,8},{10,11... | collective-permute-start | bytes 6488072 | tf_op jit(solution)/shard_map/ppermute | solution.py:252
  46.4 41.9 %collective-permute-start.14 = (bf16[128,4224]{1,0:T(8,128)(2,1)S(1)}, bf16[128,4224]{1,0:T(8,128)(2,1)}, u32[]{:S(2)}, u32[]{:S(2)}) collective-permute-start(bf16[128,4224]{1,0:T(8,128)(2,1)S(1)} %constant_dynamic-update-slice_fusion.12.mine_ref.refs_16_.refs_17_.refs_18_.refs_19_), channel_id=1, source_target_pairs={{0,1},{1,0},{2,3},{3,2},{4,5},{5,4},{6,7},{7,6},{8,9},{9,8},{10,11... | collective-permute-start | bytes 3244040 | tf_op jit(solution)/shard_map/ppermute | solution.py:252
  88.2 20.0 %copy-start.1 = (bf16[3,256,768]{2,1,0:T(8,128)(2,1)}, bf16[3,256,768]{2,1,0:T(8,128)(2,1)S(1)}, u32[]{:S(2)}) copy-start(bf16[3,256,768]{2,1,0:T(8,128)(2,1)S(1)} %get-tuple-element.11.h1.refs_24_) | copy-start | bytes 3538948
  95.5 12.7 %copy-start.3 = (bf16[3,256,768]{2,1,0:T(8,128)(2,1)}, bf16[3,256,768]{2,1,0:T(8,128)(2,1)S(1)}, u32[]{:S(2)}) copy-start(bf16[3,256,768]{2,1,0:T(8,128)(2,1)S(1)} %get-tuple-element.13.h3.refs_26_) | copy-start | bytes 3538948
  115.8 26.4 %collective-permute-start.15 = (bf16[256,2176]{1,0:T(8,128)(2,1)}, bf16[256,2176]{1,0:T(8,128)(2,1)S(1)}, u32[]{:S(2)}, u32[]{:S(2)}) collective-permute-start(bf16[256,2176]{1,0:T(8,128)(2,1)} %get-tuple-element.18), channel_id=1, source_target_pairs={{0,1},{1,0},{2,3},{3,2},{4,5},{5,4},{6,7},{7,6},{8,9},{9,8},{10,11... | collective-permute-start | bytes 3342344 | tf_op jit(solution)/shard_map/ppermute | solution.py:286
  116.0 1.3 copy-start.2
  126.3 34.8 %collective-permute-start.25 = (bf16[3,128,768]{2,1,0:T(8,128)(2,1)S(1)}, bf16[3,128,768]{2,1,0:T(8,128)(2,1)S(1)}, u32[]{:S(2)}, u32[]{:S(2)}) collective-permute-start(bf16[3,128,768]{2,1,0:T(8,128)(2,1)S(1)} %get-tuple-element.31), channel_id=1, source_target_pairs={{0,96},{32,0},{64,32},{96,64},{1,97},{33,1},{65,33},{97,65},{2,98}... | collective-permute-start | bytes 1769480 | tf_op jit(solution)/shard_map/ppermute | solution.py:274
  129.4 16.7 %collective-permute-start.23 = (bf16[3,128,768]{2,1,0:T(8,128)(2,1)S(1)}, bf16[3,128,768]{2,1,0:T(8,128)(2,1)S(1)}, u32[]{:S(2)}, u32[]{:S(2)}) collective-permute-start(bf16[3,128,768]{2,1,0:T(8,128)(2,1)S(1)} %get-tuple-element.32), channel_id=1, source_target_pairs={{0,32},{32,64},{64,96},{96,0},{1,33},{33,65},{65,97},{97,1},{2,34}... | collective-permute-start | bytes 1769480 | tf_op jit(solution)/shard_map/ppermute | solution.py:273
  129.4 25.9 %collective-permute-start.21 = (bf16[3,128,768]{2,1,0:T(8,128)(2,1)S(1)}, bf16[3,128,768]{2,1,0:T(8,128)(2,1)S(1)}, u32[]{:S(2)}, u32[]{:S(2)}) collective-permute-start(bf16[3,128,768]{2,1,0:T(8,128)(2,1)S(1)} %get-tuple-element.30), channel_id=1, source_target_pairs={{0,96},{32,0},{64,32},{96,64},{1,97},{33,1},{65,33},{97,65},{2,98}... | collective-permute-start | bytes 1769480 | tf_op jit(solution)/shard_map/ppermute | solution.py:275
  142.1 4.0 %copy-start.4 = (bf16[2,2,3,128,768]{4,3,2,1,0:T(8,128)(2,1)S(1)}, bf16[2,2,3,128,768]{4,3,2,1,0:T(8,128)(2,1)}, u32[]{:S(2)}) copy-start(bf16[2,2,3,128,768]{4,3,2,1,0:T(8,128)(2,1)} %weight_terms.2) | copy-start | bytes 7077892
  142.5 15.0 %collective-permute-start.18 = (bf16[2,32,2176]{2,1,0:T(8,128)(2,1)S(1)}, bf16[2,32,2176]{2,1,0:T(8,128)(2,1)S(1)}, u32[]{:S(2)}, u32[]{:S(2)}) collective-permute-start(bf16[2,32,2176]{2,1,0:T(8,128)(2,1)S(1)} %bitcast.88), channel_id=1, source_target_pairs={{0,4},{2,6},{4,0},{6,2},{1,5},{3,7},{5,1},{7,3},{8,12},{10,14},{12... | collective-permute-start | bytes 835592 | tf_op jit(solution)/shard_map/ppermute | solution.py:290
  143.1 16.2 %collective-permute-start.17 = (bf16[2,32,2176]{2,1,0:T(8,128)(2,1)S(1)}, bf16[2,32,2176]{2,1,0:T(8,128)(2,1)S(1)}, u32[]{:S(2)}, u32[]{:S(2)}) collective-permute-start(bf16[2,32,2176]{2,1,0:T(8,128)(2,1)S(1)} %bitcast.87), channel_id=1, source_target_pairs={{0,6},{2,4},{4,2},{6,0},{1,7},{3,5},{5,3},{7,1},{8,14},{10,12},{12... | collective-permute-start | bytes 835592 | tf_op jit(solution)/shard_map/ppermute | solution.py:290
  146.1 14.8 %collective-permute-start.16 = (bf16[2,32,2176]{2,1,0:T(8,128)(2,1)S(1)}, bf16[2,32,2176]{2,1,0:T(8,128)(2,1)S(1)}, u32[]{:S(2)}, u32[]{:S(2)}) collective-permute-start(bf16[2,32,2176]{2,1,0:T(8,128)(2,1)S(1)} %bitcast.86), channel_id=1, source_target_pairs={{0,2},{2,0},{4,6},{6,4},{1,3},{3,1},{5,7},{7,5},{8,10},{10,8},{12,... | collective-permute-start | bytes 835592 | tf_op jit(solution)/shard_map/ppermute | solution.py:290
  155.3 31.6 %collective-permute-start.20 = (bf16[3,128,768]{2,1,0:T(8,128)(2,1)}, bf16[3,128,768]{2,1,0:T(8,128)(2,1)S(1)}, u32[]{:S(2)}, u32[]{:S(2)}) collective-permute-start(bf16[3,128,768]{2,1,0:T(8,128)(2,1)} %slice_bitcast_fusion.6), channel_id=1, source_target_pairs={{0,32},{32,64},{64,96},{96,0},{1,33},{33,65},{65,97},{97,1},{2,34}... | collective-permute-start | bytes 1769480 | tf_op jit(solution)/shard_map/ppermute | solution.py:276
  157.6 27.5 %collective-permute-start.24 = (bf16[3,128,768]{2,1,0:T(8,128)(2,1)S(1)}, bf16[3,128,768]{2,1,0:T(8,128)(2,1)S(1)}, u32[]{:S(2)}, u32[]{:S(2)}) collective-permute-start(bf16[3,128,768]{2,1,0:T(8,128)(2,1)S(1)} %fusion), channel_id=1, source_target_pairs={{0,32},{32,64},{64,96},{96,0},{1,33},{33,65},{65,97},{97,1},{2,34}... | collective-permute-start | bytes 1769480 | tf_op jit(solution)/shard_map/ppermute | solution.py:277
  159.2 27.7 %collective-permute-start.22 = (bf16[3,128,768]{2,1,0:T(8,128)(2,1)S(1)}, bf16[3,128,768]{2,1,0:T(8,128)(2,1)S(1)}, u32[]{:S(2)}, u32[]{:S(2)}) collective-permute-start(bf16[3,128,768]{2,1,0:T(8,128)(2,1)S(1)} %fusion.3), channel_id=1, source_target_pairs={{0,96},{32,0},{64,32},{96,64},{1,97},{33,1},{65,33},{97,65},{2,98}... | collective-permute-start | bytes 1769480 | tf_op jit(solution)/shard_map/ppermute | solution.py:278
  161.0 24.4 %collective-permute-start.19 = (bf16[32,2176]{1,0:T(8,128)(2,1)S(1)}, bf16[32,2176]{1,0:T(8,128)(2,1)S(1)}, u32[]{:S(2)}, u32[]{:S(2)}) collective-permute-start(bf16[32,2176]{1,0:T(8,128)(2,1)S(1)} %slice_bitcast_fusion.8), channel_id=1, source_target_pairs={{0,8},{8,0},{16,24},{24,16},{1,9},{9,1},{17,25},{25,17},{2,10},{10... | collective-permute-start | bytes 417800 | tf_op jit(solution)/shard_map/ppermute | solution.py:292
  185.3 14.6 %collective-permute-start.26 = (bf16[3,128,768]{2,1,0:T(8,128)(2,1)S(1)}, bf16[3,128,768]{2,1,0:T(8,128)(2,1)}, u32[]{:S(2)}, u32[]{:S(2)}) collective-permute-start(bf16[3,128,768]{2,1,0:T(8,128)(2,1)S(1)} %fusion.2), channel_id=1, source_target_pairs={{0,8},{8,0},{16,24},{24,16},{1,9},{9,1},{17,25},{25,17},{2,10},{10... | collective-permute-start | bytes 1769480 | tf_op jit(solution)/shard_map/ppermute | solution.py:280

commit v2 on v1

v2 whole, which is shorter than its diff:
```python
import functools

import jax
import jax.numpy as jnp
from jax import lax
from jax.experimental import pallas as pl
from jax.experimental.pallas import tpu as pltpu
from jax.sharding import Mesh, PartitionSpec as P

F32 = jnp.float32
BF16 = jnp.bfloat16
LANES = 128
SIDE = 4
VMEM = 44 << 20

X_ORDER = ((1, 3, 2), (3, 1, 2))
Z_ORDER = (1, 3, 2)
PAIR = (1, 3)


def plane(step, first):
    pairs = []
    for x in range(SIDE):
        for z in range(SIDE):
            for core in range(2):
                if (core == 0) == first:
                    to = (x ^ X_ORDER[core][step], z)
                else:
                    to = (x, z ^ Z_ORDER[step])
                pairs.append(((x * SIDE + z) * 2 + core, (to[0] * SIDE + to[1]) * 2 + core))
    return pairs


SWAP = [(0, 1), (1, 0)]
Z_MOVE = [[(j, j ^ k) for j in range(SIDE)] for k in Z_ORDER]
X_PAIR = [(x * 2 + c, (x ^ PAIR[c]) * 2 + c) for x in range(SIDE) for c in range(2)]
RING = [(y * 2 + c, ((y + 1 - 2 * c) % SIDE) * 2 + c) for y in range(SIDE) for c in range(2)]


def forward_kernel(width, blocks, cols_ref, *refs):
    row_refs = refs[: 2 * blocks]
    sel_ref, gate_ref, up_ref, down_ref = refs[2 * blocks : 2 * blocks + 4]
    h_ref, gp_ref, xs_ref, ds_ref = refs[2 * blocks + 4 :]
    step = pl.program_id(0)
    half = row_refs[0].shape[0]
    for block in range(blocks):
        pair = row_refs[2 * block : 2 * block + 2]
        rows = slice(2 * half * block, 2 * half * (block + 1))
        x = jnp.concatenate([r[:, :width] for r in pair], axis=0)
        dy = jnp.concatenate([r[:, width : 2 * width] for r in pair], axis=0)
        p = jnp.concatenate([r[:, 2 * width :] for r in pair], axis=0).astype(F32)
        p = jnp.sum(p * sel_ref[...], axis=-1, keepdims=True)
        gate = jnp.dot(x, gate_ref[...], preferred_element_type=F32)
        up = jnp.dot(x, up_ref[...], preferred_element_type=F32)
        back = jnp.dot(dy, down_ref[...], preferred_element_type=F32)
        sig = 1.0 / (1.0 + jnp.exp(-gate))
        act = gate * sig
        hidden = act * up
        hidden_grad = p * back
        h_ref[0, rows] = (hidden_grad * up * (sig * (1.0 + gate * (1.0 - sig)))).astype(BF16)
        h_ref[1, rows] = (hidden_grad * act).astype(BF16)
        h_ref[2, rows] = (p * hidden).astype(BF16)
        term = jnp.sum(hidden * back, axis=-1, keepdims=True) * sel_ref[...]

        @pl.when(step == 0)
        def _():
            gp_ref[rows] = term

        @pl.when(step != 0)
        def _():
            gp_ref[rows] = gp_ref[rows] + term

    @pl.when(step == 0)
    def _():
        for n in range(xs_ref.shape[1] // LANES):
            for piece, ref in enumerate(row_refs):
                rows = slice(half * piece, half * (piece + 1))
                to = slice(n * LANES, (n + 1) * LANES)
                xs_ref[rows, to] = ref[:, pl.ds(pl.multiple_of(cols_ref[n] * LANES, LANES), LANES)]
                ds_ref[rows, to] = ref[:, pl.ds(pl.multiple_of(width + cols_ref[n] * LANES, LANES), LANES)]


def forward(cols, pieces, sel, gate_up, down):
    half, columns = pieces[0].shape
    width, hidden = down.shape
    tokens = len(pieces) * half
    count = cols.shape[0]
    tile = 256
    whole = lambda shape, **kw: pl.BlockSpec(shape, lambda j, cols: (0,) * len(shape), **kw)
    return pl.pallas_call(
        functools.partial(forward_kernel, width, len(pieces) // 2),
        name="forward",
        grid_spec=pltpu.PrefetchScalarGridSpec(
            num_scalar_prefetch=1,
            grid=(hidden // tile,),
            in_specs=[whole((half, columns), pipeline_mode=pl.Buffered(1))] * len(pieces)
            + [
                whole((1, LANES)),
                pl.BlockSpec((None, width, tile), lambda j, cols: (0, 0, j)),
                pl.BlockSpec((None, width, tile), lambda j, cols: (1, 0, j)),
                pl.BlockSpec((width, tile), lambda j, cols: (0, j)),
            ],
            out_specs=[
                pl.BlockSpec((3, tokens, tile), lambda j, cols: (0, 0, j)),
                whole((tokens, LANES)),
                whole((tokens, count * LANES)),
                whole((tokens, count * LANES)),
            ],
        ),
        out_shape=[
            jax.ShapeDtypeStruct((3, tokens, hidden), BF16),
            jax.ShapeDtypeStruct((tokens, LANES), F32),
            jax.ShapeDtypeStruct((tokens, count * LANES), BF16),
            jax.ShapeDtypeStruct((tokens, count * LANES), BF16),
        ],
        compiler_params=pltpu.CompilerParams(vmem_limit_bytes=VMEM),
        cost_estimate=pl.CostEstimate(
            flops=6 * tokens * width * hidden, bytes_accessed=6 * width * hidden, transcendentals=0
        ),
    )(cols, *pieces, sel, gate_up, gate_up, down)


def weight_kernel(x_ref, dy_ref, h_ref, other_ref, own_ref):
    kind = pl.program_id(0)
    contract = (((0,), (0,)), ((), ()))

    def store(rows_ref):
        total = lax.dot_general(rows_ref[...], h_ref[...], contract, preferred_element_type=F32)
        other_ref[...] = total[:LANES].astype(BF16)
        own_ref[...] = total[LANES:].astype(BF16)

    @pl.when(kind < 2)
    def _():
        store(x_ref)

    @pl.when(kind == 2)
    def _():
        store(dy_ref)


def weight_terms(xs, ds, h, start, steps):
    _, tokens, hidden = h.shape
    column = pl.BlockSpec((tokens, 2 * LANES), lambda k, j: (0, start + j))
    out = jax.ShapeDtypeStruct((steps, 3, LANES, hidden), BF16)
    return pl.pallas_call(
        weight_kernel,
        name="weight_terms",
        grid=(3, steps),
        in_specs=[column, column, pl.BlockSpec((None, tokens, hidden), lambda k, j: (k, 0, 0))],
        out_specs=[pl.BlockSpec((None, None, LANES, hidden), lambda k, j: (j, k, 0, 0))] * 2,
        out_shape=[out, out],
        compiler_params=pltpu.CompilerParams(vmem_limit_bytes=VMEM),
        cost_estimate=pl.CostEstimate(
            flops=12 * steps * tokens * LANES * hidden,
            bytes_accessed=6 * tokens * hidden,
            transcendentals=0,
        ),
    )(xs, ds, h)


def slot_rows(core, tokens):
    order = []
    for x in range(2):
        for which in range(2):
            place = 0 if x == 0 else 1 + which
            for z in range(SIDE):
                block, inner = (z, place) if which == core else (place, z)
                order.append(((block * 2 + which) * SIDE + inner) * tokens)
    return order


def slot_kernel(tokens, width, core_ref, h_ref, gp_ref, gate_ref, up_ref, own_ref, pair_ref, rows_ref):
    step = pl.program_id(0)
    half = own_ref.shape[0]

    @pl.when(step == 0)
    def _():
        for core in range(2):

            @pl.when(core_ref[0] == core)
            def _():
                for n, at in enumerate(slot_rows(core, tokens)):
                    to = slice(n * tokens, (n + 1) * tokens)
                    rows_ref[:, to] = h_ref[:, at : at + tokens]
                    out, first = (own_ref, 0) if n * tokens < half else (pair_ref, half)
                    out[n * tokens - first : (n + 1) * tokens - first, width:] = gp_ref[
                        at : at + tokens
                    ].astype(BF16)

    contract = (((1,), (1,)), ((), ()))
    tile = gate_ref.shape[0]
    cols = pl.ds(pl.multiple_of(step * tile, tile), tile)
    total = lax.dot_general(rows_ref[0], gate_ref[...], contract, preferred_element_type=F32)
    total += lax.dot_general(rows_ref[1], up_ref[...], contract, preferred_element_type=F32)
    own_ref[:, cols] = total[:half].astype(BF16)
    pair_ref[:, cols] = total[half:].astype(BF16)


def slot_terms(core, h, gp, gate_up, tokens):
    _, width, hidden = gate_up.shape
    tile = 512
    half = 2 * SIDE * tokens
    out = jax.ShapeDtypeStruct((half, width + LANES), BF16)
    return pl.pallas_call(
        functools.partial(slot_kernel, tokens, width),
        name="slot_terms",
        grid_spec=pltpu.PrefetchScalarGridSpec(
            num_scalar_prefetch=1,
            grid=(width // tile,),
            in_specs=[
                pl.BlockSpec((2,) + h.shape[1:], lambda j, core: (0, 0, 0)),
                pl.BlockSpec(gp.shape, lambda j, core: (0, 0)),
                pl.BlockSpec((None, tile, hidden), lambda j, core: (0, j, 0)),
                pl.BlockSpec((None, tile, hidden), lambda j, core: (1, j, 0)),
            ],
            out_specs=[pl.BlockSpec(out.shape, lambda j, core: (0, 0))] * 2,
            scratch_shapes=[pltpu.VMEM((2, 2 * half, hidden), BF16)],
        ),
        out_shape=[out, out],
        compiler_params=pltpu.CompilerParams(vmem_limit_bytes=VMEM),
        cost_estimate=pl.CostEstimate(
            flops=8 * half * width * hidden, bytes_accessed=4 * width * hidden, transcendentals=0
        ),
    )(core[None].astype(jnp.int32), h, gp, gate_up, gate_up)


def add(*terms):
    total = terms[0].astype(F32)
    for term in terms[1:]:
        total = total + term.astype(F32)
    return total.astype(BF16)


def shards(layer_input, out_grad, routes, probs, gate_up, down_t):
    tokens, width = layer_input.shape
    x, y = lax.axis_index("x"), lax.axis_index("y")
    z, core = lax.axis_index("z"), lax.axis_index("core")
    expert = x % 2
    lane = lax.broadcasted_iota(jnp.int32, (1, LANES), 1)
    sel = (lane == (z * 2 + core) * 2 + expert).astype(F32)

    hot = routes[:, :, None] == lax.broadcasted_iota(jnp.int32, (1, 1, LANES), 2)
    dense = jnp.sum(jnp.where(hot, probs.astype(F32)[:, :, None], 0.0), axis=1).astype(BF16)
    row = jnp.concatenate([layer_input, out_grad, dense], axis=1)

    axes = ("x", "z", "core")
    line = [row] + [lax.ppermute(row, axes, plane(n, True)) for n in range(3)]
    line = jnp.concatenate(line, axis=0)
    mine = [line] + [lax.ppermute(line, axes, plane(n, False)) for n in range(3)]

    gate_up = jnp.where(expert == 0, gate_up[:, :, 0], gate_up[:, :, 1])
    gate_up = jnp.transpose(gate_up, (1, 0, 2))
    down = jnp.where(expert == 0, down_t[:, 0], down_t[:, 1])
    line, gate_up, down = lax.optimization_barrier((line, gate_up, down))
    pieces = []
    for n, piece in enumerate(mine):
        pieces += [piece, lax.ppermute(line if n == 0 else piece, "core", SWAP)]

    cols = []
    pair = x ^ jnp.where(core == 0, PAIR[0], PAIR[1])
    for n in (3, 2, 1, 0):
        base = SIDE * ((y + jnp.where(core == 0, n, SIDE - n)) % SIDE)
        cols += [base + pair, base + x]
    cols = jnp.stack(cols).astype(jnp.int32)
    h, gp, xs, ds = forward(cols, pieces, sel, gate_up, down)

    first = weight_terms(xs, ds, h, 0, 1)
    other = lax.ppermute(first[0][0], ("y", "core"), RING)
    own = lax.ppermute(first[1][0], ("y", "core"), RING)
    rest = weight_terms(xs, ds, h, 1, 3)
    h_late, _ = lax.optimization_barrier((h, rest[0]))
    part, away = slot_terms(core, h_late, gp, gate_up, tokens)

    part = add(part, lax.ppermute(away, ("x", "core"), X_PAIR))
    half = part.shape[0] // 2
    part = add(part[:half], lax.ppermute(part[half:], "core", SWAP))
    part = part.reshape((SIDE, tokens, part.shape[1]))
    total = part[0].astype(F32)
    for n in range(3):
        total = total + lax.ppermute(part[n + 1], "z", Z_MOVE[n]).astype(F32)
    grad_input = total[:, :width].astype(BF16)
    grad_prob = jnp.sum(jnp.where(hot, total[:, None, width:], 0.0), axis=2)

    for n in range(2):
        other = lax.ppermute(add(rest[0][n], other), ("y", "core"), RING)
        own = lax.ppermute(add(rest[1][n], own), ("y", "core"), RING)
    other = lax.ppermute(add(rest[0][2], other), ("x", "core"), X_PAIR)
    own = add(rest[1][2], own)
    even, odd = jnp.where(expert == 0, own, other), jnp.where(expert == 0, other, own)
    grad_weights = jnp.transpose(jnp.stack([even, odd], axis=0), (2, 1, 0, 3))
    return (grad_input, grad_prob, grad_weights)


def solution(mesh):
    grid = Mesh(mesh.devices.reshape(4, 4, 4, 2), ("y", "x", "z", "core"))
    every = P(("y", "x", "z", "core"), None)
    return jax.shard_map(
        shards,
        mesh=grid,
        in_specs=(every, every, every, every, P(None, None, ("z", "core"), None), P(None, ("z", "core"), None)),
        out_specs=(every, every, P(("y", "x"), None, ("z", "core"), None)),
        check_vma=False,
    )
```

time: 204 us -> 180 us (0.88)
  waiting for transfers between devices: 60.5 us -> 40 us
  other arithmetic: 5.13 us -> 21.8 us
  starting transfers between devices: 37.9 us -> 24.9 us
  Pallas kernels: 49.8 us -> 42.1 us
    slice x4 -> x6, local copies, waits for them, and re-layouts: 1.45 us -> 36.2 us  [the longest x1 25.3 us: shards(): gate_up = jnp.where(expert == 0, gate_up[:, :, 0], gate_up[:, :, 1])]
    dynamic_slice x3 -> x0, local copies, waits for them, and re-layouts: 31.7 us -> none  [the longest x2 23.9 us: shards(): lax.dynamic_index_in_dim(gate_up, expert, 2, keepdims=False)]
    ppermute x27 -> x22, waiting for transfers between devices: 60.5 us -> 40 us  [the longest x2 11.7 us: shards(): other = lax.ppermute(add(rest[0][n], other), ('y', 'core'), RING)]
    ppermute x27 -> x22, starting transfers between devices: 37.9 us -> 24.9 us  [the longest x3 5.58 us: shards(): lax.ppermute(line, axes, plane(n, False))]
    transpose x0 -> x1, other arithmetic: none -> 9.57 us  [shards(): gate_up = jnp.transpose(gate_up, (1, 0, 2))]
    pallas_call x6 -> x4, Pallas kernels: 49.8 us -> 42.1 us  [the longest x1 24.2 us: forward(): pl.pallas_call(functools.partial(forward_kernel, width, len(pieces) // 2)...]
    select_n x0 -> x1, other arithmetic: none -> 7.07 us  [shards(): down = jnp.where(expert == 0, down_t[:, 0], down_t[:, 1])]
    squeeze x3 -> x0, local copies, waits for them, and re-layouts: 3.47 us -> none  [the longest x1 1.92 us: shards(): b_right = lax.ppermute(close[0, 1], 'y', RIGHT)]
  transfers between devices with their start and end apart: 27 -> 22, of which waited for: 8 -> 11; matrix products, arithmetic and copies ran while one was open for 23% -> 31% of each run, Pallas kernels for 15% -> 3%
where the time goes in v2:
time: 180 us; the launch traced here: 178 us
  local copies, waits for them, and re-layouts  48.6 us (27%)
  Pallas kernels  42.1 us (23%)
  waiting for transfers between devices  40 us (22%)
  starting transfers between devices  24.9 us (14%)
  other arithmetic  21.8 us (12%)
    slice x1, local copies, waits for them, and re-layouts, shards(): gate_up = jnp.where(expert == 0, gate_up[:, :, 0], gate_up[:, :, 1])  25.3 us
    pallas_call x1, Pallas kernels, forward(): pl.pallas_call(functools.partial(forward_kernel, width, len(pieces) // 2)...  24.2 us
    pallas_call x2, Pallas kernels, weight_terms(): pl.pallas_call(weight_kernel, name='weight_terms', grid=(3, steps), in_sp...  11.8 us
    ppermute x2, waiting for transfers between devices, shards(): other = lax.ppermute(add(rest[0][n], other), ('y', 'core'), RING)  11.7 us
    unnamed x27, local copies, waits for them, and re-layouts  11.6 us
    slice x1, local copies, waits for them, and re-layouts, shards(): down = jnp.where(expert == 0, down_t[:, 0], down_t[:, 1])  10.1 us
    transpose x1, other arithmetic, shards(): gate_up = jnp.transpose(gate_up, (1, 0, 2))  9.57 us
    ppermute x1, waiting for transfers between devices, shards(): other = lax.ppermute(first[0][0], ('y', 'core'), RING)  8.02 us
  transfers between devices with their start and end apart: 22, of which 11 were waited for; matrix products, arithmetic and copies ran while one was open for 31% of the time, Pallas kernels for 3%

profile of v2, /device:TPU:0, one launch (start us, length us, event | category | flops | bytes accessed | tf_op | source)
XLA Modules:
  0.0 178.2 jit_solution(10109183550080198985)
XLA Ops:
  3.5 1.7 collective-permute-start
  5.1 2.1 %collective-permute-start.1 = (bf16[32,4224]{1,0:T(8,128)(2,1)S(1)}, bf16[32,4224]{1,0:T(8,128)(2,1)S(1)}, u32[]{:S(2)}, u32[]{:S(2)}) collective-permute-start(bf16[32,4224]{1,0:T(8,128)(2,1)S(1)} %pad_maximum_fusion.1), channel_id=1, source_target_pairs={{0,24},{1,7},{2,26},{3,5},{4,28},{5,3},{6,30},{7,1},{8,16},{9,15},... | collective-permute-start | bytes 811016 | tf_op jit(solution)/shard_map/ppermute | solution.py:247
  7.9 25.3 %fusion.8 = (bf16[2048,2,1,768]{3,2,1,0:T(2,128)(2,1)}, bf16[2048,2,1,768]{3,2,1,0:T(2,128)(2,1)}) fusion(bf16[2048,2,2,768]{3,2,1,0:T(2,128)(2,1)} %param.10), kind=kLoop, calls=%fused_computation.29 | loop fusion | bytes 25165824 | tf_op jit(solution)/shard_map/slice | solution.py:251
  33.2 10.1 %fusion.9 = (bf16[2048,1,768]{2,1,0:T(2,128)(2,1)}, bf16[2048,1,768]{2,1,0:T(2,128)(2,1)}) fusion(bf16[2048,2,768]{2,1,0:T(2,128)(2,1)S(1)} %bitcast.50), kind=kLoop, calls=%fused_computation.30 | loop fusion | bytes 12582912 | tf_op jit(solution)/shard_map/slice | solution.py:253
  43.5 2.0 %collective-permute-start.4 = (bf16[128,4224]{1,0:T(8,128)(2,1)S(1)}, bf16[128,4224]{1,0:T(8,128)(2,1)S(1)}, u32[]{:S(2)}, u32[]{:S(2)}) collective-permute-start(bf16[128,4224]{1,0:T(8,128)(2,1)S(1)} %pad_maximum_fusion.refs_0_), channel_id=1, source_target_pairs={{0,2},{1,25},{2,0},{3,27},{4,6},{5,29},{6,4},{7,31},{8,10},{9,17},... | collective-permute-start | bytes 3244040 | tf_op jit(solution)/shard_map/ppermute | solution.py:249
  45.5 2.5 %collective-permute-start.6 = (bf16[128,4224]{1,0:T(8,128)(2,1)S(1)}, bf16[128,4224]{1,0:T(8,128)(2,1)S(1)}, u32[]{:S(2)}, u32[]{:S(2)}) collective-permute-start(bf16[128,4224]{1,0:T(8,128)(2,1)S(1)} %pad_maximum_fusion.refs_0_), channel_id=1, source_target_pairs={{0,6},{1,9},{2,4},{3,11},{4,2},{5,13},{6,0},{7,15},{8,14},{9,1},{1... | collective-permute-start | bytes 3244040 | tf_op jit(solution)/shard_map/ppermute | solution.py:249
  49.0 7.1 %fusion.1.refs_11_ = bf16[2048,768]{1,0:T(8,128)(2,1)} fusion(bf16[2048,1,768]{2,1,0:T(2,128)(2,1)} %get-tuple-element.40, bf16[2048,1,768]{2,1,0:T(2,128)(2,1)} %get-tuple-element.39, pred[]{:T(512)S(6)} %eq.50), kind=kLoop, calls=%fused_computation.3 | loop fusion | flops 1572864 | bytes 9437185 | tf_op jit(solution)/shard_map/jit(_where)/select_n | solution.py:253
  56.1 2.2 %copy-done.5 = bf16[2048,2,1,768]{3,2,1,0:T(2,128)(2,1)S(1)} copy-done((bf16[2048,2,1,768]{3,2,1,0:T(2,128)(2,1)S(1)}, bf16[2048,2,1,768]{3,2,1,0:T(2,128)(2,1)}, u32[]{:S(2)}) %copy-start.5) | copy-done | bytes 6291480
  58.4 9.6 %fusion.refs_9_.refs_10_.gate_ref.up_ref = bf16[2,2048,768]{2,1,0:T(8,128)(2,1)} fusion(bf16[2048,2,1,768]{3,2,1,0:T(2,128)(2,1)} %get-tuple-element.38, bf16[2048,2,1,768]{3,2,1,0:T(2,128)(2,1)S(1)} %copy-done.5, pred[]{:T(512)S(6)} %eq.50), kind=kLoop, calls=%fused_computation.1 | loop fusion | flops 3145728 | bytes 18874368 | tf_op jit(solution)/shard_map/transpose | solution.py:252
  68.4 3.8 %collective-permute-done.6.refs_4_ = bf16[128,4224]{1,0:T(8,128)(2,1)S(1)} collective-permute-done((bf16[128,4224]{1,0:T(8,128)(2,1)S(1)}, bf16[128,4224]{1,0:T(8,128)(2,1)S(1)}, u32[]{:S(2)}, u32[]{:S(2)}) %collective-permute-start.6) | collective-permute-done | bytes 1081376 | tf_op jit(solution)/shard_map/ppermute | solution.py:249
  72.2 1.6 collective-permute-done.8.refs_6_
  75.1 1.8 %collective-permute-done.9.refs_7_ = bf16[128,4224]{1,0:T(8,128)(2,1)} collective-permute-done((bf16[128,4224]{1,0:T(8,128)(2,1)}, bf16[128,4224]{1,0:T(8,128)(2,1)}, u32[]{:S(2)}, u32[]{:S(2)}) %collective-permute-start.9) | collective-permute-done | bytes 1081376 | tf_op jit(solution)/shard_map/ppermute | solution.py:257
  76.9 24.2 %forward.1 = (bf16[3,1024,768]{2,1,0:T(8,128)(2,1)}, f32[1024,128]{1,0:T(8,128)S(1)}, bf16[1024,1024]{1,0:T(8,128)(2,1)}, bf16[1024,1024]{1,0:T(8,128)(2,1)}) custom-call(s32[8]{0:T(128)S(1)} %stack.44.cols_ref, bf16[128,4224]{1,0:T(8,128)(2,1)S(1)} %pad_maximum_fusion.refs_0_, bf16[128,4224]{1,0:T(8,128)(2,1)} %collective-permute-done.3.refs_1_, ...), custom_call_target="tpu_custom_call" | custom-call | flops 9663676416 | bytes 9437184 | tf_op jit(solution)/shard_map/forward/pallas_call | solution.py:90
  101.1 2.3 %copy-done = bf16[3,1024,768]{2,1,0:T(8,128)(2,1)S(1)} copy-done((bf16[3,1024,768]{2,1,0:T(8,128)(2,1)S(1)}, bf16[3,1024,768]{2,1,0:T(8,128)(2,1)}, u32[]{:S(2)}) %copy-start) | copy-done | bytes 4718616
  103.5 1.6 copy-done.1
  105.1 1.6 copy-done.3
  106.7 2.1 %weight_terms.3 = (bf16[1,3,128,768]{3,2,1,0:T(8,128)(2,1)S(1)}, bf16[1,3,128,768]{3,2,1,0:T(8,128)(2,1)S(1)}) custom-call(bf16[1024,1024]{1,0:T(8,128)(2,1)S(1)} %copy-done.1, bf16[1024,1024]{1,0:T(8,128)(2,1)S(1)} %copy-done.3, bf16[3,1024,768]{2,1,0:T(8,128)(2,1)S(1)} %copy-done), custom_call_target="tpu_custom_call" | custom-call | flops 1207959552 | bytes 4718592 | tf_op jit(solution)/shard_map/weight_terms/pallas_call | solution.py:145
  108.9 9.8 %weight_terms.2 = (bf16[3,3,128,768]{3,2,1,0:T(8,128)(2,1)S(1)}, bf16[3,3,128,768]{3,2,1,0:T(8,128)(2,1)S(1)}) custom-call(bf16[1024,1024]{1,0:T(8,128)(2,1)S(1)} %copy-done.2, bf16[1024,1024]{1,0:T(8,128)(2,1)S(1)} %copy-done.4, bf16[3,1024,768]{2,1,0:T(8,128)(2,1)} %get-tuple-element.24.h_ref), custom_call_target="tpu_custom_call" | custom-call | flops 3623878656 | bytes 4718592 | tf_op jit(solution)/shard_map/weight_terms/pallas_call | solution.py:145
  118.6 1.6 collective-permute-start.15
  120.3 6.0 %slot_terms.1 = (bf16[256,2176]{1,0:T(8,128)(2,1)S(1)}, bf16[256,2176]{1,0:T(8,128)(2,1)S(1)}) custom-call(s32[1]{0:T(128)} %bitcast.core_ref, bf16[3,1024,768]{2,1,0:T(8,128)(2,1)S(1)} %bitcast.46, f32[1024,128]{1,0:T(8,128)S(1)} %get-tuple-element.25.gp_ref, bf16[2,2048,768]{2,1,0:T(8,128)(2,1)} %fusion.refs_9_.refs_10_.gate_ref.up_ref, ...), custom_call_target="tpu_custom_call" | custom-call | flops 3221225472 | bytes 6291456 | tf_op jit(solution)/shard_map/slot_terms/pallas_call | solution.py:204
  126.3 1.5 collective-permute-start.10
  127.8 1.6 collective-permute-start.18
  130.8 8.0 %collective-permute-done.18 = bf16[3,128,768]{2,1,0:T(8,128)(2,1)S(1)} collective-permute-done((bf16[3,128,768]{2,1,0:T(8,128)(2,1)S(1)}, bf16[3,128,768]{2,1,0:T(8,128)(2,1)S(1)}, u32[]{:S(2)}, u32[]{:S(2)}) %collective-permute-start.18) | collective-permute-done | bytes 589856 | tf_op jit(solution)/shard_map/ppermute | solution.py:268
  139.4 2.5 %collective-permute-done.10 = bf16[256,2176]{1,0:T(8,128)(2,1)S(1)} collective-permute-done((bf16[256,2176]{1,0:T(8,128)(2,1)S(1)}, bf16[256,2176]{1,0:T(8,128)(2,1)S(1)}, u32[]{:S(2)}, u32[]{:S(2)}) %collective-permute-start.10) | collective-permute-done | bytes 1114144 | tf_op jit(solution)/shard_map/ppermute | solution.py:274
  142.2 1.7 collective-permute-start.11
  146.5 5.0 %collective-permute-done.19 = bf16[3,128,768]{2,1,0:T(8,128)(2,1)S(1)} collective-permute-done((bf16[3,128,768]{2,1,0:T(8,128)(2,1)S(1)}, bf16[3,128,768]{2,1,0:T(8,128)(2,1)S(1)}, u32[]{:S(2)}, u32[]{:S(2)}) %collective-permute-start.19) | collective-permute-done | bytes 589856 | tf_op jit(solution)/shard_map/ppermute | solution.py:285
  152.3 1.5 collective-permute-start.12
  153.7 2.6 %collective-permute-start.13 = (bf16[32,2176]{1,0:T(8,128)(2,1)S(1)}, bf16[32,2176]{1,0:T(8,128)(2,1)S(1)}, u32[]{:S(2)}, u32[]{:S(2)}) collective-permute-start(bf16[32,2176]{1,0:T(8,128)(2,1)S(1)} %get-tuple-element.45), channel_id=1, source_target_pairs={{0,6},{2,4},{4,2},{6,0},{1,7},{3,5},{5,3},{7,1},{8,14},{10,12},{12... | collective-permute-start | bytes 417800 | tf_op jit(solution)/shard_map/ppermute | solution.py:280
  157.4 6.7 %collective-permute-done.20 = bf16[3,128,768]{2,1,0:T(8,128)(2,1)S(1)} collective-permute-done((bf16[3,128,768]{2,1,0:T(8,128)(2,1)S(1)}, bf16[3,128,768]{2,1,0:T(8,128)(2,1)S(1)}, u32[]{:S(2)}, u32[]{:S(2)}) %collective-permute-start.20) | collective-permute-done | bytes 589856 | tf_op jit(solution)/shard_map/ppermute | solution.py:285
  166.6 7.7 %collective-permute-done.21 = bf16[3,128,768]{2,1,0:T(8,128)(2,1)} collective-permute-done((bf16[3,128,768]{2,1,0:T(8,128)(2,1)S(1)}, bf16[3,128,768]{2,1,0:T(8,128)(2,1)}, u32[]{:S(2)}, u32[]{:S(2)}) %collective-permute-start.21) | collective-permute-done | bytes 589856 | tf_op jit(solution)/shard_map/ppermute | solution.py:287
  174.3 1.5 select_bitcast_fusion.1
  176.0 2.2 %copy.23 = bf16[128,3,2,768]{3,2,1,0:T(2,128)(2,1)} copy(bf16[128,3,2,768]{3,0,1,2:T(8,128)(2,1)S(1)} %maximum_bitcast_fusion) | data formatting | bytes 2359296
  (70 shorter events, 15.8 us)
Async XLA Ops:
  2.3 30.9 %slice-start.2 = ((s8[6291456]{0:T(1024)(128)(4,1)}), s8[4194304]{0:T(1024)(128)(4,1)S(1)}, s32[]{:S(2)}) async-start(s8[6291456]{0:T(1024)(128)(4,1)} %bitcast.49), calls=%async_computation.2 | async-start | bytes 8388608
  3.5 29.7 %slice-start.3 = ((s8[6291456]{0:T(1024)(128)(4,1)}), s8[2097152]{0:T(1024)(128)(4,1)S(1)}, s32[]{:S(2)}) async-start(s8[6291456]{0:T(1024)(128)(4,1)} %bitcast.49), calls=%async_computation.3 | async-start | bytes 4194304
  3.5 39.9 %collective-permute-start = (bf16[32,4224]{1,0:T(8,128)(2,1)S(1)}, bf16[32,4224]{1,0:T(8,128)(2,1)S(1)}, u32[]{:S(2)}, u32[]{:S(2)}) collective-permute-start(bf16[32,4224]{1,0:T(8,128)(2,1)S(1)} %pad_maximum_fusion.1), channel_id=1, source_target_pairs={{0,8},{1,3},{2,10},{3,1},{4,12},{5,7},{6,14},{7,5},{8,0},{9,11},{1... | collective-permute-start | bytes 811016 | tf_op jit(solution)/shard_map/ppermute | solution.py:247
  5.1 38.2 %collective-permute-start.1 = (bf16[32,4224]{1,0:T(8,128)(2,1)S(1)}, bf16[32,4224]{1,0:T(8,128)(2,1)S(1)}, u32[]{:S(2)}, u32[]{:S(2)}) collective-permute-start(bf16[32,4224]{1,0:T(8,128)(2,1)S(1)} %pad_maximum_fusion.1), channel_id=1, source_target_pairs={{0,24},{1,7},{2,26},{3,5},{4,28},{5,3},{6,30},{7,1},{8,16},{9,15},... | collective-permute-start | bytes 811016 | tf_op jit(solution)/shard_map/ppermute | solution.py:247
  7.2 36.1 %collective-permute-start.2 = (bf16[32,4224]{1,0:T(8,128)(2,1)S(1)}, bf16[32,4224]{1,0:T(8,128)(2,1)S(1)}, u32[]{:S(2)}, u32[]{:S(2)}) collective-permute-start(bf16[32,4224]{1,0:T(8,128)(2,1)S(1)} %pad_maximum_fusion.1), channel_id=1, source_target_pairs={{0,16},{1,5},{2,18},{3,7},{4,20},{5,1},{6,22},{7,3},{8,24},{9,13},... | collective-permute-start | bytes 811016 | tf_op jit(solution)/shard_map/ppermute | solution.py:247
  33.2 10.1 %copy-start.6 = (bf16[32,2048]{1,0:T(8,128)(2,1)S(1)}, bf16[32,2048]{1,0:T(8,128)(2,1)}, u32[]{:S(2)}) copy-start(bf16[32,2048]{1,0:T(8,128)(2,1)} %param.7) | copy-start | bytes 393220
  33.2 10.1 %copy-start.7 = (bf16[32,2048]{1,0:T(8,128)(2,1)S(1)}, bf16[32,2048]{1,0:T(8,128)(2,1)}, u32[]{:S(2)}) copy-start(bf16[32,2048]{1,0:T(8,128)(2,1)} %param.6) | copy-start | bytes 393220
  43.5 24.5 %collective-permute-start.4 = (bf16[128,4224]{1,0:T(8,128)(2,1)S(1)}, bf16[128,4224]{1,0:T(8,128)(2,1)S(1)}, u32[]{:S(2)}, u32[]{:S(2)}) collective-permute-start(bf16[128,4224]{1,0:T(8,128)(2,1)S(1)} %pad_maximum_fusion.refs_0_), channel_id=1, source_target_pairs={{0,2},{1,25},{2,0},{3,27},{4,6},{5,29},{6,4},{7,31},{8,10},{9,17},... | collective-permute-start | bytes 3244040 | tf_op jit(solution)/shard_map/ppermute | solution.py:249
  45.5 26.8 %collective-permute-start.6 = (bf16[128,4224]{1,0:T(8,128)(2,1)S(1)}, bf16[128,4224]{1,0:T(8,128)(2,1)S(1)}, u32[]{:S(2)}, u32[]{:S(2)}) collective-permute-start(bf16[128,4224]{1,0:T(8,128)(2,1)S(1)} %pad_maximum_fusion.refs_0_), channel_id=1, source_target_pairs={{0,6},{1,9},{2,4},{3,11},{4,2},{5,13},{6,0},{7,15},{8,14},{9,1},{1... | collective-permute-start | bytes 3244040 | tf_op jit(solution)/shard_map/ppermute | solution.py:249
  48.0 25.9 %collective-permute-start.8 = (bf16[128,4224]{1,0:T(8,128)(2,1)S(1)}, bf16[128,4224]{1,0:T(8,128)(2,1)}, u32[]{:S(2)}, u32[]{:S(2)}) collective-permute-start(bf16[128,4224]{1,0:T(8,128)(2,1)S(1)} %pad_maximum_fusion.refs_0_), channel_id=1, source_target_pairs={{0,4},{1,17},{2,6},{3,19},{4,0},{5,21},{6,2},{7,23},{8,12},{9,25},... | collective-permute-start | bytes 3244040 | tf_op jit(solution)/shard_map/ppermute | solution.py:249
  49.0 9.3 %copy-start.5 = (bf16[2048,2,1,768]{3,2,1,0:T(2,128)(2,1)S(1)}, bf16[2048,2,1,768]{3,2,1,0:T(2,128)(2,1)}, u32[]{:S(2)}) copy-start(bf16[2048,2,1,768]{3,2,1,0:T(2,128)(2,1)} %get-tuple-element.37) | copy-start | bytes 18874372
  67.9 6.0 %collective-permute-start.3 = (bf16[128,4224]{1,0:T(8,128)(2,1)S(1)}, bf16[128,4224]{1,0:T(8,128)(2,1)}, u32[]{:S(2)}, u32[]{:S(2)}) collective-permute-start(bf16[128,4224]{1,0:T(8,128)(2,1)S(1)} %pad_maximum_fusion.refs_0_), channel_id=1, source_target_pairs={{0,1},{1,0},{2,3},{3,2},{4,5},{5,4},{6,7},{7,6},{8,9},{9,8},{10,11... | collective-permute-start | bytes 3244040 | tf_op jit(solution)/shard_map/ppermute | solution.py:257
  67.9 6.0 %collective-permute-start.5 = (bf16[128,4224]{1,0:T(8,128)(2,1)S(1)}, bf16[128,4224]{1,0:T(8,128)(2,1)}, u32[]{:S(2)}, u32[]{:S(2)}) collective-permute-start(bf16[128,4224]{1,0:T(8,128)(2,1)S(1)} %collective-permute-done.4.refs_2_), channel_id=1, source_target_pairs={{0,1},{1,0},{2,3},{3,2},{4,5},{5,4},{6,7},{7,6},{8,9},{9,8},{10,11... | collective-permute-start | bytes 3244040 | tf_op jit(solution)/shard_map/ppermute | solution.py:257
  72.2 2.8 %collective-permute-start.7 = (bf16[128,4224]{1,0:T(8,128)(2,1)S(1)}, bf16[128,4224]{1,0:T(8,128)(2,1)}, u32[]{:S(2)}, u32[]{:S(2)}) collective-permute-start(bf16[128,4224]{1,0:T(8,128)(2,1)S(1)} %collective-permute-done.6.refs_4_), channel_id=1, source_target_pairs={{0,1},{1,0},{2,3},{3,2},{4,5},{5,4},{6,7},{7,6},{8,9},{9,8},{10,11... | collective-permute-start | bytes 3244040 | tf_op jit(solution)/shard_map/ppermute | solution.py:257
  73.9 3.0 %collective-permute-start.9 = (bf16[128,4224]{1,0:T(8,128)(2,1)}, bf16[128,4224]{1,0:T(8,128)(2,1)}, u32[]{:S(2)}, u32[]{:S(2)}) collective-permute-start(bf16[128,4224]{1,0:T(8,128)(2,1)} %collective-permute-done.8.refs_6_), channel_id=1, source_target_pairs={{0,1},{1,0},{2,3},{3,2},{4,5},{5,4},{6,7},{7,6},{8,9},{9,8},{10,11... | collective-permute-start | bytes 3244040 | tf_op jit(solution)/shard_map/ppermute | solution.py:257
  101.1 2.3 %copy-start = (bf16[3,1024,768]{2,1,0:T(8,128)(2,1)S(1)}, bf16[3,1024,768]{2,1,0:T(8,128)(2,1)}, u32[]{:S(2)}) copy-start(bf16[3,1024,768]{2,1,0:T(8,128)(2,1)} %get-tuple-element.24.h_ref) | copy-start | bytes 14155780
  106.7 2.1 %copy-start.2 = (bf16[1024,1024]{1,0:T(8,128)(2,1)S(1)}, bf16[1024,1024]{1,0:T(8,128)(2,1)}, u32[]{:S(2)}) copy-start(bf16[1024,1024]{1,0:T(8,128)(2,1)} %get-tuple-element.21.x_ref) | copy-start | bytes 6291460
  106.7 2.2 %copy-start.4 = (bf16[1024,1024]{1,0:T(8,128)(2,1)S(1)}, bf16[1024,1024]{1,0:T(8,128)(2,1)}, u32[]{:S(2)}) copy-start(bf16[1024,1024]{1,0:T(8,128)(2,1)} %get-tuple-element.22.dy_ref) | copy-start | bytes 6291460
  106.7 13.6 %slice-start = ((s8[4718592]{0:T(1024)(128)(4,1)}), s8[524288]{0:T(1024)(128)(4,1)S(1)}, s32[]{:S(2)}) async-start(s8[4718592]{0:T(1024)(128)(4,1)} %bitcast.45), calls=%async_computation | async-start | bytes 1048576
  108.9 11.4 %slice-start.1 = ((s8[4718592]{0:T(1024)(128)(4,1)}), s8[4194304]{0:T(1024)(128)(4,1)S(1)}, s32[]{:S(2)}) async-start(s8[4718592]{0:T(1024)(128)(4,1)} %bitcast.45), calls=%async_computation.1 | async-start | bytes 8388608
  118.6 11.2 %collective-permute-start.15 = (bf16[3,128,768]{2,1,0:T(8,128)(2,1)S(1)}, bf16[3,128,768]{2,1,0:T(8,128)(2,1)S(1)}, u32[]{:S(2)}, u32[]{:S(2)}) collective-permute-start(bf16[3,128,768]{2,1,0:T(8,128)(2,1)S(1)} %bitcast.48), channel_id=1, source_target_pairs={{0,32},{1,97},{32,64},{33,1},{64,96},{65,33},{96,0},{97,65},{2,34}... | collective-permute-start | bytes 1769480 | tf_op jit(solution)/shard_map/ppermute | solution.py:269
  126.3 15.6 %collective-permute-start.10 = (bf16[256,2176]{1,0:T(8,128)(2,1)S(1)}, bf16[256,2176]{1,0:T(8,128)(2,1)S(1)}, u32[]{:S(2)}, u32[]{:S(2)}) collective-permute-start(bf16[256,2176]{1,0:T(8,128)(2,1)S(1)} %get-tuple-element.27), channel_id=1, source_target_pairs={{0,8},{1,25},{8,0},{9,17},{16,24},{17,9},{24,16},{25,1},{2,10},{3,... | collective-permute-start | bytes 3342344 | tf_op jit(solution)/shard_map/ppermute | solution.py:274
  127.8 11.1 %collective-permute-start.18 = (bf16[3,128,768]{2,1,0:T(8,128)(2,1)S(1)}, bf16[3,128,768]{2,1,0:T(8,128)(2,1)S(1)}, u32[]{:S(2)}, u32[]{:S(2)}) collective-permute-start(bf16[3,128,768]{2,1,0:T(8,128)(2,1)S(1)} %bitcast.47), channel_id=1, source_target_pairs={{0,32},{1,97},{32,64},{33,1},{64,96},{65,33},{96,0},{97,65},{2,34}... | collective-permute-start | bytes 1769480 | tf_op jit(solution)/shard_map/ppermute | solution.py:268
  129.9 15.2 %collective-permute-start.16 = (bf16[3,128,768]{2,1,0:T(8,128)(2,1)S(1)}, bf16[3,128,768]{2,1,0:T(8,128)(2,1)S(1)}, u32[]{:S(2)}, u32[]{:S(2)}) collective-permute-start(bf16[3,128,768]{2,1,0:T(8,128)(2,1)S(1)} %fusion.5), channel_id=1, source_target_pairs={{0,32},{1,97},{32,64},{33,1},{64,96},{65,33},{96,0},{97,65},{2,34}... | collective-permute-start | bytes 1769480 | tf_op jit(solution)/shard_map/ppermute | solution.py:286
  139.0 12.5 %collective-permute-start.19 = (bf16[3,128,768]{2,1,0:T(8,128)(2,1)S(1)}, bf16[3,128,768]{2,1,0:T(8,128)(2,1)S(1)}, u32[]{:S(2)}, u32[]{:S(2)}) collective-permute-start(bf16[3,128,768]{2,1,0:T(8,128)(2,1)S(1)} %fusion.2), channel_id=1, source_target_pairs={{0,32},{1,97},{32,64},{33,1},{64,96},{65,33},{96,0},{97,65},{2,34}... | collective-permute-start | bytes 1769480 | tf_op jit(solution)/shard_map/ppermute | solution.py:285
  142.2 9.9 %collective-permute-start.11 = (bf16[128,2176]{1,0:T(8,128)(2,1)S(1)}, bf16[128,2176]{1,0:T(8,128)(2,1)S(1)}, u32[]{:S(2)}, u32[]{:S(2)}) collective-permute-start(bf16[128,2176]{1,0:T(8,128)(2,1)S(1)} %slice.78), channel_id=1, source_target_pairs={{0,1},{1,0},{2,3},{3,2},{4,5},{5,4},{6,7},{7,6},{8,9},{9,8},{10,11... | collective-permute-start | bytes 1671176 | tf_op jit(solution)/shard_map/ppermute | solution.py:276
  146.1 20.5 %collective-permute-start.17 = (bf16[3,128,768]{2,1,0:T(8,128)(2,1)}, bf16[3,128,768]{2,1,0:T(8,128)(2,1)}, u32[]{:S(2)}, u32[]{:S(2)}) collective-permute-start(bf16[3,128,768]{2,1,0:T(8,128)(2,1)} %fusion.6), channel_id=1, source_target_pairs={{0,32},{1,97},{32,64},{33,1},{64,96},{65,33},{96,0},{97,65},{2,34}... | collective-permute-start | bytes 1769480 | tf_op jit(solution)/shard_map/ppermute | solution.py:286
  151.7 12.5 %collective-permute-start.20 = (bf16[3,128,768]{2,1,0:T(8,128)(2,1)S(1)}, bf16[3,128,768]{2,1,0:T(8,128)(2,1)S(1)}, u32[]{:S(2)}, u32[]{:S(2)}) collective-permute-start(bf16[3,128,768]{2,1,0:T(8,128)(2,1)S(1)} %fusion.3), channel_id=1, source_target_pairs={{0,32},{1,97},{32,64},{33,1},{64,96},{65,33},{96,0},{97,65},{2,34}... | collective-permute-start | bytes 1769480 | tf_op jit(solution)/shard_map/ppermute | solution.py:285
  152.3 12.8 %collective-permute-start.12 = (bf16[32,2176]{1,0:T(8,128)(2,1)S(1)}, bf16[32,2176]{1,0:T(8,128)(2,1)S(1)}, u32[]{:S(2)}, u32[]{:S(2)}) collective-permute-start(bf16[32,2176]{1,0:T(8,128)(2,1)S(1)} %get-tuple-element.43), channel_id=1, source_target_pairs={{0,2},{2,0},{4,6},{6,4},{1,3},{3,1},{5,7},{7,5},{8,10},{10,8},{12,... | collective-permute-start | bytes 417800 | tf_op jit(solution)/shard_map/ppermute | solution.py:280
  153.7 11.3 %collective-permute-start.13 = (bf16[32,2176]{1,0:T(8,128)(2,1)S(1)}, bf16[32,2176]{1,0:T(8,128)(2,1)S(1)}, u32[]{:S(2)}, u32[]{:S(2)}) collective-permute-start(bf16[32,2176]{1,0:T(8,128)(2,1)S(1)} %get-tuple-element.45), channel_id=1, source_target_pairs={{0,6},{2,4},{4,2},{6,0},{1,7},{3,5},{5,3},{7,1},{8,14},{10,12},{12... | collective-permute-start | bytes 417800 | tf_op jit(solution)/shard_map/ppermute | solution.py:280
  156.4 8.6 %collective-permute-start.14 = (bf16[32,2176]{1,0:T(8,128)(2,1)S(1)}, bf16[32,2176]{1,0:T(8,128)(2,1)S(1)}, u32[]{:S(2)}, u32[]{:S(2)}) collective-permute-start(bf16[32,2176]{1,0:T(8,128)(2,1)S(1)} %get-tuple-element.44), channel_id=1, source_target_pairs={{0,4},{2,6},{4,0},{6,2},{1,5},{3,7},{5,1},{7,3},{8,12},{10,14},{12... | collective-permute-start | bytes 417800 | tf_op jit(solution)/shard_map/ppermute | solution.py:280
  164.3 10.1 %collective-permute-start.21 = (bf16[3,128,768]{2,1,0:T(8,128)(2,1)S(1)}, bf16[3,128,768]{2,1,0:T(8,128)(2,1)}, u32[]{:S(2)}, u32[]{:S(2)}) collective-permute-start(bf16[3,128,768]{2,1,0:T(8,128)(2,1)S(1)} %fusion.4), channel_id=1, source_target_pairs={{0,8},{1,25},{8,0},{9,17},{16,24},{17,9},{24,16},{25,1},{2,10},{3,... | collective-permute-start | bytes 1769480 | tf_op jit(solution)/shard_map/ppermute | solution.py:287
  (2 other events, 3.2 us)

commit v3 on v2

v3 whole, which is shorter than its diff:
```python
import functools

import jax
import jax.numpy as jnp
from jax import lax
from jax.experimental import pallas as pl
from jax.experimental.pallas import tpu as pltpu
from jax.sharding import Mesh, PartitionSpec as P

F32 = jnp.float32
BF16 = jnp.bfloat16
LANES = 128
SIDE = 4
VMEM = 12 << 20
LIGHT = pl.CostEstimate(flops=1 << 20, bytes_accessed=1 << 16, transcendentals=0)

X_ORDER = ((1, 3, 2), (3, 1, 2))
Z_ORDER = (1, 3, 2)
PAIR = (1, 3)
CHUNKS = ((0,), (1, 2, 3))


def plane(step, first):
    pairs = []
    for x in range(SIDE):
        for z in range(SIDE):
            for core in range(2):
                if (core == 0) == first:
                    to = (x ^ X_ORDER[core][step], z)
                else:
                    to = (x, z ^ Z_ORDER[step])
                pairs.append(((x * SIDE + z) * 2 + core, (to[0] * SIDE + to[1]) * 2 + core))
    return pairs


SWAP = [(0, 1), (1, 0)]
Z_MOVE = [[(j, j ^ k) for j in range(SIDE)] for k in Z_ORDER]
X_PAIR = [(x * 2 + c, (x ^ PAIR[c]) * 2 + c) for x in range(SIDE) for c in range(2)]
RING = [(y * 2 + c, ((y + 1 - 2 * c) % SIDE) * 2 + c) for y in range(SIDE) for c in range(2)]


def hold_kernel(place_ref, gate_up_ref, down_ref, held_ref, sem):
    expert = place_ref[1]
    sources = (gate_up_ref.at[0, expert], gate_up_ref.at[1, expert], down_ref.at[expert])
    copies = [pltpu.make_async_copy(source, held_ref.at[n], sem.at[n]) for n, source in enumerate(sources)]
    for copy in copies:
        copy.start()
    for copy in copies:
        copy.wait()


def forward_rows(row_refs, place_ref, sel_ref, weights_ref, h_ref, gp_ref):
    half = row_refs[0].shape[0]
    _, width, hidden = weights_ref.shape
    tile = 256
    gp_ref[...] = jnp.zeros_like(gp_ref)

    def step(j, carry):
        cols = pl.ds(pl.multiple_of(j * tile, tile), tile)
        for block in range(len(row_refs) // 2):
            pair = row_refs[2 * block : 2 * block + 2]
            rows = slice(2 * half * block, 2 * half * (block + 1))
            x = jnp.concatenate([r[:, :width] for r in pair], axis=0)
            dy = jnp.concatenate([r[:, width : 2 * width] for r in pair], axis=0)
            p = jnp.concatenate([r[:, 2 * width :] for r in pair], axis=0).astype(F32)
            p = jnp.sum(p * sel_ref[...], axis=-1, keepdims=True)
            gate = jnp.dot(x, weights_ref[0, :, cols], preferred_element_type=F32)
            up = jnp.dot(x, weights_ref[1, :, cols], preferred_element_type=F32)
            back = jnp.dot(dy, weights_ref[2, :, cols], preferred_element_type=F32)
            sig = 1.0 / (1.0 + jnp.exp(-gate))
            act = gate * sig
            hid = act * up
            hidden_grad = p * back
            h_ref[0, rows, cols] = (hidden_grad * up * (sig * (1.0 + gate * (1.0 - sig)))).astype(BF16)
            h_ref[1, rows, cols] = (hidden_grad * act).astype(BF16)
            h_ref[2, rows, cols] = (p * hid).astype(BF16)
            term = hid * back
            gp_ref[rows] += term[:, :LANES] + term[:, LANES:]
        return carry

    lax.fori_loop(0, hidden // tile, step, 0)


def weight_rows(width, start, cols_ref, row_refs, h_refs, other_ref, own_ref, rows_ref):
    half = row_refs[0].shape[0]

    def step(r, carry):
        for n in range(2):
            for m in range(2):
                at = pl.ds(pl.multiple_of(cols_ref[2 + 2 * (start + r) + m] * LANES + n * width, LANES), LANES)
                for piece, ref in enumerate(row_refs):
                    rows_ref[n, m * LANES : (m + 1) * LANES, half * piece : half * (piece + 1)] = ref[:, at].T
        for kind in range(3):
            total = None
            first = 0
            for h in h_refs:
                span = slice(first, first + h.shape[1])
                first += h.shape[1]
                term = jnp.dot(rows_ref[kind // 2, :, span], h[kind], preferred_element_type=F32)
                total = term if total is None else total + term
            other_ref[r, kind] = total[:LANES].astype(BF16)
            own_ref[r, kind] = total[LANES:].astype(BF16)
        return carry

    lax.fori_loop(0, other_ref.shape[0], step, 0)


def early_kernel(place_ref, sel_ref, weights_ref, *refs):
    *row_refs, h_ref, gp_ref = refs
    forward_rows(row_refs, place_ref, sel_ref, weights_ref, h_ref, gp_ref)


def late_kernel(old, count, place_ref, sel_ref, weights_ref, old_h_ref, *refs):
    row_refs, (h_ref, gp_ref, other_ref, own_ref, rows_ref) = refs[:count], refs[count:]
    forward_rows(row_refs[old:], place_ref, sel_ref, weights_ref, h_ref, gp_ref)
    cols = place_ref
    weight_rows(weights_ref.shape[1], 0, cols, row_refs, (old_h_ref, h_ref), other_ref, own_ref, rows_ref)


def rest_kernel(count, width, place_ref, *refs):
    row_refs, h_refs, (other_ref, own_ref, rows_ref) = refs[:count], refs[count:-3], refs[-3:]
    cols = place_ref
    weight_rows(width, 1, cols, row_refs, h_refs, other_ref, own_ref, rows_ref)


def on_chip(kernel, name, args, outs, scratch=(), far=0):
    vmem = pl.BlockSpec(memory_space=pltpu.VMEM)
    return pl.pallas_call(
        kernel,
        name=name,
        in_specs=[pl.BlockSpec(memory_space=pltpu.SMEM)]
        + [pl.BlockSpec(memory_space=pl.ANY)] * far
        + [vmem] * (len(args) - 1 - far),
        out_specs=[vmem] * len(outs),
        out_shape=[jax.ShapeDtypeStruct(*out) for out in outs],
        scratch_shapes=list(scratch),
        compiler_params=pltpu.CompilerParams(vmem_limit_bytes=VMEM),
        cost_estimate=LIGHT,
    )(*args)


def slot_rows(core, tokens):
    order = []
    for x in range(2):
        for which in range(2):
            place = 0 if x == 0 else 1 + which
            for z in range(SIDE):
                block, inner = (z, place) if which == core else (place, z)
                chunk = [block in blocks for blocks in CHUNKS].index(True)
                at = CHUNKS[chunk].index(block)
                order.append((chunk, ((at * 2 + which) * SIDE + inner) * tokens))
    return order


def slot_kernel(tokens, chunks, place_ref, sel_ref, weights_ref, *refs):
    hs, gps = refs[:chunks], refs[chunks : 2 * chunks]
    own_ref, pair_ref, rows_ref = refs[2 * chunks :]
    _, width, hidden = weights_ref.shape
    half = own_ref.shape[0]
    for core in range(2):

        @pl.when(place_ref[0] == core)
        def _():
            for n, (chunk, at) in enumerate(slot_rows(core, tokens)):
                to = slice(n * tokens, (n + 1) * tokens)
                rows_ref[:, to] = hs[chunk][:2, at : at + tokens]
                out, first = (own_ref, 0) if n * tokens < half else (pair_ref, half)
                gp = jnp.sum(gps[chunk][at : at + tokens], axis=-1, keepdims=True) * sel_ref[...]
                out[n * tokens - first : (n + 1) * tokens - first, width:] = gp.astype(BF16)

    contract = (((1,), (1,)), ((), ()))
    tile = 256

    def step(j, carry):
        cols = pl.ds(pl.multiple_of(j * tile, tile), tile)
        total = lax.dot_general(
            rows_ref[0], weights_ref[0, cols], contract, preferred_element_type=F32
        ) + lax.dot_general(rows_ref[1], weights_ref[1, cols], contract, preferred_element_type=F32)
        own_ref[:, cols] = total[:half].astype(BF16)
        pair_ref[:, cols] = total[half:].astype(BF16)
        return carry

    lax.fori_loop(0, width // tile, step, 0)


def add(*terms):
    total = terms[0].astype(F32)
    for term in terms[1:]:
        total = total + term.astype(F32)
    return total.astype(BF16)


def shards(layer_input, out_grad, routes, probs, gate_up, down_t):
    tokens, width = layer_input.shape
    x, y = lax.axis_index("x"), lax.axis_index("y")
    z, core = lax.axis_index("z"), lax.axis_index("core")
    expert = x % 2
    lane = lax.broadcasted_iota(jnp.int32, (1, LANES), 1)
    sel = (lane == (z * 2 + core) * 2 + expert).astype(F32)

    hot = routes[:, :, None] == lax.broadcasted_iota(jnp.int32, (1, 1, LANES), 2)
    dense = jnp.sum(jnp.where(hot, probs.astype(F32)[:, :, None], 0.0), axis=1).astype(BF16)
    row = jnp.concatenate([layer_input, out_grad, dense], axis=1)

    axes = ("x", "z", "core")
    down = jnp.transpose(down_t, (1, 0, 2))
    line = [row] + [lax.ppermute(row, axes, plane(n, True)) for n in range(3)]
    line = jnp.concatenate(line, axis=0)
    line, down = lax.optimization_barrier((line, down))
    mine = [line] + [lax.ppermute(line, axes, plane(n, False)) for n in range(3)]

    gate_up = jnp.transpose(gate_up, (1, 2, 0, 3))

    cols = []
    pair = x ^ jnp.where(core == 0, PAIR[0], PAIR[1])
    for n in (3, 2, 1, 0):
        base = SIDE * ((y + jnp.where(core == 0, n, SIDE - n)) % SIDE)
        cols += [base + pair, base + x]
    place = jnp.stack([core, expert] + cols).astype(jnp.int32)
    gate_up = pltpu.with_memory_space_constraint(gate_up, pltpu.HBM)
    down = pltpu.with_memory_space_constraint(down, pltpu.HBM)
    hidden = down.shape[2]
    (weights,) = on_chip(
        hold_kernel,
        "hold",
        (place, gate_up, down),
        [((3, width, hidden), BF16)],
        [pltpu.SemaphoreType.DMA((3,))],
        2,
    )
    swap = lambda piece: [piece, lax.ppermute(piece, "core", SWAP)]
    pieces = swap(line)
    early = 2 * line.shape[0]
    h0, gp0 = on_chip(
        early_kernel,
        "forward",
        (place, sel, weights, *pieces),
        [((3, early, hidden), BF16), ((early, LANES), F32)],
    )
    *mine[1:3], h0 = lax.optimization_barrier((*mine[1:3], h0))
    for piece in mine[1:]:
        pieces += swap(piece)
    late = 3 * early
    moving = lambda steps: ((steps, 3, LANES, hidden), BF16)
    turned = pltpu.VMEM((2, 2 * LANES, early + late), BF16)
    h1, gp1, other, own = on_chip(
        functools.partial(late_kernel, 2, len(pieces)),
        "forward_and_first",
        (place, sel, weights, h0, *pieces),
        [((3, late, hidden), BF16), ((late, LANES), F32), moving(1), moving(1)],
        [turned],
    )

    ring = lambda rows: lax.ppermute(rows, ("y", "core"), RING)
    other, own = ring(other[0]), ring(own[0])
    rest = on_chip(
        functools.partial(rest_kernel, len(pieces), width),
        "weight_terms",
        (place, *pieces, h0, h1),
        [moving(3), moving(3)],
        [turned],
    )
    other = add(rest[0][0], other)
    other, h1 = lax.optimization_barrier((other, h1))
    other, own = ring(other), ring(add(rest[1][0], own))
    half = 2 * SIDE * tokens
    rows = ((half, width + LANES), BF16)
    part, away = on_chip(
        functools.partial(slot_kernel, tokens, 2),
        "slot_terms",
        (place, sel, weights, h0, h1, gp0, gp1),
        [rows, rows],
        [pltpu.VMEM((2, 2 * half, hidden), BF16)],
    )

    part = add(part, lax.ppermute(away, ("x", "core"), X_PAIR))
    half = part.shape[0] // 2
    part = add(part[:half], lax.ppermute(part[half:], "core", SWAP))
    part = part.reshape((SIDE, tokens, part.shape[1]))
    total = part[0].astype(F32)
    for n in range(3):
        total = total + lax.ppermute(part[n + 1], "z", Z_MOVE[n]).astype(F32)
    grad_input = total[:, :width].astype(BF16)
    grad_prob = jnp.sum(jnp.where(hot, total[:, None, width:], 0.0), axis=2)

    other, own = ring(add(rest[0][1], other)), ring(add(rest[1][1], own))
    other = lax.ppermute(add(rest[0][2], other), ("x", "core"), X_PAIR)
    own = add(rest[1][2], own)
    even, odd = jnp.where(expert == 0, own, other), jnp.where(expert == 0, other, own)
    grad_weights = jnp.transpose(jnp.stack([even, odd], axis=0), (2, 1, 0, 3))
    return (grad_input, grad_prob, grad_weights)


def solution(mesh):
    grid = Mesh(mesh.devices.reshape(4, 4, 4, 2), ("y", "x", "z", "core"))
    every = P(("y", "x", "z", "core"), None)
    return jax.shard_map(
        shards,
        mesh=grid,
        in_specs=(every, every, every, every, P(None, None, ("z", "core"), None), P(None, ("z", "core"), None)),
        out_specs=(every, every, P(("y", "x"), None, ("z", "core"), None)),
        check_vma=False,
    )
```

time: 180 us -> 119 us (0.66)
  local copies, waits for them, and re-layouts: 48.6 us -> 25 us
  other arithmetic: 21.8 us -> 7.99 us
  Pallas kernels: 42.1 us -> 31.3 us
  waiting for transfers between devices: 40 us -> 31.1 us
  starting transfers between devices: 24.9 us -> 22.7 us
    slice x2 -> x0, local copies, waits for them, and re-layouts: 35.4 us -> none  [the longest x1 25.3 us: shards(): gate_up = jnp.where(expert == 0, gate_up[:, :, 0], gate_up[:, :, 1])]
    unnamed x27 -> x19, local copies, waits for them, and re-layouts: 11.6 us -> 22.6 us
    pallas_call x4 -> x5, Pallas kernels: 42.1 us -> 31.3 us  [on_chip(): pl.pallas_call(kernel, name=name, in_specs=[pl.BlockSpec(memory_space=plt...]
    transpose x1 -> x0, other arithmetic: 9.57 us -> none  [shards(): gate_up = jnp.transpose(gate_up, (1, 0, 2))]
    select_n x1 -> x0, other arithmetic: 7.07 us -> none  [shards(): down = jnp.where(expert == 0, down_t[:, 0], down_t[:, 1])]
    ppermute x1, waiting for transfers between devices: 7.73 us -> 3.32 us  [shards(): other = lax.ppermute(add(rest[0][2], other), ('x', 'core'), X_PAIR)]
    convert_element_type x7, other arithmetic: 1.92 us -> 6.12 us  [add(): return total.astype(BF16)]
    ppermute x10, waiting for transfers between devices: 24.4 us -> 20.8 us  [the longest x6 16.4 us: shards(): ring = lambda rows: lax.ppermute(rows, ('y', 'core'), RING)]
  transfers between devices with their start and end apart: 22 -> 22, of which waited for: 11 -> 13; matrix products, arithmetic and copies ran while one was open for 31% -> 23% of each run, Pallas kernels for 3% -> 17%
where the time goes in v3:
time: 119 us
  Pallas kernels  31.3 us (26%)
  waiting for transfers between devices  31.1 us (26%)
  local copies, waits for them, and re-layouts  25 us (21%)
  starting transfers between devices  22.7 us (19%)
  other arithmetic  7.99 us (7%)
    pallas_call x5, Pallas kernels, on_chip(): pl.pallas_call(kernel, name=name, in_specs=[pl.BlockSpec(memory_space=plt...  31.3 us
    unnamed x19, local copies, waits for them, and re-layouts  22.6 us
    ppermute x6, waiting for transfers between devices, shards(): ring = lambda rows: lax.ppermute(rows, ('y', 'core'), RING)  16.4 us
    convert_element_type x7, other arithmetic, add(): return total.astype(BF16)  6.12 us
    ppermute x3, starting transfers between devices, shards(): lax.ppermute(line, axes, plane(n, False))  5.48 us
    ppermute x6, starting transfers between devices, shards(): ring = lambda rows: lax.ppermute(rows, ('y', 'core'), RING)  5.24 us
    ppermute x3, starting transfers between devices, shards(): total = total + lax.ppermute(part[n + 1], 'z', Z_MOVE[n]).astype(F32)  4.73 us
    ppermute x3, waiting for transfers between devices, shards(): lax.ppermute(line, axes, plane(n, False))  4.4 us
  transfers between devices with their start and end apart: 22, of which 13 were waited for; matrix products, arithmetic and copies ran while one was open for 23% of the time, Pallas kernels for 17%

profile of v3, /device:TPU:0, one launch (start us, length us, event | category | flops | bytes accessed | tf_op | source)
XLA Modules:
  0.0 119.0 jit_solution(775363673942550573)
XLA Ops:
  2.3 1.0 pad_maximum_fusion.1
  3.3 3.2 %collective-permute-start.2 = (bf16[32,4224]{1,0:T(8,128)(2,1)S(1)}, bf16[32,4224]{1,0:T(8,128)(2,1)S(1)}, u32[]{:S(2)}, u32[]{:S(2)}) collective-permute-start(bf16[32,4224]{1,0:T(8,128)(2,1)S(1)} %pad_maximum_fusion.1), channel_id=1, source_target_pairs={{0,16},{1,5},{2,18},{3,7},{4,20},{5,1},{6,22},{7,3},{8,24},{9,13},... | collective-permute-start | bytes 811016 | tf_op jit(solution)/shard_map/ppermute | solution.py:207
  6.5 1.1 collective-permute-start.1
  7.6 6.2 %copy.23 = bf16[2048,2,768]{2,0,1:T(8,128)(2,1)} copy(bf16[2048,2,768]{2,1,0:T(2,128)(2,1)} %param.11) | data formatting | bytes 12582912 | tf_op args[5]
  14.7 1.9 %collective-permute-start.3 = (bf16[128,4224]{1,0:T(8,128)(2,1)S(1)}, bf16[128,4224]{1,0:T(8,128)(2,1)S(1)}, u32[]{:S(2)}, u32[]{:S(2)}) collective-permute-start(bf16[128,4224]{1,0:T(8,128)(2,1)S(1)} %pad_maximum_fusion.refs_0_), channel_id=1, source_target_pairs={{0,2},{1,25},{2,0},{3,27},{4,6},{5,29},{6,4},{7,31},{8,10},{9,17},... | collective-permute-start | bytes 3244040 | tf_op jit(solution)/shard_map/ppermute | solution.py:210
  16.6 2.5 %collective-permute-start.4 = (bf16[128,4224]{1,0:T(8,128)(2,1)S(1)}, bf16[128,4224]{1,0:T(8,128)(2,1)}, u32[]{:S(2)}, u32[]{:S(2)}) collective-permute-start(bf16[128,4224]{1,0:T(8,128)(2,1)S(1)} %pad_maximum_fusion.refs_0_), channel_id=1, source_target_pairs={{0,6},{1,9},{2,4},{3,11},{4,2},{5,13},{6,0},{7,15},{8,14},{9,1},{1... | collective-permute-start | bytes 3244040 | tf_op jit(solution)/shard_map/ppermute | solution.py:210
  19.2 1.1 collective-permute-start.8
  20.2 11.8 %copy.22 = bf16[2048,2,2,768]{3,0,2,1:T(8,128)(2,1)} copy(bf16[2048,2,2,768]{3,2,1,0:T(2,128)(2,1)} %param.10) | data formatting | bytes 25165824 | tf_op args[4]
  32.1 4.3 %hold.1.weights_ref = bf16[3,2048,768]{2,1,0:T(8,128)(2,1)S(1)} custom-call(s32[10]{0:T(128)S(1)} %stack.52.place_ref, bf16[2,2,2048,768]{3,2,1,0:T(8,128)(2,1)} %bitcast.48, bf16[2,2048,768]{2,1,0:T(8,128)(2,1)} %bitcast.49), custom_call_target="tpu_custom_call" | custom-call | flops 1048576 | bytes 65536 | tf_op jit(solution)/shard_map/hold/pallas_call | solution.py:128
  36.4 3.7 %forward.1 = (bf16[3,256,768]{2,1,0:T(8,128)(2,1)S(1)}, f32[256,128]{1,0:T(8,128)S(1)}) custom-call(s32[10]{0:T(128)S(1)} %stack.52.place_ref, f32[1,128]{1,0:T(1,128)S(1)} %compare_convert_fusion.sel_ref, bf16[3,2048,768]{2,1,0:T(8,128)(2,1)S(1)} %hold.1.weights_ref, bf16[128,4224]{1,0:T(8,128)(2,1)S(1)} %pad_maximum_fusion.refs_0_, ...), custom_call_target="tpu_custom_call" | custom-call | flops 1048576 | bytes 65536 | tf_op jit(solution)/shard_map/forward/pallas_call | solution.py:128
  40.1 3.3 %collective-permute-done.4.refs_4_ = bf16[128,4224]{1,0:T(8,128)(2,1)} collective-permute-done((bf16[128,4224]{1,0:T(8,128)(2,1)S(1)}, bf16[128,4224]{1,0:T(8,128)(2,1)}, u32[]{:S(2)}, u32[]{:S(2)}) %collective-permute-start.4) | collective-permute-done | bytes 1081376 | tf_op jit(solution)/shard_map/ppermute | solution.py:210
  43.9 1.1 collective-permute-done.8.refs_6_
  45.0 2.6 %collective-permute-done.6.refs_3_ = bf16[128,4224]{1,0:T(8,128)(2,1)S(1)} collective-permute-done((bf16[128,4224]{1,0:T(8,128)(2,1)S(1)}, bf16[128,4224]{1,0:T(8,128)(2,1)S(1)}, u32[]{:S(2)}, u32[]{:S(2)}) %collective-permute-start.6) | collective-permute-done | bytes 1081376 | tf_op jit(solution)/shard_map/ppermute | solution.py:231
  47.9 1.5 %collective-permute-done.9.refs_7_ = bf16[128,4224]{1,0:T(8,128)(2,1)S(1)} collective-permute-done((bf16[128,4224]{1,0:T(8,128)(2,1)}, bf16[128,4224]{1,0:T(8,128)(2,1)S(1)}, u32[]{:S(2)}, u32[]{:S(2)}) %collective-permute-start.9) | collective-permute-done | bytes 1081376 | tf_op jit(solution)/shard_map/ppermute | solution.py:231
  49.4 11.5 %forward_and_first.1 = (bf16[3,768,768]{2,1,0:T(8,128)(2,1)S(1)}, f32[768,128]{1,0:T(8,128)S(1)}, bf16[1,3,128,768]{3,2,1,0:T(8,128)(2,1)S(1)}, bf16[1,3,128,768]{3,2,1,0:T(8,128)(2,1)S(1)}) custom-call(s32[10]{0:T(128)S(1)} %stack.52.place_ref, f32[1,128]{1,0:T(1,128)S(1)} %compare_convert_fusion.sel_ref, bf16[3,2048,768]{2,1,0:T(8,128)(2,1)S(1)} %hold.1.weights_ref, ...), custom_call_target="tpu_custom_call" | custom-call | flops 1048576 | bytes 65536 | tf_op jit(solution)/shard_map/forward_and_first/pallas_call | solution.py:128
  61.0 1.6 %collective-permute-start.10 = (bf16[3,128,768]{2,1,0:T(8,128)(2,1)S(1)}, bf16[3,128,768]{2,1,0:T(8,128)(2,1)S(1)}, u32[]{:S(2)}, u32[]{:S(2)}) collective-permute-start(bf16[3,128,768]{2,1,0:T(8,128)(2,1)S(1)} %bitcast.47), channel_id=1, source_target_pairs={{0,32},{1,97},{32,64},{33,1},{64,96},{65,33},{96,0},{97,65},{2,34}... | collective-permute-start | bytes 1769480 | tf_op jit(solution)/shard_map/ppermute | solution.py:254
  62.6 1.6 %collective-permute-start.16 = (bf16[3,128,768]{2,1,0:T(8,128)(2,1)S(1)}, bf16[3,128,768]{2,1,0:T(8,128)(2,1)S(1)}, u32[]{:S(2)}, u32[]{:S(2)}) collective-permute-start(bf16[3,128,768]{2,1,0:T(8,128)(2,1)S(1)} %bitcast.46), channel_id=1, source_target_pairs={{0,32},{1,97},{32,64},{33,1},{64,96},{65,33},{96,0},{97,65},{2,34}... | collective-permute-start | bytes 1769480 | tf_op jit(solution)/shard_map/ppermute | solution.py:254
  64.2 6.0 %weight_terms.1 = (bf16[3,3,128,768]{3,2,1,0:T(8,128)(2,1)S(1)}, bf16[3,3,128,768]{3,2,1,0:T(8,128)(2,1)S(1)}) custom-call(s32[10]{0:T(128)S(1)} %stack.52.place_ref, bf16[128,4224]{1,0:T(8,128)(2,1)S(1)} %pad_maximum_fusion.refs_0_, bf16[128,4224]{1,0:T(8,128)(2,1)S(1)} %collective-permute-done.5.refs_1_, ...), custom_call_target="tpu_custom_call" | custom-call | flops 1048576 | bytes 65536 | tf_op jit(solution)/shard_map/weight_terms/pallas_call | solution.py:128
  70.2 1.9 %collective-permute-done.10 = bf16[3,128,768]{2,1,0:T(8,128)(2,1)S(1)} collective-permute-done((bf16[3,128,768]{2,1,0:T(8,128)(2,1)S(1)}, bf16[3,128,768]{2,1,0:T(8,128)(2,1)S(1)}, u32[]{:S(2)}, u32[]{:S(2)}) %collective-permute-start.10) | collective-permute-done | bytes 589856 | tf_op jit(solution)/shard_map/ppermute | solution.py:254
  72.3 5.8 %slot_terms.1 = (bf16[256,2176]{1,0:T(8,128)(2,1)S(1)}, bf16[256,2176]{1,0:T(8,128)(2,1)S(1)}) custom-call(s32[10]{0:T(128)S(1)} %stack.52.place_ref, f32[1,128]{1,0:T(1,128)S(1)} %compare_convert_fusion.sel_ref, bf16[3,2048,768]{2,1,0:T(8,128)(2,1)S(1)} %hold.1.weights_ref, bf16[3,256,768]{2,1,0:T(8,128)(2,1)S(1)} %get-tuple-element.23.old_h_ref.refs_8_.refs_0_, ...), custom_call_target="tpu_custom_call" | custom-call | flops 1048576 | bytes 65536 | tf_op jit(solution)/shard_map/slot_terms/pallas_call | solution.py:128
  78.1 1.5 %collective-permute-start.11 = (bf16[256,2176]{1,0:T(8,128)(2,1)S(1)}, bf16[256,2176]{1,0:T(8,128)(2,1)S(1)}, u32[]{:S(2)}, u32[]{:S(2)}) collective-permute-start(bf16[256,2176]{1,0:T(8,128)(2,1)S(1)} %get-tuple-element.33), channel_id=1, source_target_pairs={{0,8},{1,25},{8,0},{9,17},{16,24},{17,9},{24,16},{25,1},{2,10},{3,... | collective-permute-start | bytes 3342344 | tf_op jit(solution)/shard_map/ppermute | solution.py:276
  80.9 1.6 %collective-permute-start.17 = (bf16[3,128,768]{2,1,0:T(8,128)(2,1)}, bf16[3,128,768]{2,1,0:T(8,128)(2,1)}, u32[]{:S(2)}, u32[]{:S(2)}) collective-permute-start(bf16[3,128,768]{2,1,0:T(8,128)(2,1)} %fusion.2), channel_id=1, source_target_pairs={{0,32},{1,97},{32,64},{33,1},{64,96},{65,33},{96,0},{97,65},{2,34}... | collective-permute-start | bytes 1769480 | tf_op jit(solution)/shard_map/ppermute | solution.py:254
  82.5 8.2 %collective-permute-done.19 = bf16[3,128,768]{2,1,0:T(8,128)(2,1)S(1)} collective-permute-done((bf16[3,128,768]{2,1,0:T(8,128)(2,1)S(1)}, bf16[3,128,768]{2,1,0:T(8,128)(2,1)S(1)}, u32[]{:S(2)}, u32[]{:S(2)}) %collective-permute-start.19) | collective-permute-done | bytes 589856 | tf_op jit(solution)/shard_map/ppermute | solution.py:254
  91.6 2.0 %collective-permute-done.11 = bf16[256,2176]{1,0:T(8,128)(2,1)S(1)} collective-permute-done((bf16[256,2176]{1,0:T(8,128)(2,1)S(1)}, bf16[256,2176]{1,0:T(8,128)(2,1)S(1)}, u32[]{:S(2)}, u32[]{:S(2)}) %collective-permute-start.11) | collective-permute-done | bytes 1114144 | tf_op jit(solution)/shard_map/ppermute | solution.py:276
  95.8 1.3 %collective-permute-done.17 = bf16[3,128,768]{2,1,0:T(8,128)(2,1)} collective-permute-done((bf16[3,128,768]{2,1,0:T(8,128)(2,1)}, bf16[3,128,768]{2,1,0:T(8,128)(2,1)}, u32[]{:S(2)}, u32[]{:S(2)}) %collective-permute-start.17) | collective-permute-done | bytes 589856 | tf_op jit(solution)/shard_map/ppermute | solution.py:254
  97.1 1.2 %fusion.3 = bf16[3,128,768]{2,1,0:T(8,128)(2,1)S(1)} fusion(bf16[3,128,768]{2,1,0:T(8,128)(2,1)} %collective-permute-done.17, bf16[3,3,128,768]{3,2,1,0:T(8,128)(2,1)S(1)} %copy-done.2), kind=kLoop, calls=%fused_computation.11 | loop fusion | flops 1179648 | bytes 1769472 | tf_op jit(solution)/shard_map/convert_element_type | solution.py:190
  98.4 5.0 %collective-permute-done.20 = bf16[3,128,768]{2,1,0:T(8,128)(2,1)} collective-permute-done((bf16[3,128,768]{2,1,0:T(8,128)(2,1)}, bf16[3,128,768]{2,1,0:T(8,128)(2,1)}, u32[]{:S(2)}, u32[]{:S(2)}) %collective-permute-start.20) | collective-permute-done | bytes 589856 | tf_op jit(solution)/shard_map/ppermute | solution.py:254
  103.4 1.4 %fusion.1 = bf16[3,128,768]{2,1,0:T(8,128)(2,1)S(1)} fusion(bf16[3,128,768]{2,1,0:T(8,128)(2,1)} %collective-permute-done.20, bf16[3,3,128,768]{3,2,1,0:T(8,128)(2,1)} %copy-done), kind=kLoop, calls=%fused_computation.7 | loop fusion | flops 1179648 | bytes 1769472 | tf_op jit(solution)/shard_map/convert_element_type | solution.py:190
  105.5 1.2 add_convert_fusion.1
  106.7 3.7 %collective-permute-start.15 = (bf16[32,2176]{1,0:T(8,128)(2,1)S(1)}, bf16[32,2176]{1,0:T(8,128)(2,1)S(1)}, u32[]{:S(2)}, u32[]{:S(2)}) collective-permute-start(bf16[32,2176]{1,0:T(8,128)(2,1)S(1)} %get-tuple-element.46), channel_id=1, source_target_pairs={{0,4},{2,6},{4,0},{6,2},{1,5},{3,7},{5,1},{7,3},{8,12},{10,14},{12... | collective-permute-start | bytes 417800 | tf_op jit(solution)/shard_map/ppermute | solution.py:282
  111.4 3.3 %collective-permute-done.21 = bf16[3,128,768]{2,1,0:T(8,128)(2,1)S(1)} collective-permute-done((bf16[3,128,768]{2,1,0:T(8,128)(2,1)S(1)}, bf16[3,128,768]{2,1,0:T(8,128)(2,1)S(1)}, u32[]{:S(2)}, u32[]{:S(2)}) %collective-permute-start.21) | collective-permute-done | bytes 589856 | tf_op jit(solution)/shard_map/ppermute | solution.py:287
  115.2 2.2 %copy.19 = bf16[128,3,2,768]{3,2,1,0:T(2,128)(2,1)} copy(bf16[128,3,2,768]{3,0,1,2:T(8,128)(2,1)S(1)} %maximum_bitcast_fusion) | data formatting | bytes 2359296
  (57 shorter events, 11.8 us)
Async XLA Ops:
  3.3 11.2 %copy-start.5 = (bf16[32,2048]{1,0:T(8,128)(2,1)S(1)}, bf16[32,2048]{1,0:T(8,128)(2,1)}, u32[]{:S(2)}) copy-start(bf16[32,2048]{1,0:T(8,128)(2,1)} %param.7) | copy-start | bytes 393220
  3.3 11.2 %copy-start.6 = (bf16[32,2048]{1,0:T(8,128)(2,1)S(1)}, bf16[32,2048]{1,0:T(8,128)(2,1)}, u32[]{:S(2)}) copy-start(bf16[32,2048]{1,0:T(8,128)(2,1)} %param.6) | copy-start | bytes 393220
  3.3 10.5 %collective-permute-start.2 = (bf16[32,4224]{1,0:T(8,128)(2,1)S(1)}, bf16[32,4224]{1,0:T(8,128)(2,1)S(1)}, u32[]{:S(2)}, u32[]{:S(2)}) collective-permute-start(bf16[32,4224]{1,0:T(8,128)(2,1)S(1)} %pad_maximum_fusion.1), channel_id=1, source_target_pairs={{0,16},{1,5},{2,18},{3,7},{4,20},{5,1},{6,22},{7,3},{8,24},{9,13},... | collective-permute-start | bytes 811016 | tf_op jit(solution)/shard_map/ppermute | solution.py:207
  6.5 7.8 %collective-permute-start.1 = (bf16[32,4224]{1,0:T(8,128)(2,1)S(1)}, bf16[32,4224]{1,0:T(8,128)(2,1)S(1)}, u32[]{:S(2)}, u32[]{:S(2)}) collective-permute-start(bf16[32,4224]{1,0:T(8,128)(2,1)S(1)} %pad_maximum_fusion.1), channel_id=1, source_target_pairs={{0,24},{1,7},{2,26},{3,5},{4,28},{5,3},{6,30},{7,1},{8,16},{9,15},... | collective-permute-start | bytes 811016 | tf_op jit(solution)/shard_map/ppermute | solution.py:207
  7.6 6.8 %collective-permute-start = (bf16[32,4224]{1,0:T(8,128)(2,1)S(1)}, bf16[32,4224]{1,0:T(8,128)(2,1)S(1)}, u32[]{:S(2)}, u32[]{:S(2)}) collective-permute-start(bf16[32,4224]{1,0:T(8,128)(2,1)S(1)} %pad_maximum_fusion.1), channel_id=1, source_target_pairs={{0,8},{1,3},{2,10},{3,1},{4,12},{5,7},{6,14},{7,5},{8,0},{9,11},{1... | collective-permute-start | bytes 811016 | tf_op jit(solution)/shard_map/ppermute | solution.py:207
  14.6 21.9 %collective-permute-start.5 = (bf16[128,4224]{1,0:T(8,128)(2,1)S(1)}, bf16[128,4224]{1,0:T(8,128)(2,1)S(1)}, u32[]{:S(2)}, u32[]{:S(2)}) collective-permute-start(bf16[128,4224]{1,0:T(8,128)(2,1)S(1)} %pad_maximum_fusion.refs_0_), channel_id=1, source_target_pairs={{0,1},{1,0},{2,3},{3,2},{4,5},{5,4},{6,7},{7,6},{8,9},{9,8},{10,11... | collective-permute-start | bytes 3244040 | tf_op jit(solution)/shard_map/ppermute | solution.py:231
  14.7 25.4 %collective-permute-start.3 = (bf16[128,4224]{1,0:T(8,128)(2,1)S(1)}, bf16[128,4224]{1,0:T(8,128)(2,1)S(1)}, u32[]{:S(2)}, u32[]{:S(2)}) collective-permute-start(bf16[128,4224]{1,0:T(8,128)(2,1)S(1)} %pad_maximum_fusion.refs_0_), channel_id=1, source_target_pairs={{0,2},{1,25},{2,0},{3,27},{4,6},{5,29},{6,4},{7,31},{8,10},{9,17},... | collective-permute-start | bytes 3244040 | tf_op jit(solution)/shard_map/ppermute | solution.py:210
  16.6 26.8 %collective-permute-start.4 = (bf16[128,4224]{1,0:T(8,128)(2,1)S(1)}, bf16[128,4224]{1,0:T(8,128)(2,1)}, u32[]{:S(2)}, u32[]{:S(2)}) collective-permute-start(bf16[128,4224]{1,0:T(8,128)(2,1)S(1)} %pad_maximum_fusion.refs_0_), channel_id=1, source_target_pairs={{0,6},{1,9},{2,4},{3,11},{4,2},{5,13},{6,0},{7,15},{8,14},{9,1},{1... | collective-permute-start | bytes 3244040 | tf_op jit(solution)/shard_map/ppermute | solution.py:210
  19.2 25.9 %collective-permute-start.8 = (bf16[128,4224]{1,0:T(8,128)(2,1)S(1)}, bf16[128,4224]{1,0:T(8,128)(2,1)}, u32[]{:S(2)}, u32[]{:S(2)}) collective-permute-start(bf16[128,4224]{1,0:T(8,128)(2,1)S(1)} %pad_maximum_fusion.refs_0_), channel_id=1, source_target_pairs={{0,4},{1,17},{2,6},{3,19},{4,0},{5,21},{6,2},{7,23},{8,12},{9,25},... | collective-permute-start | bytes 3244040 | tf_op jit(solution)/shard_map/ppermute | solution.py:210
  43.4 4.2 %collective-permute-start.6 = (bf16[128,4224]{1,0:T(8,128)(2,1)S(1)}, bf16[128,4224]{1,0:T(8,128)(2,1)S(1)}, u32[]{:S(2)}, u32[]{:S(2)}) collective-permute-start(bf16[128,4224]{1,0:T(8,128)(2,1)S(1)} %collective-permute-done.3.refs_2_), channel_id=1, source_target_pairs={{0,1},{1,0},{2,3},{3,2},{4,5},{5,4},{6,7},{7,6},{8,9},{9,8},{10,11... | collective-permute-start | bytes 3244040 | tf_op jit(solution)/shard_map/ppermute | solution.py:231
  43.4 4.5 %collective-permute-start.7 = (bf16[128,4224]{1,0:T(8,128)(2,1)}, bf16[128,4224]{1,0:T(8,128)(2,1)S(1)}, u32[]{:S(2)}, u32[]{:S(2)}) collective-permute-start(bf16[128,4224]{1,0:T(8,128)(2,1)} %collective-permute-done.4.refs_4_), channel_id=1, source_target_pairs={{0,1},{1,0},{2,3},{3,2},{4,5},{5,4},{6,7},{7,6},{8,9},{9,8},{10,11... | collective-permute-start | bytes 3244040 | tf_op jit(solution)/shard_map/ppermute | solution.py:231
  45.0 4.4 %collective-permute-start.9 = (bf16[128,4224]{1,0:T(8,128)(2,1)}, bf16[128,4224]{1,0:T(8,128)(2,1)S(1)}, u32[]{:S(2)}, u32[]{:S(2)}) collective-permute-start(bf16[128,4224]{1,0:T(8,128)(2,1)} %collective-permute-done.8.refs_6_), channel_id=1, source_target_pairs={{0,1},{1,0},{2,3},{3,2},{4,5},{5,4},{6,7},{7,6},{8,9},{9,8},{10,11... | collective-permute-start | bytes 3244040 | tf_op jit(solution)/shard_map/ppermute | solution.py:231
  61.0 11.2 %collective-permute-start.10 = (bf16[3,128,768]{2,1,0:T(8,128)(2,1)S(1)}, bf16[3,128,768]{2,1,0:T(8,128)(2,1)S(1)}, u32[]{:S(2)}, u32[]{:S(2)}) collective-permute-start(bf16[3,128,768]{2,1,0:T(8,128)(2,1)S(1)} %bitcast.47), channel_id=1, source_target_pairs={{0,32},{1,97},{32,64},{33,1},{64,96},{65,33},{96,0},{97,65},{2,34}... | collective-permute-start | bytes 1769480 | tf_op jit(solution)/shard_map/ppermute | solution.py:254
  62.6 17.3 %collective-permute-start.16 = (bf16[3,128,768]{2,1,0:T(8,128)(2,1)S(1)}, bf16[3,128,768]{2,1,0:T(8,128)(2,1)S(1)}, u32[]{:S(2)}, u32[]{:S(2)}) collective-permute-start(bf16[3,128,768]{2,1,0:T(8,128)(2,1)S(1)} %bitcast.46), channel_id=1, source_target_pairs={{0,32},{1,97},{32,64},{33,1},{64,96},{65,33},{96,0},{97,65},{2,34}... | collective-permute-start | bytes 1769480 | tf_op jit(solution)/shard_map/ppermute | solution.py:254
  70.2 9.7 %copy-start.1 = (bf16[3,3,128,768]{3,2,1,0:T(8,128)(2,1)}, bf16[3,3,128,768]{3,2,1,0:T(8,128)(2,1)S(1)}, u32[]{:S(2)}) copy-start(bf16[3,3,128,768]{3,2,1,0:T(8,128)(2,1)S(1)} %get-tuple-element.34) | copy-start | bytes 5308420
  70.2 20.4 %copy-start = (bf16[3,3,128,768]{3,2,1,0:T(8,128)(2,1)}, bf16[3,3,128,768]{3,2,1,0:T(8,128)(2,1)S(1)}, u32[]{:S(2)}) copy-start(bf16[3,3,128,768]{3,2,1,0:T(8,128)(2,1)S(1)} %get-tuple-element.27) | copy-start | bytes 5308420
  78.1 15.6 %collective-permute-start.11 = (bf16[256,2176]{1,0:T(8,128)(2,1)S(1)}, bf16[256,2176]{1,0:T(8,128)(2,1)S(1)}, u32[]{:S(2)}, u32[]{:S(2)}) collective-permute-start(bf16[256,2176]{1,0:T(8,128)(2,1)S(1)} %get-tuple-element.33), channel_id=1, source_target_pairs={{0,8},{1,25},{8,0},{9,17},{16,24},{17,9},{24,16},{25,1},{2,10},{3,... | collective-permute-start | bytes 3342344 | tf_op jit(solution)/shard_map/ppermute | solution.py:276
  79.6 11.1 %collective-permute-start.19 = (bf16[3,128,768]{2,1,0:T(8,128)(2,1)S(1)}, bf16[3,128,768]{2,1,0:T(8,128)(2,1)S(1)}, u32[]{:S(2)}, u32[]{:S(2)}) collective-permute-start(bf16[3,128,768]{2,1,0:T(8,128)(2,1)S(1)} %fusion.5), channel_id=1, source_target_pairs={{0,32},{1,97},{32,64},{33,1},{64,96},{65,33},{96,0},{97,65},{2,34}... | collective-permute-start | bytes 1769480 | tf_op jit(solution)/shard_map/ppermute | solution.py:254
  80.9 16.2 %collective-permute-start.17 = (bf16[3,128,768]{2,1,0:T(8,128)(2,1)}, bf16[3,128,768]{2,1,0:T(8,128)(2,1)}, u32[]{:S(2)}, u32[]{:S(2)}) collective-permute-start(bf16[3,128,768]{2,1,0:T(8,128)(2,1)} %fusion.2), channel_id=1, source_target_pairs={{0,32},{1,97},{32,64},{33,1},{64,96},{65,33},{96,0},{97,65},{2,34}... | collective-permute-start | bytes 1769480 | tf_op jit(solution)/shard_map/ppermute | solution.py:254
  91.6 11.8 %collective-permute-start.20 = (bf16[3,128,768]{2,1,0:T(8,128)(2,1)}, bf16[3,128,768]{2,1,0:T(8,128)(2,1)}, u32[]{:S(2)}, u32[]{:S(2)}) collective-permute-start(bf16[3,128,768]{2,1,0:T(8,128)(2,1)} %fusion), channel_id=1, source_target_pairs={{0,32},{1,97},{32,64},{33,1},{64,96},{65,33},{96,0},{97,65},{2,34}... | collective-permute-start | bytes 1769480 | tf_op jit(solution)/shard_map/ppermute | solution.py:254
  93.6 3.4 %copy-start.2 = (bf16[3,3,128,768]{3,2,1,0:T(8,128)(2,1)S(1)}, bf16[3,3,128,768]{3,2,1,0:T(8,128)(2,1)}, u32[]{:S(2)}) copy-start(bf16[3,3,128,768]{3,2,1,0:T(8,128)(2,1)} %copy-done.1) | copy-start | bytes 5308420
  93.9 1.0 copy-start.3
  95.8 9.7 %collective-permute-start.12 = (bf16[128,2176]{1,0:T(8,128)(2,1)}, bf16[128,2176]{1,0:T(8,128)(2,1)}, u32[]{:S(2)}, u32[]{:S(2)}) collective-permute-start(bf16[128,2176]{1,0:T(8,128)(2,1)} %slice.62), channel_id=1, source_target_pairs={{0,1},{1,0},{2,3},{3,2},{4,5},{5,4},{6,7},{7,6},{8,9},{9,8},{10,11... | collective-permute-start | bytes 1671176 | tf_op jit(solution)/shard_map/ppermute | solution.py:278
  98.3 7.2 %copy-start.4 = (bf16[256,2176]{1,0:T(8,128)(2,1)S(1)}, bf16[256,2176]{1,0:T(8,128)(2,1)}, u32[]{:S(2)}) copy-start(bf16[256,2176]{1,0:T(8,128)(2,1)} %copy-done.3) | copy-start | bytes 3342340
  98.3 13.1 %collective-permute-start.18 = (bf16[3,128,768]{2,1,0:T(8,128)(2,1)S(1)}, bf16[3,128,768]{2,1,0:T(8,128)(2,1)S(1)}, u32[]{:S(2)}, u32[]{:S(2)}) collective-permute-start(bf16[3,128,768]{2,1,0:T(8,128)(2,1)S(1)} %fusion.3), channel_id=1, source_target_pairs={{0,32},{1,97},{32,64},{33,1},{64,96},{65,33},{96,0},{97,65},{2,34}... | collective-permute-start | bytes 1769480 | tf_op jit(solution)/shard_map/ppermute | solution.py:254
  104.8 10.0 %collective-permute-start.21 = (bf16[3,128,768]{2,1,0:T(8,128)(2,1)S(1)}, bf16[3,128,768]{2,1,0:T(8,128)(2,1)S(1)}, u32[]{:S(2)}, u32[]{:S(2)}) collective-permute-start(bf16[3,128,768]{2,1,0:T(8,128)(2,1)S(1)} %fusion.1), channel_id=1, source_target_pairs={{0,8},{1,25},{8,0},{9,17},{16,24},{17,9},{24,16},{25,1},{2,10},{3,... | collective-permute-start | bytes 1769480 | tf_op jit(solution)/shard_map/ppermute | solution.py:287
  106.7 10.7 %collective-permute-start.15 = (bf16[32,2176]{1,0:T(8,128)(2,1)S(1)}, bf16[32,2176]{1,0:T(8,128)(2,1)S(1)}, u32[]{:S(2)}, u32[]{:S(2)}) collective-permute-start(bf16[32,2176]{1,0:T(8,128)(2,1)S(1)} %get-tuple-element.46), channel_id=1, source_target_pairs={{0,4},{2,6},{4,0},{6,2},{1,5},{3,7},{5,1},{7,3},{8,12},{10,14},{12... | collective-permute-start | bytes 417800 | tf_op jit(solution)/shard_map/ppermute | solution.py:282
  110.4 7.0 %collective-permute-start.14 = (bf16[32,2176]{1,0:T(8,128)(2,1)S(1)}, bf16[32,2176]{1,0:T(8,128)(2,1)S(1)}, u32[]{:S(2)}, u32[]{:S(2)}) collective-permute-start(bf16[32,2176]{1,0:T(8,128)(2,1)S(1)} %get-tuple-element.47), channel_id=1, source_target_pairs={{0,6},{2,4},{4,2},{6,0},{1,7},{3,5},{5,3},{7,1},{8,14},{10,12},{12... | collective-permute-start | bytes 417800 | tf_op jit(solution)/shard_map/ppermute | solution.py:282
  111.0 6.4 %collective-permute-start.13 = (bf16[32,2176]{1,0:T(8,128)(2,1)S(1)}, bf16[32,2176]{1,0:T(8,128)(2,1)S(1)}, u32[]{:S(2)}, u32[]{:S(2)}) collective-permute-start(bf16[32,2176]{1,0:T(8,128)(2,1)S(1)} %get-tuple-element.45), channel_id=1, source_target_pairs={{0,2},{2,0},{4,6},{6,4},{1,3},{3,1},{5,7},{7,5},{8,10},{10,8},{12,... | collective-permute-start | bytes 417800 | tf_op jit(solution)/shard_map/ppermute | solution.py:282

commit v4 on v3

--- a/solution.py
+++ b/solution.py
@@ -17,7 +17,6 @@
 X_ORDER = ((1, 3, 2), (3, 1, 2))
 Z_ORDER = (1, 3, 2)
 PAIR = (1, 3)
-CHUNKS = ((0,), (1, 2, 3))
 
 
 def plane(step, first):
@@ -49,7 +48,7 @@
         copy.wait()
 
 
-def forward_rows(row_refs, place_ref, sel_ref, weights_ref, h_ref, gp_ref):
+def forward_rows(row_refs, size, sel_ref, weights_ref, h_ref, gp_ref):
     half = row_refs[0].shape[0]
     _, width, hidden = weights_ref.shape
     tile = 256
@@ -57,9 +56,9 @@
 
     def step(j, carry):
         cols = pl.ds(pl.multiple_of(j * tile, tile), tile)
-        for block in range(len(row_refs) // 2):
-            pair = row_refs[2 * block : 2 * block + 2]
-            rows = slice(2 * half * block, 2 * half * (block + 1))
+        for first in range(0, len(row_refs), size):
+            pair = row_refs[first : first + size]
+            rows = slice(half * first, half * (first + size))
             x = jnp.concatenate([r[:, :width] for r in pair], axis=0)
             dy = jnp.concatenate([r[:, width : 2 * width] for r in pair], axis=0)
             p = jnp.concatenate([r[:, 2 * width :] for r in pair], axis=0).astype(F32)
@@ -107,20 +106,21 @@
 
 def early_kernel(place_ref, sel_ref, weights_ref, *refs):
     *row_refs, h_ref, gp_ref = refs
-    forward_rows(row_refs, place_ref, sel_ref, weights_ref, h_ref, gp_ref)
-
-
-def late_kernel(old, count, place_ref, sel_ref, weights_ref, old_h_ref, *refs):
-    row_refs, (h_ref, gp_ref, other_ref, own_ref, rows_ref) = refs[:count], refs[count:]
-    forward_rows(row_refs[old:], place_ref, sel_ref, weights_ref, h_ref, gp_ref)
-    cols = place_ref
-    weight_rows(weights_ref.shape[1], 0, cols, row_refs, (old_h_ref, h_ref), other_ref, own_ref, rows_ref)
+    forward_rows(row_refs, len(row_refs), sel_ref, weights_ref, h_ref, gp_ref)
+
+
+def late_kernel(old, place_ref, sel_ref, weights_ref, *refs):
+    h_refs, refs = refs[: len(old)], refs[len(old) :]
+    row_refs, (h_ref, gp_ref, other_ref, own_ref, turned_ref) = refs[:-5], refs[-5:]
+    last = row_refs[sum(old) :]
+    forward_rows(last, len(last), sel_ref, weights_ref, h_ref, gp_ref)
+    hs = (*h_refs, h_ref)
+    weight_rows(weights_ref.shape[1], 0, place_ref, row_refs, hs, other_ref, own_ref, turned_ref)
 
 
 def rest_kernel(count, width, place_ref, *refs):
     row_refs, h_refs, (other_ref, own_ref, rows_ref) = refs[:count], refs[count:-3], refs[-3:]
-    cols = place_ref
-    weight_rows(width, 1, cols, row_refs, h_refs, other_ref, own_ref, rows_ref)
+    weight_rows(width, 2, place_ref, row_refs, h_refs, other_ref, own_ref, rows_ref)
 
 
 def on_chip(kernel, name, args, outs, scratch=(), far=0):
@@ -146,16 +146,16 @@
             place = 0 if x == 0 else 1 + which
             for z in range(SIDE):
                 block, inner = (z, place) if which == core else (place, z)
-                chunk = [block in blocks for blocks in CHUNKS].index(True)
-                at = CHUNKS[chunk].index(block)
-                order.append((chunk, ((at * 2 + which) * SIDE + inner) * tokens))
+                chunk, at = (0, which) if block == 0 else (1 + which, block - 1)
+                order.append((chunk, (at * SIDE + inner) * tokens))
     return order
 
 
 def slot_kernel(tokens, chunks, place_ref, sel_ref, weights_ref, *refs):
-    hs, gps = refs[:chunks], refs[chunks : 2 * chunks]
-    own_ref, pair_ref, rows_ref = refs[2 * chunks :]
+    hs, gps, refs = refs[:chunks], refs[chunks : 2 * chunks], refs[2 * chunks :]
+    row_refs, (next_other_ref, next_own_ref, own_ref, pair_ref, turned_ref, rows_ref) = refs[:-6], refs[-6:]
     _, width, hidden = weights_ref.shape
+    weight_rows(width, 1, place_ref, row_refs, hs, next_other_ref, next_own_ref, turned_ref)
     half = own_ref.shape[0]
     for core in range(2):
 
@@ -230,50 +230,49 @@
     )
     swap = lambda piece: [piece, lax.ppermute(piece, "core", SWAP)]
     pieces = swap(line)
-    early = 2 * line.shape[0]
-    h0, gp0 = on_chip(
-        early_kernel,
-        "forward",
-        (place, sel, weights, *pieces),
-        [((3, early, hidden), BF16), ((early, LANES), F32)],
-    )
-    *mine[1:3], h0 = lax.optimization_barrier((*mine[1:3], h0))
-    for piece in mine[1:]:
-        pieces += swap(piece)
-    late = 3 * early
+    span = line.shape[0]
+    forwarded = lambda count: [((3, count * span, hidden), BF16), ((count * span, LANES), F32)]
+    h0, gp0 = on_chip(early_kernel, "forward", (place, sel, weights, *pieces), forwarded(2))
+    *mine[1:], h0 = lax.optimization_barrier((*mine[1:], h0))
+    others = [swap(piece)[1] for piece in mine[1:]]
+    h1, gp1 = on_chip(early_kernel, "forward_mine", (place, sel, weights, *mine[1:]), forwarded(3))
+    pieces += mine[1:] + others
     moving = lambda steps: ((steps, 3, LANES, hidden), BF16)
-    turned = pltpu.VMEM((2, 2 * LANES, early + late), BF16)
-    h1, gp1, other, own = on_chip(
-        functools.partial(late_kernel, 2, len(pieces)),
+    turned = pltpu.VMEM((2, 2 * LANES, len(pieces) * span), BF16)
+    h2, gp2, other, own = on_chip(
+        functools.partial(late_kernel, (2, 3)),
         "forward_and_first",
-        (place, sel, weights, h0, *pieces),
-        [((3, late, hidden), BF16), ((late, LANES), F32), moving(1), moving(1)],
+        (place, sel, weights, h0, h1, *pieces),
+        forwarded(3) + [moving(1)] * 2,
         [turned],
     )
 
     ring = lambda rows: lax.ppermute(rows, ("y", "core"), RING)
     other, own = ring(other[0]), ring(own[0])
+    half = 2 * SIDE * tokens
+    rows = ((half, width + LANES), BF16)
+    other_next, own_next, part, away = on_chip(
+        functools.partial(slot_kernel, tokens, 3),
+        "second_and_slots",
+        (place, sel, weights, h0, h1, h2, gp0, gp1, gp2, *pieces),
+        [moving(1), moving(1), rows, rows],
+        [turned, pltpu.VMEM((2, 2 * half, hidden), BF16)],
+    )
+    other, h2 = lax.optimization_barrier((add(other_next[0], other), h2))
+    other = ring(other)
     rest = on_chip(
         functools.partial(rest_kernel, len(pieces), width),
         "weight_terms",
-        (place, *pieces, h0, h1),
-        [moving(3), moving(3)],
+        (place, *pieces, h0, h1, h2),
+        [moving(2), moving(2)],
         [turned],
     )
-    other = add(rest[0][0], other)
-    other, h1 = lax.optimization_barrier((other, h1))
-    other, own = ring(other), ring(add(rest[1][0], own))
-    half = 2 * SIDE * tokens
-    rows = ((half, width + LANES), BF16)
-    part, away = on_chip(
-        functools.partial(slot_kernel, tokens, 2),
-        "slot_terms",
-        (place, sel, weights, h0, h1, gp0, gp1),
-        [rows, rows],
-        [pltpu.VMEM((2, 2 * half, hidden), BF16)],
-    )
-
-    part = add(part, lax.ppermute(away, ("x", "core"), X_PAIR))
+    own, rest = lax.optimization_barrier((own, rest))
+    own = ring(add(own_next[0], own))
+
+    away = lax.ppermute(away, ("x", "core"), X_PAIR)
+    other, away = lax.optimization_barrier((add(rest[0][0], other), away))
+    part = add(part, away)
     half = part.shape[0] // 2
     part = add(part[:half], lax.ppermute(part[half:], "core", SWAP))
     part = part.reshape((SIDE, tokens, part.shape[1]))
@@ -283,9 +282,9 @@
     grad_input = total[:, :width].astype(BF16)
     grad_prob = jnp.sum(jnp.where(hot, total[:, None, width:], 0.0), axis=2)
 
-    other, own = ring(add(rest[0][1], other)), ring(add(rest[1][1], own))
-    other = lax.ppermute(add(rest[0][2], other), ("x", "core"), X_PAIR)
-    own = add(rest[1][2], own)
+    other, own = ring(other), ring(add(rest[1][0], own))
+    other = lax.ppermute(add(rest[0][1], other), ("x", "core"), X_PAIR)
+    own = add(rest[1][1], own)
     even, odd = jnp.where(expert == 0, own, other), jnp.where(expert == 0, other, own)
     grad_weights = jnp.transpose(jnp.stack([even, odd], axis=0), (2, 1, 0, 3))
     return (grad_input, grad_prob, grad_weights)

time: 119 us -> 115 us (0.966)
  waiting for transfers between devices: 31.1 us -> 23.1 us
  Pallas kernels: 31.3 us -> 35.1 us
    ppermute x6, waiting for transfers between devices: 16.4 us -> 7.62 us  [shards(): ring = lambda rows: lax.ppermute(rows, ('y', 'core'), RING)]
    ppermute x4, waiting for transfers between devices: 4.39 us -> 0.01 us  [shards(): swap = lambda piece: [piece, lax.ppermute(piece, 'core', SWAP)]]
    pallas_call x5 -> x6, Pallas kernels: 31.3 us -> 35.1 us  [on_chip(): pl.pallas_call(kernel, name=name, in_specs=[pl.BlockSpec(memory_space=plt...]
    ppermute x3, waiting for transfers between devices: 0.01 us -> 3.73 us  [shards(): total = total + lax.ppermute(part[n + 1], 'z', Z_MOVE[n]).astype(F32)]
    another operation x1, other arithmetic: 0.29 us -> 1.51 us  [shards(): grad_weights = jnp.transpose(jnp.stack([even, odd], axis=0), (2, 1, 0, 3))]
  transfers between devices with their start and end apart: 22 -> 22, of which waited for: 13 -> 11; matrix products, arithmetic and copies ran while one was open for 23% -> 23% of each run, Pallas kernels for 17% -> 24%
where the time goes in v4:
time: 115 us
  Pallas kernels  35.1 us (31%)
  local copies, waits for them, and re-layouts  24.1 us (21%)
  waiting for transfers between devices  23.1 us (20%)
  starting transfers between devices  22.8 us (20%)
  other arithmetic  9.01 us (8%)
    pallas_call x6, Pallas kernels, on_chip(): pl.pallas_call(kernel, name=name, in_specs=[pl.BlockSpec(memory_space=plt...  35.1 us
    unnamed x19, local copies, waits for them, and re-layouts  21.7 us
    ppermute x6, waiting for transfers between devices, shards(): ring = lambda rows: lax.ppermute(rows, ('y', 'core'), RING)  7.62 us
    convert_element_type x7, other arithmetic, add(): return total.astype(BF16)  5.92 us
    ppermute x6, starting transfers between devices, shards(): ring = lambda rows: lax.ppermute(rows, ('y', 'core'), RING)  5.74 us
    ppermute x3, starting transfers between devices, shards(): lax.ppermute(line, axes, plane(n, False))  5.48 us
    ppermute x3, waiting for transfers between devices, shards(): lax.ppermute(line, axes, plane(n, False))  4.9 us
    ppermute x1, waiting for transfers between devices, shards(): other = lax.ppermute(add(rest[0][1], other), ('x', 'core'), X_PAIR)  4.43 us
  transfers between devices with their start and end apart: 22, of which 11 were waited for; matrix products, arithmetic and copies ran while one was open for 23% of the time, Pallas kernels for 24%

profile of v4, /device:TPU:0, one launch (start us, length us, event | category | flops | bytes accessed | tf_op | source)
XLA Modules:
  0.0 115.0 jit_solution(7303539389529083185)
XLA Ops:
  2.3 1.0 pad_maximum_fusion.1
  3.3 3.2 %collective-permute-start.2 = (bf16[32,4224]{1,0:T(8,128)(2,1)S(1)}, bf16[32,4224]{1,0:T(8,128)(2,1)S(1)}, u32[]{:S(2)}, u32[]{:S(2)}) collective-permute-start(bf16[32,4224]{1,0:T(8,128)(2,1)S(1)} %pad_maximum_fusion.1), channel_id=1, source_target_pairs={{0,16},{1,5},{2,18},{3,7},{4,20},{5,1},{6,22},{7,3},{8,24},{9,13},... | collective-permute-start | bytes 811016 | tf_op jit(solution)/shard_map/ppermute | solution.py:207
  6.5 1.1 collective-permute-start.1
  7.6 6.2 %copy.23 = bf16[2048,2,768]{2,0,1:T(8,128)(2,1)} copy(bf16[2048,2,768]{2,1,0:T(2,128)(2,1)} %param.11) | data formatting | bytes 12582912 | tf_op args[5]
  14.7 1.9 %collective-permute-start.3 = (bf16[128,4224]{1,0:T(8,128)(2,1)S(1)}, bf16[128,4224]{1,0:T(8,128)(2,1)S(1)}, u32[]{:S(2)}, u32[]{:S(2)}) collective-permute-start(bf16[128,4224]{1,0:T(8,128)(2,1)S(1)} %pad_maximum_fusion.refs_0_.refs_2_.refs_6_), channel_id=1, source_target_pairs={{0,2},{1,25},{2,0},{3,27},{4,6},{5,29},{6,4},{7,31},{8,10},{9,17},... | collective-permute-start | bytes 3244040 | tf_op jit(solution)/shard_map/ppermute | solution.py:210
  16.6 2.5 %collective-permute-start.4 = (bf16[128,4224]{1,0:T(8,128)(2,1)S(1)}, bf16[128,4224]{1,0:T(8,128)(2,1)}, u32[]{:S(2)}, u32[]{:S(2)}) collective-permute-start(bf16[128,4224]{1,0:T(8,128)(2,1)S(1)} %pad_maximum_fusion.refs_0_.refs_2_.refs_6_), channel_id=1, source_target_pairs={{0,6},{1,9},{2,4},{3,11},{4,2},{5,13},{6,0},{7,15},{8,14},{9,1},{1... | collective-permute-start | bytes 3244040 | tf_op jit(solution)/shard_map/ppermute | solution.py:210
  19.2 1.1 collective-permute-start.5
  20.2 11.8 %copy.22 = bf16[2048,2,2,768]{3,0,2,1:T(8,128)(2,1)} copy(bf16[2048,2,2,768]{3,2,1,0:T(2,128)(2,1)} %param.10) | data formatting | bytes 25165824 | tf_op args[4]
  32.1 4.3 %hold.1.weights_ref = bf16[3,2048,768]{2,1,0:T(8,128)(2,1)S(1)} custom-call(s32[10]{0:T(128)S(1)} %stack.52.place_ref, bf16[2,2,2048,768]{3,2,1,0:T(8,128)(2,1)} %bitcast.48, bf16[2,2048,768]{2,1,0:T(8,128)(2,1)} %bitcast.49), custom_call_target="tpu_custom_call" | custom-call | flops 1048576 | bytes 65536 | tf_op jit(solution)/shard_map/hold/pallas_call | solution.py:128
  36.5 3.6 %forward.1 = (bf16[3,256,768]{2,1,0:T(8,128)(2,1)S(1)}, f32[256,128]{1,0:T(8,128)S(1)}) custom-call(s32[10]{0:T(128)S(1)} %stack.52.place_ref, f32[1,128]{1,0:T(1,128)S(1)} %compare_convert_fusion.sel_ref, bf16[3,2048,768]{2,1,0:T(8,128)(2,1)S(1)} %hold.1.weights_ref, bf16[128,4224]{1,0:T(8,128)(2,1)S(1)} %pad_maximum_fusion.refs_0_.refs_2_.refs_6_, ...), custom_call_target="tpu_custom_call" | custom-call | flops 1048576 | bytes 65536 | tf_op jit(solution)/shard_map/forward/pallas_call | solution.py:128
  40.1 3.3 %collective-permute-done.4.refs_1_.refs_5_.refs_9_.refs_3_ = bf16[128,4224]{1,0:T(8,128)(2,1)} collective-permute-done((bf16[128,4224]{1,0:T(8,128)(2,1)S(1)}, bf16[128,4224]{1,0:T(8,128)(2,1)}, u32[]{:S(2)}, u32[]{:S(2)}) %collective-permute-start.4) | collective-permute-done | bytes 1081376 | tf_op jit(solution)/shard_map/ppermute | solution.py:210
  43.4 1.6 %collective-permute-done.5.refs_2_.refs_6_.refs_10_.refs_4_ = bf16[128,4224]{1,0:T(8,128)(2,1)} collective-permute-done((bf16[128,4224]{1,0:T(8,128)(2,1)S(1)}, bf16[128,4224]{1,0:T(8,128)(2,1)}, u32[]{:S(2)}, u32[]{:S(2)}) %collective-permute-start.5) | collective-permute-done | bytes 1081376 | tf_op jit(solution)/shard_map/ppermute | solution.py:210
  45.6 5.9 %forward_mine.1 = (bf16[3,384,768]{2,1,0:T(8,128)(2,1)S(1)}, f32[384,128]{1,0:T(8,128)S(1)}) custom-call(s32[10]{0:T(128)S(1)} %stack.52.place_ref, f32[1,128]{1,0:T(1,128)S(1)} %compare_convert_fusion.sel_ref, bf16[3,2048,768]{2,1,0:T(8,128)(2,1)S(1)} %hold.1.weights_ref, bf16[128,4224]{1,0:T(8,128)(2,1)S(1)} %collective-permute-done.3.refs_0_.refs_4_.refs_8_.refs_2_, ...), custom_call_target="tpu_custom_call" | custom-call | flops 1048576 | bytes 65536 | tf_op jit(solution)/shard_map/forward_mine/pallas_call | solution.py:128
  51.5 7.7 %forward_and_first.1 = (bf16[3,384,768]{2,1,0:T(8,128)(2,1)S(1)}, f32[384,128]{1,0:T(8,128)S(1)}, bf16[1,3,128,768]{3,2,1,0:T(8,128)(2,1)S(1)}, bf16[1,3,128,768]{3,2,1,0:T(8,128)(2,1)S(1)}) custom-call(s32[10]{0:T(128)S(1)} %stack.52.place_ref, f32[1,128]{1,0:T(1,128)S(1)} %compare_convert_fusion.sel_ref, bf16[3,2048,768]{2,1,0:T(8,128)(2,1)S(1)} %hold.1.weights_ref, ...), custom_call_target="tpu_custom_call" | custom-call | flops 1048576 | bytes 65536 | tf_op jit(solution)/shard_map/forward_and_first/pallas_call | solution.py:128
  59.2 1.6 %collective-permute-start.11 = (bf16[3,128,768]{2,1,0:T(8,128)(2,1)S(1)}, bf16[3,128,768]{2,1,0:T(8,128)(2,1)S(1)}, u32[]{:S(2)}, u32[]{:S(2)}) collective-permute-start(bf16[3,128,768]{2,1,0:T(8,128)(2,1)S(1)} %bitcast.47), channel_id=1, source_target_pairs={{0,32},{1,97},{32,64},{33,1},{64,96},{65,33},{96,0},{97,65},{2,34}... | collective-permute-start | bytes 1769480 | tf_op jit(solution)/shard_map/ppermute | solution.py:250
  60.8 1.6 %collective-permute-start.10 = (bf16[3,128,768]{2,1,0:T(8,128)(2,1)S(1)}, bf16[3,128,768]{2,1,0:T(8,128)(2,1)S(1)}, u32[]{:S(2)}, u32[]{:S(2)}) collective-permute-start(bf16[3,128,768]{2,1,0:T(8,128)(2,1)S(1)} %bitcast.46), channel_id=1, source_target_pairs={{0,32},{1,97},{32,64},{33,1},{64,96},{65,33},{96,0},{97,65},{2,34}... | collective-permute-start | bytes 1769480 | tf_op jit(solution)/shard_map/ppermute | solution.py:250
  62.4 8.5 %second_and_slots.1 = (bf16[1,3,128,768]{3,2,1,0:T(8,128)(2,1)S(1)}, bf16[1,3,128,768]{3,2,1,0:T(8,128)(2,1)S(1)}, bf16[256,2176]{1,0:T(8,128)(2,1)S(1)}, bf16[256,2176]{1,0:T(8,128)(2,1)S(1)}) custom-call(s32[10]{0:T(128)S(1)} %stack.52.place_ref, f32[1,128]{1,0:T(1,128)S(1)} %compare_convert_fusion.sel_ref, bf16[3,2048,768]{2,1,0:T(8,128)(2,1)S(1)} %hold.1.weights_ref, ...), custom_call_target="tpu_custom_call" | custom-call | flops 1048576 | bytes 65536 | tf_op jit(solution)/shard_map/second_and_slots/pallas_call | solution.py:128
  70.9 1.5 %collective-permute-start.13 = (bf16[256,2176]{1,0:T(8,128)(2,1)S(1)}, bf16[256,2176]{1,0:T(8,128)(2,1)S(1)}, u32[]{:S(2)}, u32[]{:S(2)}) collective-permute-start(bf16[256,2176]{1,0:T(8,128)(2,1)S(1)} %get-tuple-element.51), channel_id=1, source_target_pairs={{0,8},{1,25},{8,0},{9,17},{16,24},{17,9},{24,16},{25,1},{2,10},{3,... | collective-permute-start | bytes 3342344 | tf_op jit(solution)/shard_map/ppermute | solution.py:273
  72.6 1.3 %collective-permute-start.12 = (bf16[3,128,768]{2,1,0:T(8,128)(2,1)S(1)}, bf16[3,128,768]{2,1,0:T(8,128)(2,1)S(1)}, u32[]{:S(2)}, u32[]{:S(2)}) collective-permute-start(bf16[3,128,768]{2,1,0:T(8,128)(2,1)S(1)} %fusion.5), channel_id=1, source_target_pairs={{0,32},{1,97},{32,64},{33,1},{64,96},{65,33},{96,0},{97,65},{2,34}... | collective-permute-start | bytes 1769480 | tf_op jit(solution)/shard_map/ppermute | solution.py:250
  73.9 5.1 %weight_terms.1 = (bf16[2,3,128,768]{3,2,1,0:T(8,128)(2,1)S(1)}, bf16[2,3,128,768]{3,2,1,0:T(8,128)(2,1)S(1)}) custom-call(s32[10]{0:T(128)S(1)} %stack.52.place_ref, bf16[128,4224]{1,0:T(8,128)(2,1)S(1)} %pad_maximum_fusion.refs_0_.refs_2_.refs_6_, bf16[128,4224]{1,0:T(8,128)(2,1)S(1)} %collective-permute-done.6.refs_1_.refs_3_.refs_7_, ...), custom_call_target="tpu_custom_call" | custom-call | flops 1048576 | bytes 65536 | tf_op jit(solution)/shard_map/weight_terms/pallas_call | solution.py:128
  79.5 4.3 %collective-permute-done.12 = bf16[3,128,768]{2,1,0:T(8,128)(2,1)S(1)} collective-permute-done((bf16[3,128,768]{2,1,0:T(8,128)(2,1)S(1)}, bf16[3,128,768]{2,1,0:T(8,128)(2,1)S(1)}, u32[]{:S(2)}, u32[]{:S(2)}) %collective-permute-start.12) | collective-permute-done | bytes 589856 | tf_op jit(solution)/shard_map/ppermute | solution.py:250
  83.8 1.0 fusion.4
  84.7 1.8 %collective-permute-done.13 = bf16[256,2176]{1,0:T(8,128)(2,1)S(1)} collective-permute-done((bf16[256,2176]{1,0:T(8,128)(2,1)S(1)}, bf16[256,2176]{1,0:T(8,128)(2,1)S(1)}, u32[]{:S(2)}, u32[]{:S(2)}) %collective-permute-start.13) | collective-permute-done | bytes 1114144 | tf_op jit(solution)/shard_map/ppermute | solution.py:273
  87.6 1.0 collective-permute-start.14
  90.4 2.0 %fusion.2 = bf16[3,128,768]{2,1,0:T(8,128)(2,1)} fusion(bf16[3,128,768]{2,1,0:T(8,128)(2,1)} %collective-permute-done.18, bf16[2,3,128,768]{3,2,1,0:T(8,128)(2,1)S(1)} %copy-done.3), kind=kLoop, calls=%fused_computation.9 | loop fusion | flops 1179648 | bytes 1769472 | tf_op jit(solution)/shard_map/convert_element_type | solution.py:190
  92.5 1.4 %add_convert_fusion.1 = bf16[128,2176]{1,0:T(8,128)(2,1)S(1)} fusion(bf16[128,2176]{1,0:T(8,128)(2,1)} %collective-permute-done.14, bf16[256,2176]{1,0:T(8,128)(2,1)} %copy-done.4), kind=kLoop, calls=%fused_computation.16 | loop fusion | flops 1114112 | bytes 1671168 | tf_op jit(solution)/shard_map/convert_element_type | solution.py:190
  94.0 2.1 %collective-permute-start.17 = (bf16[32,2176]{1,0:T(8,128)(2,1)S(1)}, bf16[32,2176]{1,0:T(8,128)(2,1)S(1)}, u32[]{:S(2)}, u32[]{:S(2)}) collective-permute-start(bf16[32,2176]{1,0:T(8,128)(2,1)S(1)} %get-tuple-element.66), channel_id=1, source_target_pairs={{0,4},{2,6},{4,0},{6,2},{1,5},{3,7},{5,1},{7,3},{8,12},{10,14},{12... | collective-permute-start | bytes 417800 | tf_op jit(solution)/shard_map/ppermute | solution.py:281
  97.5 2.4 %collective-permute-done.20 = bf16[3,128,768]{2,1,0:T(8,128)(2,1)S(1)} collective-permute-done((bf16[3,128,768]{2,1,0:T(8,128)(2,1)}, bf16[3,128,768]{2,1,0:T(8,128)(2,1)S(1)}, u32[]{:S(2)}, u32[]{:S(2)}) %collective-permute-start.20) | collective-permute-done | bytes 589856 | tf_op jit(solution)/shard_map/ppermute | solution.py:250
  102.2 2.9 %collective-permute-done.16 = bf16[32,2176]{1,0:T(8,128)(2,1)S(1)} collective-permute-done((bf16[32,2176]{1,0:T(8,128)(2,1)S(1)}, bf16[32,2176]{1,0:T(8,128)(2,1)S(1)}, u32[]{:S(2)}, u32[]{:S(2)}) %collective-permute-start.16) | collective-permute-done | bytes 139296 | tf_op jit(solution)/shard_map/ppermute | solution.py:281
  106.7 4.4 %collective-permute-done.21 = bf16[3,128,768]{2,1,0:T(8,128)(2,1)} collective-permute-done((bf16[3,128,768]{2,1,0:T(8,128)(2,1)}, bf16[3,128,768]{2,1,0:T(8,128)(2,1)}, u32[]{:S(2)}, u32[]{:S(2)}) %collective-permute-start.21) | collective-permute-done | bytes 589856 | tf_op jit(solution)/shard_map/ppermute | solution.py:286
  111.1 1.5 %select_bitcast_fusion.1 = (bf16[1,3,128,768]{3,2,1,0:T(8,128)(2,1)S(1)}, bf16[1,3,128,768]{3,2,1,0:T(8,128)(2,1)S(1)}) fusion(bf16[3,128,768]{2,1,0:T(8,128)(2,1)} %collective-permute-done.21, pred[]{:T(512)S(6)} %eq.50, bf16[3,128,768]{2,1,0:T(8,128)(2,1)} %collective-permute-done.19, bf16[2,3,128,768]{3,2,1,0:T(8,128)(2,1)S(1)} %copy-done.3), kind=kLoop, calls=%fused_computation.19 | loop fusion | flops 1769472 | bytes 2949121 | tf_op jit(solution)/shard_map/stack | solution.py:289
  112.7 2.2 %copy.19 = bf16[128,3,2,768]{3,2,1,0:T(2,128)(2,1)} copy(bf16[128,3,2,768]{3,0,1,2:T(8,128)(2,1)S(1)} %maximum_bitcast_fusion) | data formatting | bytes 2359296
  (58 shorter events, 12.1 us)
Async XLA Ops:
  3.3 11.2 %copy-start.5 = (bf16[32,2048]{1,0:T(8,128)(2,1)S(1)}, bf16[32,2048]{1,0:T(8,128)(2,1)}, u32[]{:S(2)}) copy-start(bf16[32,2048]{1,0:T(8,128)(2,1)} %param.7) | copy-start | bytes 393220
  3.3 11.2 %copy-start.6 = (bf16[32,2048]{1,0:T(8,128)(2,1)S(1)}, bf16[32,2048]{1,0:T(8,128)(2,1)}, u32[]{:S(2)}) copy-start(bf16[32,2048]{1,0:T(8,128)(2,1)} %param.6) | copy-start | bytes 393220
  3.3 10.5 %collective-permute-start.2 = (bf16[32,4224]{1,0:T(8,128)(2,1)S(1)}, bf16[32,4224]{1,0:T(8,128)(2,1)S(1)}, u32[]{:S(2)}, u32[]{:S(2)}) collective-permute-start(bf16[32,4224]{1,0:T(8,128)(2,1)S(1)} %pad_maximum_fusion.1), channel_id=1, source_target_pairs={{0,16},{1,5},{2,18},{3,7},{4,20},{5,1},{6,22},{7,3},{8,24},{9,13},... | collective-permute-start | bytes 811016 | tf_op jit(solution)/shard_map/ppermute | solution.py:207
  6.5 7.8 %collective-permute-start.1 = (bf16[32,4224]{1,0:T(8,128)(2,1)S(1)}, bf16[32,4224]{1,0:T(8,128)(2,1)S(1)}, u32[]{:S(2)}, u32[]{:S(2)}) collective-permute-start(bf16[32,4224]{1,0:T(8,128)(2,1)S(1)} %pad_maximum_fusion.1), channel_id=1, source_target_pairs={{0,24},{1,7},{2,26},{3,5},{4,28},{5,3},{6,30},{7,1},{8,16},{9,15},... | collective-permute-start | bytes 811016 | tf_op jit(solution)/shard_map/ppermute | solution.py:207
  7.6 6.8 %collective-permute-start = (bf16[32,4224]{1,0:T(8,128)(2,1)S(1)}, bf16[32,4224]{1,0:T(8,128)(2,1)S(1)}, u32[]{:S(2)}, u32[]{:S(2)}) collective-permute-start(bf16[32,4224]{1,0:T(8,128)(2,1)S(1)} %pad_maximum_fusion.1), channel_id=1, source_target_pairs={{0,8},{1,3},{2,10},{3,1},{4,12},{5,7},{6,14},{7,5},{8,0},{9,11},{1... | collective-permute-start | bytes 811016 | tf_op jit(solution)/shard_map/ppermute | solution.py:207
  14.6 21.9 %collective-permute-start.6 = (bf16[128,4224]{1,0:T(8,128)(2,1)S(1)}, bf16[128,4224]{1,0:T(8,128)(2,1)S(1)}, u32[]{:S(2)}, u32[]{:S(2)}) collective-permute-start(bf16[128,4224]{1,0:T(8,128)(2,1)S(1)} %pad_maximum_fusion.refs_0_.refs_2_.refs_6_), channel_id=1, source_target_pairs={{0,1},{1,0},{2,3},{3,2},{4,5},{5,4},{6,7},{7,6},{8,9},{9,8},{10,11... | collective-permute-start | bytes 3244040 | tf_op jit(solution)/shard_map/ppermute | solution.py:231
  14.7 25.4 %collective-permute-start.3 = (bf16[128,4224]{1,0:T(8,128)(2,1)S(1)}, bf16[128,4224]{1,0:T(8,128)(2,1)S(1)}, u32[]{:S(2)}, u32[]{:S(2)}) collective-permute-start(bf16[128,4224]{1,0:T(8,128)(2,1)S(1)} %pad_maximum_fusion.refs_0_.refs_2_.refs_6_), channel_id=1, source_target_pairs={{0,2},{1,25},{2,0},{3,27},{4,6},{5,29},{6,4},{7,31},{8,10},{9,17},... | collective-permute-start | bytes 3244040 | tf_op jit(solution)/shard_map/ppermute | solution.py:210
  16.6 26.8 %collective-permute-start.4 = (bf16[128,4224]{1,0:T(8,128)(2,1)S(1)}, bf16[128,4224]{1,0:T(8,128)(2,1)}, u32[]{:S(2)}, u32[]{:S(2)}) collective-permute-start(bf16[128,4224]{1,0:T(8,128)(2,1)S(1)} %pad_maximum_fusion.refs_0_.refs_2_.refs_6_), channel_id=1, source_target_pairs={{0,6},{1,9},{2,4},{3,11},{4,2},{5,13},{6,0},{7,15},{8,14},{9,1},{1... | collective-permute-start | bytes 3244040 | tf_op jit(solution)/shard_map/ppermute | solution.py:210
  19.2 25.9 %collective-permute-start.5 = (bf16[128,4224]{1,0:T(8,128)(2,1)S(1)}, bf16[128,4224]{1,0:T(8,128)(2,1)}, u32[]{:S(2)}, u32[]{:S(2)}) collective-permute-start(bf16[128,4224]{1,0:T(8,128)(2,1)S(1)} %pad_maximum_fusion.refs_0_.refs_2_.refs_6_), channel_id=1, source_target_pairs={{0,4},{1,17},{2,6},{3,19},{4,0},{5,21},{6,2},{7,23},{8,12},{9,25},... | collective-permute-start | bytes 3244040 | tf_op jit(solution)/shard_map/ppermute | solution.py:210
  45.0 6.4 %collective-permute-start.7 = (bf16[128,4224]{1,0:T(8,128)(2,1)S(1)}, bf16[128,4224]{1,0:T(8,128)(2,1)S(1)}, u32[]{:S(2)}, u32[]{:S(2)}) collective-permute-start(bf16[128,4224]{1,0:T(8,128)(2,1)S(1)} %collective-permute-done.3.refs_0_.refs_4_.refs_8_.refs_2_), channel_id=1, source_target_pairs={{0,1},{1,0},{2,3},{3,2},{4,5},{5,4},{6,7},{7,6},{8,9},{9,8},{10,11... | collective-permute-start | bytes 3244040 | tf_op jit(solution)/shard_map/ppermute | solution.py:231
  45.0 6.5 %collective-permute-start.8 = (bf16[128,4224]{1,0:T(8,128)(2,1)}, bf16[128,4224]{1,0:T(8,128)(2,1)S(1)}, u32[]{:S(2)}, u32[]{:S(2)}) collective-permute-start(bf16[128,4224]{1,0:T(8,128)(2,1)} %collective-permute-done.4.refs_1_.refs_5_.refs_9_.refs_3_), channel_id=1, source_target_pairs={{0,1},{1,0},{2,3},{3,2},{4,5},{5,4},{6,7},{7,6},{8,9},{9,8},{10,11... | collective-permute-start | bytes 3244040 | tf_op jit(solution)/shard_map/ppermute | solution.py:231
  45.6 6.0 %collective-permute-start.9 = (bf16[128,4224]{1,0:T(8,128)(2,1)}, bf16[128,4224]{1,0:T(8,128)(2,1)S(1)}, u32[]{:S(2)}, u32[]{:S(2)}) collective-permute-start(bf16[128,4224]{1,0:T(8,128)(2,1)} %collective-permute-done.5.refs_2_.refs_6_.refs_10_.refs_4_), channel_id=1, source_target_pairs={{0,1},{1,0},{2,3},{3,2},{4,5},{5,4},{6,7},{7,6},{8,9},{9,8},{10,11... | collective-permute-start | bytes 3244040 | tf_op jit(solution)/shard_map/ppermute | solution.py:231
  59.2 13.3 %collective-permute-start.11 = (bf16[3,128,768]{2,1,0:T(8,128)(2,1)S(1)}, bf16[3,128,768]{2,1,0:T(8,128)(2,1)S(1)}, u32[]{:S(2)}, u32[]{:S(2)}) collective-permute-start(bf16[3,128,768]{2,1,0:T(8,128)(2,1)S(1)} %bitcast.47), channel_id=1, source_target_pairs={{0,32},{1,97},{32,64},{33,1},{64,96},{65,33},{96,0},{97,65},{2,34}... | collective-permute-start | bytes 1769480 | tf_op jit(solution)/shard_map/ppermute | solution.py:250
  60.8 18.2 %collective-permute-start.10 = (bf16[3,128,768]{2,1,0:T(8,128)(2,1)S(1)}, bf16[3,128,768]{2,1,0:T(8,128)(2,1)S(1)}, u32[]{:S(2)}, u32[]{:S(2)}) collective-permute-start(bf16[3,128,768]{2,1,0:T(8,128)(2,1)S(1)} %bitcast.46), channel_id=1, source_target_pairs={{0,32},{1,97},{32,64},{33,1},{64,96},{65,33},{96,0},{97,65},{2,34}... | collective-permute-start | bytes 1769480 | tf_op jit(solution)/shard_map/ppermute | solution.py:250
  70.9 15.6 %collective-permute-start.13 = (bf16[256,2176]{1,0:T(8,128)(2,1)S(1)}, bf16[256,2176]{1,0:T(8,128)(2,1)S(1)}, u32[]{:S(2)}, u32[]{:S(2)}) collective-permute-start(bf16[256,2176]{1,0:T(8,128)(2,1)S(1)} %get-tuple-element.51), channel_id=1, source_target_pairs={{0,8},{1,25},{8,0},{9,17},{16,24},{17,9},{24,16},{25,1},{2,10},{3,... | collective-permute-start | bytes 3342344 | tf_op jit(solution)/shard_map/ppermute | solution.py:273
  72.6 11.2 %collective-permute-start.12 = (bf16[3,128,768]{2,1,0:T(8,128)(2,1)S(1)}, bf16[3,128,768]{2,1,0:T(8,128)(2,1)S(1)}, u32[]{:S(2)}, u32[]{:S(2)}) collective-permute-start(bf16[3,128,768]{2,1,0:T(8,128)(2,1)S(1)} %fusion.5), channel_id=1, source_target_pairs={{0,32},{1,97},{32,64},{33,1},{64,96},{65,33},{96,0},{97,65},{2,34}... | collective-permute-start | bytes 1769480 | tf_op jit(solution)/shard_map/ppermute | solution.py:250
  79.0 5.7 %copy-start = (bf16[2,3,128,768]{3,2,1,0:T(8,128)(2,1)}, bf16[2,3,128,768]{3,2,1,0:T(8,128)(2,1)S(1)}, u32[]{:S(2)}) copy-start(bf16[2,3,128,768]{3,2,1,0:T(8,128)(2,1)S(1)} %get-tuple-element.49) | copy-start | bytes 3538948
  79.0 5.7 %copy-start.2 = (bf16[2,3,128,768]{3,2,1,0:T(8,128)(2,1)}, bf16[2,3,128,768]{3,2,1,0:T(8,128)(2,1)S(1)}, u32[]{:S(2)}) copy-start(bf16[2,3,128,768]{3,2,1,0:T(8,128)(2,1)S(1)} %get-tuple-element.53) | copy-start | bytes 3538948
  79.2 11.3 %collective-permute-start.18 = (bf16[3,128,768]{2,1,0:T(8,128)(2,1)S(1)}, bf16[3,128,768]{2,1,0:T(8,128)(2,1)}, u32[]{:S(2)}, u32[]{:S(2)}) collective-permute-start(bf16[3,128,768]{2,1,0:T(8,128)(2,1)S(1)} %fusion.1), channel_id=1, source_target_pairs={{0,32},{1,97},{32,64},{33,1},{64,96},{65,33},{96,0},{97,65},{2,34}... | collective-permute-start | bytes 1769480 | tf_op jit(solution)/shard_map/ppermute | solution.py:250
  86.5 4.0 %copy-start.3 = (bf16[2,3,128,768]{3,2,1,0:T(8,128)(2,1)S(1)}, bf16[2,3,128,768]{3,2,1,0:T(8,128)(2,1)}, u32[]{:S(2)}) copy-start(bf16[2,3,128,768]{3,2,1,0:T(8,128)(2,1)} %copy-done.2) | copy-start | bytes 3538948
  86.8 3.7 %copy-start.4 = (bf16[256,2176]{1,0:T(8,128)(2,1)}, bf16[256,2176]{1,0:T(8,128)(2,1)S(1)}, u32[]{:S(2)}) copy-start(bf16[256,2176]{1,0:T(8,128)(2,1)S(1)} %add_convert_fusion) | copy-start | bytes 3342340
  87.6 4.8 %collective-permute-start.14 = (bf16[128,2176]{1,0:T(8,128)(2,1)}, bf16[128,2176]{1,0:T(8,128)(2,1)}, u32[]{:S(2)}, u32[]{:S(2)}) collective-permute-start(bf16[128,2176]{1,0:T(8,128)(2,1)} %slice.54), channel_id=1, source_target_pairs={{0,1},{1,0},{2,3},{3,2},{4,5},{5,4},{6,7},{7,6},{8,9},{9,8},{10,11... | collective-permute-start | bytes 1671176 | tf_op jit(solution)/shard_map/ppermute | solution.py:277
  88.7 11.3 %collective-permute-start.20 = (bf16[3,128,768]{2,1,0:T(8,128)(2,1)}, bf16[3,128,768]{2,1,0:T(8,128)(2,1)S(1)}, u32[]{:S(2)}, u32[]{:S(2)}) collective-permute-start(bf16[3,128,768]{2,1,0:T(8,128)(2,1)} %fusion.4), channel_id=1, source_target_pairs={{0,32},{1,97},{32,64},{33,1},{64,96},{65,33},{96,0},{97,65},{2,34}... | collective-permute-start | bytes 1769480 | tf_op jit(solution)/shard_map/ppermute | solution.py:250
  92.5 7.5 %copy-start.1 = (bf16[2,3,128,768]{3,2,1,0:T(8,128)(2,1)S(1)}, bf16[2,3,128,768]{3,2,1,0:T(8,128)(2,1)}, u32[]{:S(2)}) copy-start(bf16[2,3,128,768]{3,2,1,0:T(8,128)(2,1)} %copy-done) | copy-start | bytes 3538948
  92.5 14.2 %collective-permute-start.19 = (bf16[3,128,768]{2,1,0:T(8,128)(2,1)}, bf16[3,128,768]{2,1,0:T(8,128)(2,1)}, u32[]{:S(2)}, u32[]{:S(2)}) collective-permute-start(bf16[3,128,768]{2,1,0:T(8,128)(2,1)} %fusion.2), channel_id=1, source_target_pairs={{0,32},{1,97},{32,64},{33,1},{64,96},{65,33},{96,0},{97,65},{2,34}... | collective-permute-start | bytes 1769480 | tf_op jit(solution)/shard_map/ppermute | solution.py:250
  94.0 8.2 %collective-permute-start.17 = (bf16[32,2176]{1,0:T(8,128)(2,1)S(1)}, bf16[32,2176]{1,0:T(8,128)(2,1)S(1)}, u32[]{:S(2)}, u32[]{:S(2)}) collective-permute-start(bf16[32,2176]{1,0:T(8,128)(2,1)S(1)} %get-tuple-element.66), channel_id=1, source_target_pairs={{0,4},{2,6},{4,0},{6,2},{1,5},{3,7},{5,1},{7,3},{8,12},{10,14},{12... | collective-permute-start | bytes 417800 | tf_op jit(solution)/shard_map/ppermute | solution.py:281
  96.1 9.0 %collective-permute-start.16 = (bf16[32,2176]{1,0:T(8,128)(2,1)S(1)}, bf16[32,2176]{1,0:T(8,128)(2,1)S(1)}, u32[]{:S(2)}, u32[]{:S(2)}) collective-permute-start(bf16[32,2176]{1,0:T(8,128)(2,1)S(1)} %get-tuple-element.67), channel_id=1, source_target_pairs={{0,6},{2,4},{4,2},{6,0},{1,7},{3,5},{5,3},{7,1},{8,14},{10,12},{12... | collective-permute-start | bytes 417800 | tf_op jit(solution)/shard_map/ppermute | solution.py:281
  96.7 8.4 %collective-permute-start.15 = (bf16[32,2176]{1,0:T(8,128)(2,1)S(1)}, bf16[32,2176]{1,0:T(8,128)(2,1)S(1)}, u32[]{:S(2)}, u32[]{:S(2)}) collective-permute-start(bf16[32,2176]{1,0:T(8,128)(2,1)S(1)} %get-tuple-element.65), channel_id=1, source_target_pairs={{0,2},{2,0},{4,6},{6,4},{1,3},{3,1},{5,7},{7,5},{8,10},{10,8},{12,... | collective-permute-start | bytes 417800 | tf_op jit(solution)/shard_map/ppermute | solution.py:281
  100.9 10.2 %collective-permute-start.21 = (bf16[3,128,768]{2,1,0:T(8,128)(2,1)}, bf16[3,128,768]{2,1,0:T(8,128)(2,1)}, u32[]{:S(2)}, u32[]{:S(2)}) collective-permute-start(bf16[3,128,768]{2,1,0:T(8,128)(2,1)} %fusion), channel_id=1, source_target_pairs={{0,8},{1,25},{8,0},{9,17},{16,24},{17,9},{24,16},{25,1},{2,10},{3,... | collective-permute-start | bytes 1769480 | tf_op jit(solution)/shard_map/ppermute | solution.py:286

commit v5 on v4

--- a/solution.py
+++ b/solution.py
@@ -146,7 +146,10 @@
             place = 0 if x == 0 else 1 + which
             for z in range(SIDE):
                 block, inner = (z, place) if which == core else (place, z)
-                chunk, at = (0, which) if block == 0 else (1 + which, block - 1)
+                if block == 0 or which == 0 and block == 1:
+                    chunk, at = 0, which + 2 * block
+                else:
+                    chunk, at = (2, block - 1) if which else (1, block - 2)
                 order.append((chunk, (at * SIDE + inner) * tokens))
     return order
 
@@ -232,15 +235,15 @@
     pieces = swap(line)
     span = line.shape[0]
     forwarded = lambda count: [((3, count * span, hidden), BF16), ((count * span, LANES), F32)]
-    h0, gp0 = on_chip(early_kernel, "forward", (place, sel, weights, *pieces), forwarded(2))
+    h0, gp0 = on_chip(early_kernel, "forward", (place, sel, weights, *pieces, mine[1]), forwarded(3))
     *mine[1:], h0 = lax.optimization_barrier((*mine[1:], h0))
     others = [swap(piece)[1] for piece in mine[1:]]
-    h1, gp1 = on_chip(early_kernel, "forward_mine", (place, sel, weights, *mine[1:]), forwarded(3))
+    h1, gp1 = on_chip(early_kernel, "forward_mine", (place, sel, weights, *mine[2:]), forwarded(2))
     pieces += mine[1:] + others
     moving = lambda steps: ((steps, 3, LANES, hidden), BF16)
     turned = pltpu.VMEM((2, 2 * LANES, len(pieces) * span), BF16)
     h2, gp2, other, own = on_chip(
-        functools.partial(late_kernel, (2, 3)),
+        functools.partial(late_kernel, (3, 2)),
         "forward_and_first",
         (place, sel, weights, h0, h1, *pieces),
         forwarded(3) + [moving(1)] * 2,

time: 115 us -> 115 us (level)
  waiting for transfers between devices: 23.1 us -> 21.6 us
    ppermute x3, waiting for transfers between devices: 4.9 us -> 3.54 us  [shards(): lax.ppermute(line, axes, plane(n, False))]
  transfers between devices with their start and end apart: 22 -> 22, of which waited for: 11 -> 12; matrix products, arithmetic and copies ran while one was open for 23% -> 23% of each run, Pallas kernels for 24% -> 24%
where the time goes in v5:
time: 115 us; the launch traced here: 114 us
  Pallas kernels  35.1 us (31%)
  local copies, waits for them, and re-layouts  25.1 us (22%)
  starting transfers between devices  22.6 us (20%)
  waiting for transfers between devices  21.6 us (19%)
  other arithmetic  9 us (8%)
    pallas_call x6, Pallas kernels, on_chip(): pl.pallas_call(kernel, name=name, in_specs=[pl.BlockSpec(memory_space=plt...  35.1 us
    unnamed x19, local copies, waits for them, and re-layouts  22.7 us
    ppermute x6, waiting for transfers between devices, shards(): ring = lambda rows: lax.ppermute(rows, ('y', 'core'), RING)  6.58 us
    convert_element_type x7, other arithmetic, add(): return total.astype(BF16)  5.9 us
    ppermute x6, starting transfers between devices, shards(): ring = lambda rows: lax.ppermute(rows, ('y', 'core'), RING)  5.75 us
    ppermute x3, starting transfers between devices, shards(): lax.ppermute(line, axes, plane(n, False))  5.35 us
    ppermute x3, starting transfers between devices, shards(): line = [row] + [lax.ppermute(row, axes, plane(n, True)) for n in range(3)]  4.33 us
    ppermute x1, waiting for transfers between devices, shards(): other = lax.ppermute(add(rest[0][1], other), ('x', 'core'), X_PAIR)  4.17 us
  transfers between devices with their start and end apart: 22, of which 12 were waited for; matrix products, arithmetic and copies ran while one was open for 23% of the time, Pallas kernels for 24%

profile of v5, /device:TPU:0, one launch (start us, length us, event | category | flops | bytes accessed | tf_op | source)
XLA Modules:
  0.0 114.3 jit_solution(13378499712459909352)
XLA Ops:
  2.3 1.0 pad_maximum_fusion.1
  3.3 3.2 %collective-permute-start.2 = (bf16[32,4224]{1,0:T(8,128)(2,1)S(1)}, bf16[32,4224]{1,0:T(8,128)(2,1)S(1)}, u32[]{:S(2)}, u32[]{:S(2)}) collective-permute-start(bf16[32,4224]{1,0:T(8,128)(2,1)S(1)} %pad_maximum_fusion.1), channel_id=1, source_target_pairs={{0,16},{1,5},{2,18},{3,7},{4,20},{5,1},{6,22},{7,3},{8,24},{9,13},... | collective-permute-start | bytes 811016 | tf_op jit(solution)/shard_map/ppermute | solution.py:210
  6.5 1.1 collective-permute-start.1
  7.6 6.2 %copy.23 = bf16[2048,2,768]{2,0,1:T(8,128)(2,1)} copy(bf16[2048,2,768]{2,1,0:T(2,128)(2,1)} %param.11) | data formatting | bytes 12582912 | tf_op args[5]
  14.6 2.0 %collective-permute-start.3 = (bf16[128,4224]{1,0:T(8,128)(2,1)S(1)}, bf16[128,4224]{1,0:T(8,128)(2,1)S(1)}, u32[]{:S(2)}, u32[]{:S(2)}) collective-permute-start(bf16[128,4224]{1,0:T(8,128)(2,1)S(1)} %pad_maximum_fusion.refs_0_.refs_2_.refs_6_), channel_id=1, source_target_pairs={{0,2},{1,25},{2,0},{3,27},{4,6},{5,29},{6,4},{7,31},{8,10},{9,17},... | collective-permute-start | bytes 3244040 | tf_op jit(solution)/shard_map/ppermute | solution.py:213
  17.1 2.9 %collective-permute-start.4 = (bf16[128,4224]{1,0:T(8,128)(2,1)S(1)}, bf16[128,4224]{1,0:T(8,128)(2,1)}, u32[]{:S(2)}, u32[]{:S(2)}) collective-permute-start(bf16[128,4224]{1,0:T(8,128)(2,1)S(1)} %pad_maximum_fusion.refs_0_.refs_2_.refs_6_), channel_id=1, source_target_pairs={{0,6},{1,9},{2,4},{3,11},{4,2},{5,13},{6,0},{7,15},{8,14},{9,1},{1... | collective-permute-start | bytes 3244040 | tf_op jit(solution)/shard_map/ppermute | solution.py:213
  20.5 11.8 %copy.22 = bf16[2048,2,2,768]{3,0,2,1:T(8,128)(2,1)} copy(bf16[2048,2,2,768]{3,2,1,0:T(2,128)(2,1)} %param.10) | data formatting | bytes 25165824 | tf_op args[4]
  32.4 4.3 %hold.1.weights_ref = bf16[3,2048,768]{2,1,0:T(8,128)(2,1)S(1)} custom-call(s32[10]{0:T(128)S(1)} %stack.52.place_ref, bf16[2,2,2048,768]{3,2,1,0:T(8,128)(2,1)} %bitcast.48, bf16[2,2048,768]{2,1,0:T(8,128)(2,1)} %bitcast.49), custom_call_target="tpu_custom_call" | custom-call | flops 1048576 | bytes 65536 | tf_op jit(solution)/shard_map/hold/pallas_call | solution.py:128
  36.7 4.9 %forward.1 = (bf16[3,384,768]{2,1,0:T(8,128)(2,1)S(1)}, f32[384,128]{1,0:T(8,128)S(1)}) custom-call(s32[10]{0:T(128)S(1)} %stack.52.place_ref, f32[1,128]{1,0:T(1,128)S(1)} %compare_convert_fusion.sel_ref, bf16[3,2048,768]{2,1,0:T(8,128)(2,1)S(1)} %hold.1.weights_ref, bf16[128,4224]{1,0:T(8,128)(2,1)S(1)} %pad_maximum_fusion.refs_0_.refs_2_.refs_6_, ...), custom_call_target="tpu_custom_call" | custom-call | flops 1048576 | bytes 65536 | tf_op jit(solution)/shard_map/forward/pallas_call | solution.py:128
  41.6 3.5 %collective-permute-done.4.refs_0_.refs_5_.refs_9_.refs_3_ = bf16[128,4224]{1,0:T(8,128)(2,1)} collective-permute-done((bf16[128,4224]{1,0:T(8,128)(2,1)S(1)}, bf16[128,4224]{1,0:T(8,128)(2,1)}, u32[]{:S(2)}, u32[]{:S(2)}) %collective-permute-start.4) | collective-permute-done | bytes 1081376 | tf_op jit(solution)/shard_map/ppermute | solution.py:213
  45.7 4.6 %forward_mine.1 = (bf16[3,256,768]{2,1,0:T(8,128)(2,1)S(1)}, f32[256,128]{1,0:T(8,128)S(1)}) custom-call(s32[10]{0:T(128)S(1)} %stack.52.place_ref, f32[1,128]{1,0:T(1,128)S(1)} %compare_convert_fusion.sel_ref, bf16[3,2048,768]{2,1,0:T(8,128)(2,1)S(1)} %hold.1.weights_ref, bf16[128,4224]{1,0:T(8,128)(2,1)} %collective-permute-done.4.refs_0_.refs_5_.refs_9_.refs_3_, ...), custom_call_target="tpu_custom_call" | custom-call | flops 1048576 | bytes 65536 | tf_op jit(solution)/shard_map/forward_mine/pallas_call | solution.py:128
  51.2 7.7 %forward_and_first.1 = (bf16[3,384,768]{2,1,0:T(8,128)(2,1)S(1)}, f32[384,128]{1,0:T(8,128)S(1)}, bf16[1,3,128,768]{3,2,1,0:T(8,128)(2,1)S(1)}, bf16[1,3,128,768]{3,2,1,0:T(8,128)(2,1)S(1)}) custom-call(s32[10]{0:T(128)S(1)} %stack.52.place_ref, f32[1,128]{1,0:T(1,128)S(1)} %compare_convert_fusion.sel_ref, bf16[3,2048,768]{2,1,0:T(8,128)(2,1)S(1)} %hold.1.weights_ref, ...), custom_call_target="tpu_custom_call" | custom-call | flops 1048576 | bytes 65536 | tf_op jit(solution)/shard_map/forward_and_first/pallas_call | solution.py:128
  58.9 1.6 %collective-permute-start.11 = (bf16[3,128,768]{2,1,0:T(8,128)(2,1)S(1)}, bf16[3,128,768]{2,1,0:T(8,128)(2,1)S(1)}, u32[]{:S(2)}, u32[]{:S(2)}) collective-permute-start(bf16[3,128,768]{2,1,0:T(8,128)(2,1)S(1)} %bitcast.47), channel_id=1, source_target_pairs={{0,32},{1,97},{32,64},{33,1},{64,96},{65,33},{96,0},{97,65},{2,34}... | collective-permute-start | bytes 1769480 | tf_op jit(solution)/shard_map/ppermute | solution.py:253
  60.5 1.6 %collective-permute-start.10 = (bf16[3,128,768]{2,1,0:T(8,128)(2,1)S(1)}, bf16[3,128,768]{2,1,0:T(8,128)(2,1)S(1)}, u32[]{:S(2)}, u32[]{:S(2)}) collective-permute-start(bf16[3,128,768]{2,1,0:T(8,128)(2,1)S(1)} %bitcast.46), channel_id=1, source_target_pairs={{0,32},{1,97},{32,64},{33,1},{64,96},{65,33},{96,0},{97,65},{2,34}... | collective-permute-start | bytes 1769480 | tf_op jit(solution)/shard_map/ppermute | solution.py:253
  62.1 8.5 %second_and_slots.1 = (bf16[1,3,128,768]{3,2,1,0:T(8,128)(2,1)S(1)}, bf16[1,3,128,768]{3,2,1,0:T(8,128)(2,1)S(1)}, bf16[256,2176]{1,0:T(8,128)(2,1)S(1)}, bf16[256,2176]{1,0:T(8,128)(2,1)S(1)}) custom-call(s32[10]{0:T(128)S(1)} %stack.52.place_ref, f32[1,128]{1,0:T(1,128)S(1)} %compare_convert_fusion.sel_ref, bf16[3,2048,768]{2,1,0:T(8,128)(2,1)S(1)} %hold.1.weights_ref, ...), custom_call_target="tpu_custom_call" | custom-call | flops 1048576 | bytes 65536 | tf_op jit(solution)/shard_map/second_and_slots/pallas_call | solution.py:128
  70.6 1.3 %collective-permute-start.13 = (bf16[256,2176]{1,0:T(8,128)(2,1)S(1)}, bf16[256,2176]{1,0:T(8,128)(2,1)S(1)}, u32[]{:S(2)}, u32[]{:S(2)}) collective-permute-start(bf16[256,2176]{1,0:T(8,128)(2,1)S(1)} %get-tuple-element.51), channel_id=1, source_target_pairs={{0,8},{1,25},{8,0},{9,17},{16,24},{17,9},{24,16},{25,1},{2,10},{3,... | collective-permute-start | bytes 3342344 | tf_op jit(solution)/shard_map/ppermute | solution.py:276
  72.0 1.4 %collective-permute-start.12 = (bf16[3,128,768]{2,1,0:T(8,128)(2,1)S(1)}, bf16[3,128,768]{2,1,0:T(8,128)(2,1)S(1)}, u32[]{:S(2)}, u32[]{:S(2)}) collective-permute-start(bf16[3,128,768]{2,1,0:T(8,128)(2,1)S(1)} %fusion.5), channel_id=1, source_target_pairs={{0,32},{1,97},{32,64},{33,1},{64,96},{65,33},{96,0},{97,65},{2,34}... | collective-permute-start | bytes 1769480 | tf_op jit(solution)/shard_map/ppermute | solution.py:253
  73.4 5.1 %weight_terms.1 = (bf16[2,3,128,768]{3,2,1,0:T(8,128)(2,1)S(1)}, bf16[2,3,128,768]{3,2,1,0:T(8,128)(2,1)S(1)}) custom-call(s32[10]{0:T(128)S(1)} %stack.52.place_ref, bf16[128,4224]{1,0:T(8,128)(2,1)S(1)} %pad_maximum_fusion.refs_0_.refs_2_.refs_6_, bf16[128,4224]{1,0:T(8,128)(2,1)S(1)} %collective-permute-done.6.refs_1_.refs_3_.refs_7_, ...), custom_call_target="tpu_custom_call" | custom-call | flops 1048576 | bytes 65536 | tf_op jit(solution)/shard_map/weight_terms/pallas_call | solution.py:128
  78.5 1.0 copy-done.2
  80.0 3.3 %collective-permute-done.12 = bf16[3,128,768]{2,1,0:T(8,128)(2,1)S(1)} collective-permute-done((bf16[3,128,768]{2,1,0:T(8,128)(2,1)S(1)}, bf16[3,128,768]{2,1,0:T(8,128)(2,1)S(1)}, u32[]{:S(2)}, u32[]{:S(2)}) %collective-permute-start.12) | collective-permute-done | bytes 589856 | tf_op jit(solution)/shard_map/ppermute | solution.py:253
  83.2 1.0 fusion.4
  84.2 2.0 %collective-permute-done.13 = bf16[256,2176]{1,0:T(8,128)(2,1)S(1)} collective-permute-done((bf16[256,2176]{1,0:T(8,128)(2,1)S(1)}, bf16[256,2176]{1,0:T(8,128)(2,1)S(1)}, u32[]{:S(2)}, u32[]{:S(2)}) %collective-permute-start.13) | collective-permute-done | bytes 1114144 | tf_op jit(solution)/shard_map/ppermute | solution.py:276
  88.8 2.1 %collective-permute-done.18 = bf16[3,128,768]{2,1,0:T(8,128)(2,1)} collective-permute-done((bf16[3,128,768]{2,1,0:T(8,128)(2,1)S(1)}, bf16[3,128,768]{2,1,0:T(8,128)(2,1)}, u32[]{:S(2)}, u32[]{:S(2)}) %collective-permute-start.18) | collective-permute-done | bytes 589856 | tf_op jit(solution)/shard_map/ppermute | solution.py:253
  90.9 2.0 %fusion.2 = bf16[3,128,768]{2,1,0:T(8,128)(2,1)} fusion(bf16[3,128,768]{2,1,0:T(8,128)(2,1)} %collective-permute-done.18, bf16[2,3,128,768]{3,2,1,0:T(8,128)(2,1)S(1)} %copy-done.3), kind=kLoop, calls=%fused_computation.9 | loop fusion | flops 1179648 | bytes 1769472 | tf_op jit(solution)/shard_map/convert_element_type | solution.py:193
  93.0 1.4 %add_convert_fusion.1 = bf16[128,2176]{1,0:T(8,128)(2,1)S(1)} fusion(bf16[128,2176]{1,0:T(8,128)(2,1)} %collective-permute-done.14, bf16[256,2176]{1,0:T(8,128)(2,1)} %copy-done.4), kind=kLoop, calls=%fused_computation.16 | loop fusion | flops 1114112 | bytes 1671168 | tf_op jit(solution)/shard_map/convert_element_type | solution.py:193
  94.5 2.1 %collective-permute-start.17 = (bf16[32,2176]{1,0:T(8,128)(2,1)S(1)}, bf16[32,2176]{1,0:T(8,128)(2,1)S(1)}, u32[]{:S(2)}, u32[]{:S(2)}) collective-permute-start(bf16[32,2176]{1,0:T(8,128)(2,1)S(1)} %get-tuple-element.66), channel_id=1, source_target_pairs={{0,4},{2,6},{4,0},{6,2},{1,5},{3,7},{5,1},{7,3},{8,12},{10,14},{12... | collective-permute-start | bytes 417800 | tf_op jit(solution)/shard_map/ppermute | solution.py:284
  98.0 1.2 %collective-permute-done.20 = bf16[3,128,768]{2,1,0:T(8,128)(2,1)S(1)} collective-permute-done((bf16[3,128,768]{2,1,0:T(8,128)(2,1)}, bf16[3,128,768]{2,1,0:T(8,128)(2,1)S(1)}, u32[]{:S(2)}, u32[]{:S(2)}) %collective-permute-start.20) | collective-permute-done | bytes 589856 | tf_op jit(solution)/shard_map/ppermute | solution.py:253
  99.3 1.0 fusion
  101.4 2.9 %collective-permute-done.16 = bf16[32,2176]{1,0:T(8,128)(2,1)S(1)} collective-permute-done((bf16[32,2176]{1,0:T(8,128)(2,1)S(1)}, bf16[32,2176]{1,0:T(8,128)(2,1)S(1)}, u32[]{:S(2)}, u32[]{:S(2)}) %collective-permute-start.16) | collective-permute-done | bytes 139296 | tf_op jit(solution)/shard_map/ppermute | solution.py:284
  106.2 4.2 %collective-permute-done.21 = bf16[3,128,768]{2,1,0:T(8,128)(2,1)} collective-permute-done((bf16[3,128,768]{2,1,0:T(8,128)(2,1)}, bf16[3,128,768]{2,1,0:T(8,128)(2,1)}, u32[]{:S(2)}, u32[]{:S(2)}) %collective-permute-start.21) | collective-permute-done | bytes 589856 | tf_op jit(solution)/shard_map/ppermute | solution.py:289
  110.4 1.5 %select_bitcast_fusion.1 = (bf16[1,3,128,768]{3,2,1,0:T(8,128)(2,1)S(1)}, bf16[1,3,128,768]{3,2,1,0:T(8,128)(2,1)S(1)}) fusion(bf16[3,128,768]{2,1,0:T(8,128)(2,1)} %collective-permute-done.21, pred[]{:T(512)S(6)} %eq.50, bf16[3,128,768]{2,1,0:T(8,128)(2,1)} %collective-permute-done.19, bf16[2,3,128,768]{3,2,1,0:T(8,128)(2,1)S(1)} %copy-done.3), kind=kLoop, calls=%fused_computation.19 | loop fusion | flops 1769472 | bytes 2949121 | tf_op jit(solution)/shard_map/stack | solution.py:292
  112.0 2.2 %copy.19 = bf16[128,3,2,768]{3,2,1,0:T(2,128)(2,1)} copy(bf16[128,3,2,768]{3,0,1,2:T(8,128)(2,1)S(1)} %maximum_bitcast_fusion) | data formatting | bytes 2359296
  (58 shorter events, 12.7 us)
Async XLA Ops:
  3.3 11.2 %copy-start.5 = (bf16[32,2048]{1,0:T(8,128)(2,1)S(1)}, bf16[32,2048]{1,0:T(8,128)(2,1)}, u32[]{:S(2)}) copy-start(bf16[32,2048]{1,0:T(8,128)(2,1)} %param.7) | copy-start | bytes 393220
  3.3 11.2 %copy-start.6 = (bf16[32,2048]{1,0:T(8,128)(2,1)S(1)}, bf16[32,2048]{1,0:T(8,128)(2,1)}, u32[]{:S(2)}) copy-start(bf16[32,2048]{1,0:T(8,128)(2,1)} %param.6) | copy-start | bytes 393220
  3.3 10.5 %collective-permute-start.2 = (bf16[32,4224]{1,0:T(8,128)(2,1)S(1)}, bf16[32,4224]{1,0:T(8,128)(2,1)S(1)}, u32[]{:S(2)}, u32[]{:S(2)}) collective-permute-start(bf16[32,4224]{1,0:T(8,128)(2,1)S(1)} %pad_maximum_fusion.1), channel_id=1, source_target_pairs={{0,16},{1,5},{2,18},{3,7},{4,20},{5,1},{6,22},{7,3},{8,24},{9,13},... | collective-permute-start | bytes 811016 | tf_op jit(solution)/shard_map/ppermute | solution.py:210
  6.5 7.8 %collective-permute-start.1 = (bf16[32,4224]{1,0:T(8,128)(2,1)S(1)}, bf16[32,4224]{1,0:T(8,128)(2,1)S(1)}, u32[]{:S(2)}, u32[]{:S(2)}) collective-permute-start(bf16[32,4224]{1,0:T(8,128)(2,1)S(1)} %pad_maximum_fusion.1), channel_id=1, source_target_pairs={{0,24},{1,7},{2,26},{3,5},{4,28},{5,3},{6,30},{7,1},{8,16},{9,15},... | collective-permute-start | bytes 811016 | tf_op jit(solution)/shard_map/ppermute | solution.py:210
  7.6 6.8 %collective-permute-start = (bf16[32,4224]{1,0:T(8,128)(2,1)S(1)}, bf16[32,4224]{1,0:T(8,128)(2,1)S(1)}, u32[]{:S(2)}, u32[]{:S(2)}) collective-permute-start(bf16[32,4224]{1,0:T(8,128)(2,1)S(1)} %pad_maximum_fusion.1), channel_id=1, source_target_pairs={{0,8},{1,3},{2,10},{3,1},{4,12},{5,7},{6,14},{7,5},{8,0},{9,11},{1... | collective-permute-start | bytes 811016 | tf_op jit(solution)/shard_map/ppermute | solution.py:210
  14.6 22.1 %collective-permute-start.3 = (bf16[128,4224]{1,0:T(8,128)(2,1)S(1)}, bf16[128,4224]{1,0:T(8,128)(2,1)S(1)}, u32[]{:S(2)}, u32[]{:S(2)}) collective-permute-start(bf16[128,4224]{1,0:T(8,128)(2,1)S(1)} %pad_maximum_fusion.refs_0_.refs_2_.refs_6_), channel_id=1, source_target_pairs={{0,2},{1,25},{2,0},{3,27},{4,6},{5,29},{6,4},{7,31},{8,10},{9,17},... | collective-permute-start | bytes 3244040 | tf_op jit(solution)/shard_map/ppermute | solution.py:213
  16.6 20.2 %collective-permute-start.6 = (bf16[128,4224]{1,0:T(8,128)(2,1)S(1)}, bf16[128,4224]{1,0:T(8,128)(2,1)S(1)}, u32[]{:S(2)}, u32[]{:S(2)}) collective-permute-start(bf16[128,4224]{1,0:T(8,128)(2,1)S(1)} %pad_maximum_fusion.refs_0_.refs_2_.refs_6_), channel_id=1, source_target_pairs={{0,1},{1,0},{2,3},{3,2},{4,5},{5,4},{6,7},{7,6},{8,9},{9,8},{10,11... | collective-permute-start | bytes 3244040 | tf_op jit(solution)/shard_map/ppermute | solution.py:234
  17.1 28.1 %collective-permute-start.4 = (bf16[128,4224]{1,0:T(8,128)(2,1)S(1)}, bf16[128,4224]{1,0:T(8,128)(2,1)}, u32[]{:S(2)}, u32[]{:S(2)}) collective-permute-start(bf16[128,4224]{1,0:T(8,128)(2,1)S(1)} %pad_maximum_fusion.refs_0_.refs_2_.refs_6_), channel_id=1, source_target_pairs={{0,6},{1,9},{2,4},{3,11},{4,2},{5,13},{6,0},{7,15},{8,14},{9,1},{1... | collective-permute-start | bytes 3244040 | tf_op jit(solution)/shard_map/ppermute | solution.py:213
  20.0 25.2 %collective-permute-start.5 = (bf16[128,4224]{1,0:T(8,128)(2,1)S(1)}, bf16[128,4224]{1,0:T(8,128)(2,1)}, u32[]{:S(2)}, u32[]{:S(2)}) collective-permute-start(bf16[128,4224]{1,0:T(8,128)(2,1)S(1)} %pad_maximum_fusion.refs_0_.refs_2_.refs_6_), channel_id=1, source_target_pairs={{0,4},{1,17},{2,6},{3,19},{4,0},{5,21},{6,2},{7,23},{8,12},{9,25},... | collective-permute-start | bytes 3244040 | tf_op jit(solution)/shard_map/ppermute | solution.py:213
  45.2 5.2 %collective-permute-start.7 = (bf16[128,4224]{1,0:T(8,128)(2,1)S(1)}, bf16[128,4224]{1,0:T(8,128)(2,1)S(1)}, u32[]{:S(2)}, u32[]{:S(2)}) collective-permute-start(bf16[128,4224]{1,0:T(8,128)(2,1)S(1)} %collective-permute-done.3.refs_2_.refs_4_.refs_8_), channel_id=1, source_target_pairs={{0,1},{1,0},{2,3},{3,2},{4,5},{5,4},{6,7},{7,6},{8,9},{9,8},{10,11... | collective-permute-start | bytes 3244040 | tf_op jit(solution)/shard_map/ppermute | solution.py:234
  45.2 5.2 %collective-permute-start.8 = (bf16[128,4224]{1,0:T(8,128)(2,1)}, bf16[128,4224]{1,0:T(8,128)(2,1)S(1)}, u32[]{:S(2)}, u32[]{:S(2)}) collective-permute-start(bf16[128,4224]{1,0:T(8,128)(2,1)} %collective-permute-done.4.refs_0_.refs_5_.refs_9_.refs_3_), channel_id=1, source_target_pairs={{0,1},{1,0},{2,3},{3,2},{4,5},{5,4},{6,7},{7,6},{8,9},{9,8},{10,11... | collective-permute-start | bytes 3244040 | tf_op jit(solution)/shard_map/ppermute | solution.py:234
  45.7 5.5 %collective-permute-start.9 = (bf16[128,4224]{1,0:T(8,128)(2,1)}, bf16[128,4224]{1,0:T(8,128)(2,1)S(1)}, u32[]{:S(2)}, u32[]{:S(2)}) collective-permute-start(bf16[128,4224]{1,0:T(8,128)(2,1)} %collective-permute-done.5.refs_1_.refs_6_.refs_10_.refs_4_), channel_id=1, source_target_pairs={{0,1},{1,0},{2,3},{3,2},{4,5},{5,4},{6,7},{7,6},{8,9},{9,8},{10,11... | collective-permute-start | bytes 3244040 | tf_op jit(solution)/shard_map/ppermute | solution.py:234
  58.9 13.0 %collective-permute-start.11 = (bf16[3,128,768]{2,1,0:T(8,128)(2,1)S(1)}, bf16[3,128,768]{2,1,0:T(8,128)(2,1)S(1)}, u32[]{:S(2)}, u32[]{:S(2)}) collective-permute-start(bf16[3,128,768]{2,1,0:T(8,128)(2,1)S(1)} %bitcast.47), channel_id=1, source_target_pairs={{0,32},{1,97},{32,64},{33,1},{64,96},{65,33},{96,0},{97,65},{2,34}... | collective-permute-start | bytes 1769480 | tf_op jit(solution)/shard_map/ppermute | solution.py:253
  60.5 19.0 %collective-permute-start.10 = (bf16[3,128,768]{2,1,0:T(8,128)(2,1)S(1)}, bf16[3,128,768]{2,1,0:T(8,128)(2,1)S(1)}, u32[]{:S(2)}, u32[]{:S(2)}) collective-permute-start(bf16[3,128,768]{2,1,0:T(8,128)(2,1)S(1)} %bitcast.46), channel_id=1, source_target_pairs={{0,32},{1,97},{32,64},{33,1},{64,96},{65,33},{96,0},{97,65},{2,34}... | collective-permute-start | bytes 1769480 | tf_op jit(solution)/shard_map/ppermute | solution.py:253
  70.6 15.6 %collective-permute-start.13 = (bf16[256,2176]{1,0:T(8,128)(2,1)S(1)}, bf16[256,2176]{1,0:T(8,128)(2,1)S(1)}, u32[]{:S(2)}, u32[]{:S(2)}) collective-permute-start(bf16[256,2176]{1,0:T(8,128)(2,1)S(1)} %get-tuple-element.51), channel_id=1, source_target_pairs={{0,8},{1,25},{8,0},{9,17},{16,24},{17,9},{24,16},{25,1},{2,10},{3,... | collective-permute-start | bytes 3342344 | tf_op jit(solution)/shard_map/ppermute | solution.py:276
  72.0 11.2 %collective-permute-start.12 = (bf16[3,128,768]{2,1,0:T(8,128)(2,1)S(1)}, bf16[3,128,768]{2,1,0:T(8,128)(2,1)S(1)}, u32[]{:S(2)}, u32[]{:S(2)}) collective-permute-start(bf16[3,128,768]{2,1,0:T(8,128)(2,1)S(1)} %fusion.5), channel_id=1, source_target_pairs={{0,32},{1,97},{32,64},{33,1},{64,96},{65,33},{96,0},{97,65},{2,34}... | collective-permute-start | bytes 1769480 | tf_op jit(solution)/shard_map/ppermute | solution.py:253
  78.5 1.0 copy-start.2
  79.5 4.6 %copy-start = (bf16[2,3,128,768]{3,2,1,0:T(8,128)(2,1)}, bf16[2,3,128,768]{3,2,1,0:T(8,128)(2,1)S(1)}, u32[]{:S(2)}) copy-start(bf16[2,3,128,768]{3,2,1,0:T(8,128)(2,1)S(1)} %get-tuple-element.49) | copy-start | bytes 3538948
  79.7 11.3 %collective-permute-start.18 = (bf16[3,128,768]{2,1,0:T(8,128)(2,1)S(1)}, bf16[3,128,768]{2,1,0:T(8,128)(2,1)}, u32[]{:S(2)}, u32[]{:S(2)}) collective-permute-start(bf16[3,128,768]{2,1,0:T(8,128)(2,1)S(1)} %fusion.1), channel_id=1, source_target_pairs={{0,32},{1,97},{32,64},{33,1},{64,96},{65,33},{96,0},{97,65},{2,34}... | collective-permute-start | bytes 1769480 | tf_op jit(solution)/shard_map/ppermute | solution.py:253
  86.2 4.8 %copy-start.3 = (bf16[2,3,128,768]{3,2,1,0:T(8,128)(2,1)S(1)}, bf16[2,3,128,768]{3,2,1,0:T(8,128)(2,1)}, u32[]{:S(2)}) copy-start(bf16[2,3,128,768]{3,2,1,0:T(8,128)(2,1)} %copy-done.2) | copy-start | bytes 3538948
  86.4 4.5 %copy-start.4 = (bf16[256,2176]{1,0:T(8,128)(2,1)}, bf16[256,2176]{1,0:T(8,128)(2,1)S(1)}, u32[]{:S(2)}) copy-start(bf16[256,2176]{1,0:T(8,128)(2,1)S(1)} %add_convert_fusion) | copy-start | bytes 3342340
  87.3 5.7 %collective-permute-start.14 = (bf16[128,2176]{1,0:T(8,128)(2,1)}, bf16[128,2176]{1,0:T(8,128)(2,1)}, u32[]{:S(2)}, u32[]{:S(2)}) collective-permute-start(bf16[128,2176]{1,0:T(8,128)(2,1)} %slice.54), channel_id=1, source_target_pairs={{0,1},{1,0},{2,3},{3,2},{4,5},{5,4},{6,7},{7,6},{8,9},{9,8},{10,11... | collective-permute-start | bytes 1671176 | tf_op jit(solution)/shard_map/ppermute | solution.py:280
  88.0 11.3 %collective-permute-start.20 = (bf16[3,128,768]{2,1,0:T(8,128)(2,1)}, bf16[3,128,768]{2,1,0:T(8,128)(2,1)S(1)}, u32[]{:S(2)}, u32[]{:S(2)}) collective-permute-start(bf16[3,128,768]{2,1,0:T(8,128)(2,1)} %fusion.4), channel_id=1, source_target_pairs={{0,32},{1,97},{32,64},{33,1},{64,96},{65,33},{96,0},{97,65},{2,34}... | collective-permute-start | bytes 1769480 | tf_op jit(solution)/shard_map/ppermute | solution.py:253
  93.0 6.3 %copy-start.1 = (bf16[2,3,128,768]{3,2,1,0:T(8,128)(2,1)S(1)}, bf16[2,3,128,768]{3,2,1,0:T(8,128)(2,1)}, u32[]{:S(2)}) copy-start(bf16[2,3,128,768]{3,2,1,0:T(8,128)(2,1)} %copy-done) | copy-start | bytes 3538948
  93.0 13.3 %collective-permute-start.19 = (bf16[3,128,768]{2,1,0:T(8,128)(2,1)}, bf16[3,128,768]{2,1,0:T(8,128)(2,1)}, u32[]{:S(2)}, u32[]{:S(2)}) collective-permute-start(bf16[3,128,768]{2,1,0:T(8,128)(2,1)} %fusion.2), channel_id=1, source_target_pairs={{0,32},{1,97},{32,64},{33,1},{64,96},{65,33},{96,0},{97,65},{2,34}... | collective-permute-start | bytes 1769480 | tf_op jit(solution)/shard_map/ppermute | solution.py:253
  94.5 7.0 %collective-permute-start.17 = (bf16[32,2176]{1,0:T(8,128)(2,1)S(1)}, bf16[32,2176]{1,0:T(8,128)(2,1)S(1)}, u32[]{:S(2)}, u32[]{:S(2)}) collective-permute-start(bf16[32,2176]{1,0:T(8,128)(2,1)S(1)} %get-tuple-element.66), channel_id=1, source_target_pairs={{0,4},{2,6},{4,0},{6,2},{1,5},{3,7},{5,1},{7,3},{8,12},{10,14},{12... | collective-permute-start | bytes 417800 | tf_op jit(solution)/shard_map/ppermute | solution.py:284
  96.6 7.8 %collective-permute-start.16 = (bf16[32,2176]{1,0:T(8,128)(2,1)S(1)}, bf16[32,2176]{1,0:T(8,128)(2,1)S(1)}, u32[]{:S(2)}, u32[]{:S(2)}) collective-permute-start(bf16[32,2176]{1,0:T(8,128)(2,1)S(1)} %get-tuple-element.67), channel_id=1, source_target_pairs={{0,6},{2,4},{4,2},{6,0},{1,7},{3,5},{5,3},{7,1},{8,14},{10,12},{12... | collective-permute-start | bytes 417800 | tf_op jit(solution)/shard_map/ppermute | solution.py:284
  97.2 7.5 %collective-permute-start.15 = (bf16[32,2176]{1,0:T(8,128)(2,1)S(1)}, bf16[32,2176]{1,0:T(8,128)(2,1)S(1)}, u32[]{:S(2)}, u32[]{:S(2)}) collective-permute-start(bf16[32,2176]{1,0:T(8,128)(2,1)S(1)} %get-tuple-element.65), channel_id=1, source_target_pairs={{0,2},{2,0},{4,6},{6,4},{1,3},{3,1},{5,7},{7,5},{8,10},{10,8},{12,... | collective-permute-start | bytes 417800 | tf_op jit(solution)/shard_map/ppermute | solution.py:284
  100.2 10.2 %collective-permute-start.21 = (bf16[3,128,768]{2,1,0:T(8,128)(2,1)}, bf16[3,128,768]{2,1,0:T(8,128)(2,1)}, u32[]{:S(2)}, u32[]{:S(2)}) collective-permute-start(bf16[3,128,768]{2,1,0:T(8,128)(2,1)} %fusion), channel_id=1, source_target_pairs={{0,8},{1,25},{8,0},{9,17},{16,24},{17,9},{24,16},{25,1},{2,10},{3,... | collective-permute-start | bytes 1769480 | tf_op jit(solution)/shard_map/ppermute | solution.py:289

commit v6 on v5

--- a/solution.py
+++ b/solution.py
@@ -35,6 +35,12 @@
 SWAP = [(0, 1), (1, 0)]
 Z_MOVE = [[(j, j ^ k) for j in range(SIDE)] for k in Z_ORDER]
 X_PAIR = [(x * 2 + c, (x ^ PAIR[c]) * 2 + c) for x in range(SIDE) for c in range(2)]
+LAST = [
+    ((y * SIDE + x) * 2 + c, (((y + 1 - 2 * c) % SIDE) * SIDE + (x ^ PAIR[c])) * 2 + c)
+    for y in range(SIDE)
+    for x in range(SIDE)
+    for c in range(2)
+]
 RING = [(y * 2 + c, ((y + 1 - 2 * c) % SIDE) * 2 + c) for y in range(SIDE) for c in range(2)]
 
 
@@ -201,8 +207,8 @@
     lane = lax.broadcasted_iota(jnp.int32, (1, LANES), 1)
     sel = (lane == (z * 2 + core) * 2 + expert).astype(F32)
 
-    hot = routes[:, :, None] == lax.broadcasted_iota(jnp.int32, (1, 1, LANES), 2)
-    dense = jnp.sum(jnp.where(hot, probs.astype(F32)[:, :, None], 0.0), axis=1).astype(BF16)
+    hot = routes.T[:, None, :] == lax.broadcasted_iota(jnp.int32, (1, LANES, 1), 1)
+    dense = jnp.sum(jnp.where(hot, probs.T.astype(F32)[:, None, :], 0.0), axis=0).astype(BF16).T
     row = jnp.concatenate([layer_input, out_grad, dense], axis=1)
 
     axes = ("x", "z", "core")
@@ -283,10 +289,11 @@
     for n in range(3):
         total = total + lax.ppermute(part[n + 1], "z", Z_MOVE[n]).astype(F32)
     grad_input = total[:, :width].astype(BF16)
-    grad_prob = jnp.sum(jnp.where(hot, total[:, None, width:], 0.0), axis=2)
-
-    other, own = ring(other), ring(add(rest[1][0], own))
-    other = lax.ppermute(add(rest[0][1], other), ("x", "core"), X_PAIR)
+    grad_prob = jnp.sum(jnp.where(hot, total[:, width:].T[None], 0.0), axis=1).T
+
+    home = lax.ppermute(rest[0][1], ("x", "core"), X_PAIR)
+    other, own = lax.ppermute(other, ("y", "x", "core"), LAST), ring(add(rest[1][0], own))
+    other = add(home, other)
     own = add(rest[1][1], own)
     even, odd = jnp.where(expert == 0, own, other), jnp.where(expert == 0, other, own)
     grad_weights = jnp.transpose(jnp.stack([even, odd], axis=0), (2, 1, 0, 3))

time: 115 us -> 115 us (level)
  waiting for transfers between devices: 21.6 us -> 23.2 us
  other arithmetic: 9 us -> 7.79 us
  local copies, waits for them, and re-layouts: 25.1 us -> 23.9 us
    ppermute x1 -> x2, waiting for transfers between devices: 4.17 us -> 8.58 us  [the longest x1 6.79 us: shards(): lax.ppermute(other, ('y', 'x', 'core'), LAST)]
    ppermute x3, waiting for transfers between devices: 3.85 us -> 0.01 us  [shards(): total = total + lax.ppermute(part[n + 1], 'z', Z_MOVE[n]).astype(F32)]
    convert_element_type x7 -> x6, other arithmetic: 5.9 us -> 3.89 us  [add(): return total.astype(BF16)]
    ppermute x1 -> x2, starting transfers between devices: 0.59 us -> 2.43 us  [the longest x1 1.76 us: shards(): lax.ppermute(other, ('y', 'x', 'core'), LAST)]
    reduce_sum x2, other arithmetic: 0.32 us -> 1.59 us  [the longest x1 0.82 us: shards(): jnp.sum(jnp.where(hot, probs.T.astype(F32)[:, None, :], 0.0), axis=0)]
    ppermute x6 -> x5, waiting for transfers between devices: 6.58 us -> 7.55 us  [shards(): ring = lambda rows: lax.ppermute(rows, ('y', 'core'), RING)]
    ppermute x6 -> x5, starting transfers between devices: 5.75 us -> 4.94 us  [shards(): ring = lambda rows: lax.ppermute(rows, ('y', 'core'), RING)]
    unnamed x19 -> x21, local copies, waits for them, and re-layouts: 22.7 us -> 22.2 us
  transfers between devices with their start and end apart: 22 -> 22, of which waited for: 12 -> 9; matrix products, arithmetic and copies ran while one was open for 23% -> 22% of each run, Pallas kernels for 24% -> 24%
where the time goes in v6:
time: 115 us; the launch traced here: 114 us
  Pallas kernels  35.1 us (31%)
  local copies, waits for them, and re-layouts  23.9 us (21%)
  starting transfers between devices  23.4 us (20%)
  waiting for transfers between devices  23.2 us (20%)
  other arithmetic  7.79 us (7%)
    pallas_call x6, Pallas kernels, on_chip(): pl.pallas_call(kernel, name=name, in_specs=[pl.BlockSpec(memory_space=plt...  35.1 us
    unnamed x21, local copies, waits for them, and re-layouts  22.2 us
    ppermute x5, waiting for transfers between devices, shards(): ring = lambda rows: lax.ppermute(rows, ('y', 'core'), RING)  7.55 us
    ppermute x1, waiting for transfers between devices, shards(): lax.ppermute(other, ('y', 'x', 'core'), LAST)  6.79 us
    ppermute x3, starting transfers between devices, shards(): lax.ppermute(line, axes, plane(n, False))  5.35 us
    ppermute x5, starting transfers between devices, shards(): ring = lambda rows: lax.ppermute(rows, ('y', 'core'), RING)  4.94 us
    ppermute x3, starting transfers between devices, shards(): line = [row] + [lax.ppermute(row, axes, plane(n, True)) for n in range(3)]  4.33 us
    convert_element_type x6, other arithmetic, add(): return total.astype(BF16)  3.89 us
  transfers between devices with their start and end apart: 22, of which 9 were waited for; matrix products, arithmetic and copies ran while one was open for 22% of the time, Pallas kernels for 24%

profile of v6, /device:TPU:0, one launch (start us, length us, event | category | flops | bytes accessed | tf_op | source)
XLA Modules:
  0.0 114.2 jit_solution(7067793797566391080)
XLA Ops:
  2.1 1.0 pad_maximum_fusion.1
  3.2 3.2 %collective-permute-start.2 = (bf16[32,4224]{1,0:T(8,128)(2,1)S(1)}, bf16[32,4224]{1,0:T(8,128)(2,1)S(1)}, u32[]{:S(2)}, u32[]{:S(2)}) collective-permute-start(bf16[32,4224]{1,0:T(8,128)(2,1)S(1)} %pad_maximum_fusion.1), channel_id=1, source_target_pairs={{0,16},{1,5},{2,18},{3,7},{4,20},{5,1},{6,22},{7,3},{8,24},{9,13},... | collective-permute-start | bytes 811016 | tf_op jit(solution)/shard_map/ppermute | solution.py:216
  6.3 1.1 collective-permute-start.1
  7.5 6.2 %copy.19 = bf16[2048,2,768]{2,0,1:T(8,128)(2,1)} copy(bf16[2048,2,768]{2,1,0:T(2,128)(2,1)} %param.11) | data formatting | bytes 12582912 | tf_op args[5]
  14.4 2.0 %collective-permute-start.3 = (bf16[128,4224]{1,0:T(8,128)(2,1)S(1)}, bf16[128,4224]{1,0:T(8,128)(2,1)S(1)}, u32[]{:S(2)}, u32[]{:S(2)}) collective-permute-start(bf16[128,4224]{1,0:T(8,128)(2,1)S(1)} %pad_maximum_fusion.refs_0_.refs_2_.refs_6_), channel_id=1, source_target_pairs={{0,2},{1,25},{2,0},{3,27},{4,6},{5,29},{6,4},{7,31},{8,10},{9,17},... | collective-permute-start | bytes 3244040 | tf_op jit(solution)/shard_map/ppermute | solution.py:219
  16.9 2.9 %collective-permute-start.4 = (bf16[128,4224]{1,0:T(8,128)(2,1)S(1)}, bf16[128,4224]{1,0:T(8,128)(2,1)}, u32[]{:S(2)}, u32[]{:S(2)}) collective-permute-start(bf16[128,4224]{1,0:T(8,128)(2,1)S(1)} %pad_maximum_fusion.refs_0_.refs_2_.refs_6_), channel_id=1, source_target_pairs={{0,6},{1,9},{2,4},{3,11},{4,2},{5,13},{6,0},{7,15},{8,14},{9,1},{1... | collective-permute-start | bytes 3244040 | tf_op jit(solution)/shard_map/ppermute | solution.py:219
  20.3 11.8 %copy.18 = bf16[2048,2,2,768]{3,0,2,1:T(8,128)(2,1)} copy(bf16[2048,2,2,768]{3,2,1,0:T(2,128)(2,1)} %param.10) | data formatting | bytes 25165824 | tf_op args[4]
  32.2 4.3 %hold.1.weights_ref = bf16[3,2048,768]{2,1,0:T(8,128)(2,1)S(1)} custom-call(s32[10]{0:T(128)S(1)} %stack.52.place_ref, bf16[2,2,2048,768]{3,2,1,0:T(8,128)(2,1)} %bitcast.56, bf16[2,2048,768]{2,1,0:T(8,128)(2,1)} %bitcast.57), custom_call_target="tpu_custom_call" | custom-call | flops 1048576 | bytes 65536 | tf_op jit(solution)/shard_map/hold/pallas_call | solution.py:134
  36.5 4.9 %forward.1 = (bf16[3,384,768]{2,1,0:T(8,128)(2,1)S(1)}, f32[384,128]{1,0:T(8,128)S(1)}) custom-call(s32[10]{0:T(128)S(1)} %stack.52.place_ref, f32[1,128]{1,0:T(1,128)S(1)} %compare_convert_fusion.sel_ref, bf16[3,2048,768]{2,1,0:T(8,128)(2,1)S(1)} %hold.1.weights_ref, bf16[128,4224]{1,0:T(8,128)(2,1)S(1)} %pad_maximum_fusion.refs_0_.refs_2_.refs_6_, ...), custom_call_target="tpu_custom_call" | custom-call | flops 1048576 | bytes 65536 | tf_op jit(solution)/shard_map/forward/pallas_call | solution.py:134
  41.4 3.6 %collective-permute-done.4.refs_0_.refs_5_.refs_9_.refs_3_ = bf16[128,4224]{1,0:T(8,128)(2,1)} collective-permute-done((bf16[128,4224]{1,0:T(8,128)(2,1)S(1)}, bf16[128,4224]{1,0:T(8,128)(2,1)}, u32[]{:S(2)}, u32[]{:S(2)}) %collective-permute-start.4) | collective-permute-done | bytes 1081376 | tf_op jit(solution)/shard_map/ppermute | solution.py:219
  45.5 4.6 %forward_mine.1 = (bf16[3,256,768]{2,1,0:T(8,128)(2,1)S(1)}, f32[256,128]{1,0:T(8,128)S(1)}) custom-call(s32[10]{0:T(128)S(1)} %stack.52.place_ref, f32[1,128]{1,0:T(1,128)S(1)} %compare_convert_fusion.sel_ref, bf16[3,2048,768]{2,1,0:T(8,128)(2,1)S(1)} %hold.1.weights_ref, bf16[128,4224]{1,0:T(8,128)(2,1)} %collective-permute-done.4.refs_0_.refs_5_.refs_9_.refs_3_, ...), custom_call_target="tpu_custom_call" | custom-call | flops 1048576 | bytes 65536 | tf_op jit(solution)/shard_map/forward_mine/pallas_call | solution.py:134
  51.0 7.7 %forward_and_first.1 = (bf16[3,384,768]{2,1,0:T(8,128)(2,1)S(1)}, f32[384,128]{1,0:T(8,128)S(1)}, bf16[1,3,128,768]{3,2,1,0:T(8,128)(2,1)S(1)}, bf16[1,3,128,768]{3,2,1,0:T(8,128)(2,1)S(1)}) custom-call(s32[10]{0:T(128)S(1)} %stack.52.place_ref, f32[1,128]{1,0:T(1,128)S(1)} %compare_convert_fusion.sel_ref, bf16[3,2048,768]{2,1,0:T(8,128)(2,1)S(1)} %hold.1.weights_ref, ...), custom_call_target="tpu_custom_call" | custom-call | flops 1048576 | bytes 65536 | tf_op jit(solution)/shard_map/forward_and_first/pallas_call | solution.py:134
  58.7 1.6 %collective-permute-start.11 = (bf16[3,128,768]{2,1,0:T(8,128)(2,1)S(1)}, bf16[3,128,768]{2,1,0:T(8,128)(2,1)S(1)}, u32[]{:S(2)}, u32[]{:S(2)}) collective-permute-start(bf16[3,128,768]{2,1,0:T(8,128)(2,1)S(1)} %bitcast.55), channel_id=1, source_target_pairs={{0,32},{1,97},{32,64},{33,1},{64,96},{65,33},{96,0},{97,65},{2,34}... | collective-permute-start | bytes 1769480 | tf_op jit(solution)/shard_map/ppermute | solution.py:259
  60.3 1.6 %collective-permute-start.10 = (bf16[3,128,768]{2,1,0:T(8,128)(2,1)S(1)}, bf16[3,128,768]{2,1,0:T(8,128)(2,1)S(1)}, u32[]{:S(2)}, u32[]{:S(2)}) collective-permute-start(bf16[3,128,768]{2,1,0:T(8,128)(2,1)S(1)} %bitcast.54), channel_id=1, source_target_pairs={{0,32},{1,97},{32,64},{33,1},{64,96},{65,33},{96,0},{97,65},{2,34}... | collective-permute-start | bytes 1769480 | tf_op jit(solution)/shard_map/ppermute | solution.py:259
  61.9 8.5 %second_and_slots.1 = (bf16[1,3,128,768]{3,2,1,0:T(8,128)(2,1)S(1)}, bf16[1,3,128,768]{3,2,1,0:T(8,128)(2,1)S(1)}, bf16[256,2176]{1,0:T(8,128)(2,1)S(1)}, bf16[256,2176]{1,0:T(8,128)(2,1)S(1)}) custom-call(s32[10]{0:T(128)S(1)} %stack.52.place_ref, f32[1,128]{1,0:T(1,128)S(1)} %compare_convert_fusion.sel_ref, bf16[3,2048,768]{2,1,0:T(8,128)(2,1)S(1)} %hold.1.weights_ref, ...), custom_call_target="tpu_custom_call" | custom-call | flops 1048576 | bytes 65536 | tf_op jit(solution)/shard_map/second_and_slots/pallas_call | solution.py:134
  70.4 1.3 %collective-permute-start.13 = (bf16[256,2176]{1,0:T(8,128)(2,1)S(1)}, bf16[256,2176]{1,0:T(8,128)(2,1)S(1)}, u32[]{:S(2)}, u32[]{:S(2)}) collective-permute-start(bf16[256,2176]{1,0:T(8,128)(2,1)S(1)} %get-tuple-element.51), channel_id=1, source_target_pairs={{0,8},{1,25},{8,0},{9,17},{16,24},{17,9},{24,16},{25,1},{2,10},{3,... | collective-permute-start | bytes 3342344 | tf_op jit(solution)/shard_map/ppermute | solution.py:282
  71.9 1.4 %collective-permute-start.12 = (bf16[3,128,768]{2,1,0:T(8,128)(2,1)S(1)}, bf16[3,128,768]{2,1,0:T(8,128)(2,1)S(1)}, u32[]{:S(2)}, u32[]{:S(2)}) collective-permute-start(bf16[3,128,768]{2,1,0:T(8,128)(2,1)S(1)} %fusion.4), channel_id=1, source_target_pairs={{0,32},{1,97},{32,64},{33,1},{64,96},{65,33},{96,0},{97,65},{2,34}... | collective-permute-start | bytes 1769480 | tf_op jit(solution)/shard_map/ppermute | solution.py:259
  73.2 5.1 %weight_terms.1 = (bf16[2,3,128,768]{3,2,1,0:T(8,128)(2,1)S(1)}, bf16[2,3,128,768]{3,2,1,0:T(8,128)(2,1)S(1)}) custom-call(s32[10]{0:T(128)S(1)} %stack.52.place_ref, bf16[128,4224]{1,0:T(8,128)(2,1)S(1)} %pad_maximum_fusion.refs_0_.refs_2_.refs_6_, bf16[128,4224]{1,0:T(8,128)(2,1)S(1)} %collective-permute-done.6.refs_1_.refs_3_.refs_7_, ...), custom_call_target="tpu_custom_call" | custom-call | flops 1048576 | bytes 65536 | tf_op jit(solution)/shard_map/weight_terms/pallas_call | solution.py:134
  78.3 1.0 copy-done.2
  79.8 3.3 %collective-permute-done.12 = bf16[3,128,768]{2,1,0:T(8,128)(2,1)S(1)} collective-permute-done((bf16[3,128,768]{2,1,0:T(8,128)(2,1)S(1)}, bf16[3,128,768]{2,1,0:T(8,128)(2,1)S(1)}, u32[]{:S(2)}, u32[]{:S(2)}) %collective-permute-start.12) | collective-permute-done | bytes 589856 | tf_op jit(solution)/shard_map/ppermute | solution.py:259
  83.0 1.0 fusion.3
  84.0 2.0 %collective-permute-done.13 = bf16[256,2176]{1,0:T(8,128)(2,1)S(1)} collective-permute-done((bf16[256,2176]{1,0:T(8,128)(2,1)S(1)}, bf16[256,2176]{1,0:T(8,128)(2,1)S(1)}, u32[]{:S(2)}, u32[]{:S(2)}) %collective-permute-start.13) | collective-permute-done | bytes 1114144 | tf_op jit(solution)/shard_map/ppermute | solution.py:282
  86.3 1.0 copy-done.4
  87.3 0.8 slice.54
  89.5 1.8 %collective-permute-start.21 = (bf16[3,128,768]{2,1,0:T(8,128)(2,1)}, bf16[3,128,768]{2,1,0:T(8,128)(2,1)S(1)}, u32[]{:S(2)}, u32[]{:S(2)}) collective-permute-start(bf16[3,128,768]{2,1,0:T(8,128)(2,1)} %fusion.3), channel_id=1, source_target_pairs={{0,40},{1,121},{8,32},{9,113},{16,56},{17,105},{24,48},{25,97},{32... | collective-permute-start | bytes 1769480 | tf_op jit(solution)/shard_map/ppermute | solution.py:295
  91.3 1.2 %fusion.1 = bf16[3,128,768]{2,1,0:T(8,128)(2,1)S(1)} fusion(bf16[3,128,768]{2,1,0:T(8,128)(2,1)} %collective-permute-done.18, bf16[2,3,128,768]{3,2,1,0:T(8,128)(2,1)S(1)} %copy-done.3), kind=kLoop, calls=%fused_computation.7 | loop fusion | flops 1179648 | bytes 1769472 | tf_op jit(solution)/shard_map/convert_element_type | solution.py:199
  92.6 1.2 %add_convert_fusion.2 = bf16[128,2176]{1,0:T(8,128)(2,1)S(1)} fusion(bf16[128,2176]{1,0:T(8,128)(2,1)} %collective-permute-done.14, bf16[256,2176]{1,0:T(8,128)(2,1)S(1)} %copy-done.5), kind=kLoop, calls=%fused_computation.15 | loop fusion | flops 1114112 | bytes 1671168 | tf_op jit(solution)/shard_map/convert_element_type | solution.py:199
  93.8 3.2 %collective-permute-start.17 = (bf16[32,2176]{1,0:T(8,128)(2,1)S(1)}, bf16[32,2176]{1,0:T(8,128)(2,1)S(1)}, u32[]{:S(2)}, u32[]{:S(2)}) collective-permute-start(bf16[32,2176]{1,0:T(8,128)(2,1)S(1)} %get-tuple-element.66), channel_id=1, source_target_pairs={{0,4},{2,6},{4,0},{6,2},{1,5},{3,7},{5,1},{7,3},{8,12},{10,14},{12... | collective-permute-start | bytes 417800 | tf_op jit(solution)/shard_map/ppermute | solution.py:290
  97.0 1.8 %collective-permute-done.20 = bf16[3,128,768]{2,1,0:T(8,128)(2,1)S(1)} collective-permute-done((bf16[3,128,768]{2,1,0:T(8,128)(2,1)S(1)}, bf16[3,128,768]{2,1,0:T(8,128)(2,1)S(1)}, u32[]{:S(2)}, u32[]{:S(2)}) %collective-permute-start.20) | collective-permute-done | bytes 589856 | tf_op jit(solution)/shard_map/ppermute | solution.py:294
  98.9 6.8 %collective-permute-done.21 = bf16[3,128,768]{2,1,0:T(8,128)(2,1)S(1)} collective-permute-done((bf16[3,128,768]{2,1,0:T(8,128)(2,1)}, bf16[3,128,768]{2,1,0:T(8,128)(2,1)S(1)}, u32[]{:S(2)}, u32[]{:S(2)}) %collective-permute-start.21) | collective-permute-done | bytes 589856 | tf_op jit(solution)/shard_map/ppermute | solution.py:295
  105.7 4.3 %collective-permute-done.19 = bf16[3,128,768]{2,1,0:T(8,128)(2,1)S(1)} collective-permute-done((bf16[3,128,768]{2,1,0:T(8,128)(2,1)S(1)}, bf16[3,128,768]{2,1,0:T(8,128)(2,1)S(1)}, u32[]{:S(2)}, u32[]{:S(2)}) %collective-permute-start.19) | collective-permute-done | bytes 589856 | tf_op jit(solution)/shard_map/ppermute | solution.py:259
  110.5 2.2 %copy.15 = bf16[128,3,2,768]{3,2,1,0:T(2,128)(2,1)} copy(bf16[128,3,2,768]{3,0,1,2:T(8,128)(2,1)S(1)} %maximum_bitcast_fusion) | data formatting | bytes 2359296
  (60 shorter events, 9.1 us)
Async XLA Ops:
  3.1 11.2 %copy-start.6 = (bf16[32,2048]{1,0:T(8,128)(2,1)S(1)}, bf16[32,2048]{1,0:T(8,128)(2,1)}, u32[]{:S(2)}) copy-start(bf16[32,2048]{1,0:T(8,128)(2,1)} %param.7) | copy-start | bytes 393220
  3.1 11.2 %copy-start.7 = (bf16[32,2048]{1,0:T(8,128)(2,1)S(1)}, bf16[32,2048]{1,0:T(8,128)(2,1)}, u32[]{:S(2)}) copy-start(bf16[32,2048]{1,0:T(8,128)(2,1)} %param.6) | copy-start | bytes 393220
  3.2 10.5 %collective-permute-start.2 = (bf16[32,4224]{1,0:T(8,128)(2,1)S(1)}, bf16[32,4224]{1,0:T(8,128)(2,1)S(1)}, u32[]{:S(2)}, u32[]{:S(2)}) collective-permute-start(bf16[32,4224]{1,0:T(8,128)(2,1)S(1)} %pad_maximum_fusion.1), channel_id=1, source_target_pairs={{0,16},{1,5},{2,18},{3,7},{4,20},{5,1},{6,22},{7,3},{8,24},{9,13},... | collective-permute-start | bytes 811016 | tf_op jit(solution)/shard_map/ppermute | solution.py:216
  6.3 7.8 %collective-permute-start.1 = (bf16[32,4224]{1,0:T(8,128)(2,1)S(1)}, bf16[32,4224]{1,0:T(8,128)(2,1)S(1)}, u32[]{:S(2)}, u32[]{:S(2)}) collective-permute-start(bf16[32,4224]{1,0:T(8,128)(2,1)S(1)} %pad_maximum_fusion.1), channel_id=1, source_target_pairs={{0,24},{1,7},{2,26},{3,5},{4,28},{5,3},{6,30},{7,1},{8,16},{9,15},... | collective-permute-start | bytes 811016 | tf_op jit(solution)/shard_map/ppermute | solution.py:216
  7.5 6.8 %collective-permute-start = (bf16[32,4224]{1,0:T(8,128)(2,1)S(1)}, bf16[32,4224]{1,0:T(8,128)(2,1)S(1)}, u32[]{:S(2)}, u32[]{:S(2)}) collective-permute-start(bf16[32,4224]{1,0:T(8,128)(2,1)S(1)} %pad_maximum_fusion.1), channel_id=1, source_target_pairs={{0,8},{1,3},{2,10},{3,1},{4,12},{5,7},{6,14},{7,5},{8,0},{9,11},{1... | collective-permute-start | bytes 811016 | tf_op jit(solution)/shard_map/ppermute | solution.py:216
  14.4 22.1 %collective-permute-start.3 = (bf16[128,4224]{1,0:T(8,128)(2,1)S(1)}, bf16[128,4224]{1,0:T(8,128)(2,1)S(1)}, u32[]{:S(2)}, u32[]{:S(2)}) collective-permute-start(bf16[128,4224]{1,0:T(8,128)(2,1)S(1)} %pad_maximum_fusion.refs_0_.refs_2_.refs_6_), channel_id=1, source_target_pairs={{0,2},{1,25},{2,0},{3,27},{4,6},{5,29},{6,4},{7,31},{8,10},{9,17},... | collective-permute-start | bytes 3244040 | tf_op jit(solution)/shard_map/ppermute | solution.py:219
  16.4 20.1 %collective-permute-start.6 = (bf16[128,4224]{1,0:T(8,128)(2,1)S(1)}, bf16[128,4224]{1,0:T(8,128)(2,1)S(1)}, u32[]{:S(2)}, u32[]{:S(2)}) collective-permute-start(bf16[128,4224]{1,0:T(8,128)(2,1)S(1)} %pad_maximum_fusion.refs_0_.refs_2_.refs_6_), channel_id=1, source_target_pairs={{0,1},{1,0},{2,3},{3,2},{4,5},{5,4},{6,7},{7,6},{8,9},{9,8},{10,11... | collective-permute-start | bytes 3244040 | tf_op jit(solution)/shard_map/ppermute | solution.py:240
  16.9 28.1 %collective-permute-start.4 = (bf16[128,4224]{1,0:T(8,128)(2,1)S(1)}, bf16[128,4224]{1,0:T(8,128)(2,1)}, u32[]{:S(2)}, u32[]{:S(2)}) collective-permute-start(bf16[128,4224]{1,0:T(8,128)(2,1)S(1)} %pad_maximum_fusion.refs_0_.refs_2_.refs_6_), channel_id=1, source_target_pairs={{0,6},{1,9},{2,4},{3,11},{4,2},{5,13},{6,0},{7,15},{8,14},{9,1},{1... | collective-permute-start | bytes 3244040 | tf_op jit(solution)/shard_map/ppermute | solution.py:219
  19.8 25.2 %collective-permute-start.5 = (bf16[128,4224]{1,0:T(8,128)(2,1)S(1)}, bf16[128,4224]{1,0:T(8,128)(2,1)}, u32[]{:S(2)}, u32[]{:S(2)}) collective-permute-start(bf16[128,4224]{1,0:T(8,128)(2,1)S(1)} %pad_maximum_fusion.refs_0_.refs_2_.refs_6_), channel_id=1, source_target_pairs={{0,4},{1,17},{2,6},{3,19},{4,0},{5,21},{6,2},{7,23},{8,12},{9,25},... | collective-permute-start | bytes 3244040 | tf_op jit(solution)/shard_map/ppermute | solution.py:219
  45.0 5.2 %collective-permute-start.7 = (bf16[128,4224]{1,0:T(8,128)(2,1)S(1)}, bf16[128,4224]{1,0:T(8,128)(2,1)S(1)}, u32[]{:S(2)}, u32[]{:S(2)}) collective-permute-start(bf16[128,4224]{1,0:T(8,128)(2,1)S(1)} %collective-permute-done.3.refs_2_.refs_4_.refs_8_), channel_id=1, source_target_pairs={{0,1},{1,0},{2,3},{3,2},{4,5},{5,4},{6,7},{7,6},{8,9},{9,8},{10,11... | collective-permute-start | bytes 3244040 | tf_op jit(solution)/shard_map/ppermute | solution.py:240
  45.0 5.2 %collective-permute-start.8 = (bf16[128,4224]{1,0:T(8,128)(2,1)}, bf16[128,4224]{1,0:T(8,128)(2,1)S(1)}, u32[]{:S(2)}, u32[]{:S(2)}) collective-permute-start(bf16[128,4224]{1,0:T(8,128)(2,1)} %collective-permute-done.4.refs_0_.refs_5_.refs_9_.refs_3_), channel_id=1, source_target_pairs={{0,1},{1,0},{2,3},{3,2},{4,5},{5,4},{6,7},{7,6},{8,9},{9,8},{10,11... | collective-permute-start | bytes 3244040 | tf_op jit(solution)/shard_map/ppermute | solution.py:240
  45.5 5.5 %collective-permute-start.9 = (bf16[128,4224]{1,0:T(8,128)(2,1)}, bf16[128,4224]{1,0:T(8,128)(2,1)S(1)}, u32[]{:S(2)}, u32[]{:S(2)}) collective-permute-start(bf16[128,4224]{1,0:T(8,128)(2,1)} %collective-permute-done.5.refs_1_.refs_6_.refs_10_.refs_4_), channel_id=1, source_target_pairs={{0,1},{1,0},{2,3},{3,2},{4,5},{5,4},{6,7},{7,6},{8,9},{9,8},{10,11... | collective-permute-start | bytes 3244040 | tf_op jit(solution)/shard_map/ppermute | solution.py:240
  58.7 13.0 %collective-permute-start.11 = (bf16[3,128,768]{2,1,0:T(8,128)(2,1)S(1)}, bf16[3,128,768]{2,1,0:T(8,128)(2,1)S(1)}, u32[]{:S(2)}, u32[]{:S(2)}) collective-permute-start(bf16[3,128,768]{2,1,0:T(8,128)(2,1)S(1)} %bitcast.55), channel_id=1, source_target_pairs={{0,32},{1,97},{32,64},{33,1},{64,96},{65,33},{96,0},{97,65},{2,34}... | collective-permute-start | bytes 1769480 | tf_op jit(solution)/shard_map/ppermute | solution.py:259
  60.3 19.0 %collective-permute-start.10 = (bf16[3,128,768]{2,1,0:T(8,128)(2,1)S(1)}, bf16[3,128,768]{2,1,0:T(8,128)(2,1)S(1)}, u32[]{:S(2)}, u32[]{:S(2)}) collective-permute-start(bf16[3,128,768]{2,1,0:T(8,128)(2,1)S(1)} %bitcast.54), channel_id=1, source_target_pairs={{0,32},{1,97},{32,64},{33,1},{64,96},{65,33},{96,0},{97,65},{2,34}... | collective-permute-start | bytes 1769480 | tf_op jit(solution)/shard_map/ppermute | solution.py:259
  70.4 15.6 %collective-permute-start.13 = (bf16[256,2176]{1,0:T(8,128)(2,1)S(1)}, bf16[256,2176]{1,0:T(8,128)(2,1)S(1)}, u32[]{:S(2)}, u32[]{:S(2)}) collective-permute-start(bf16[256,2176]{1,0:T(8,128)(2,1)S(1)} %get-tuple-element.51), channel_id=1, source_target_pairs={{0,8},{1,25},{8,0},{9,17},{16,24},{17,9},{24,16},{25,1},{2,10},{3,... | collective-permute-start | bytes 3342344 | tf_op jit(solution)/shard_map/ppermute | solution.py:282
  71.9 11.2 %collective-permute-start.12 = (bf16[3,128,768]{2,1,0:T(8,128)(2,1)S(1)}, bf16[3,128,768]{2,1,0:T(8,128)(2,1)S(1)}, u32[]{:S(2)}, u32[]{:S(2)}) collective-permute-start(bf16[3,128,768]{2,1,0:T(8,128)(2,1)S(1)} %fusion.4), channel_id=1, source_target_pairs={{0,32},{1,97},{32,64},{33,1},{64,96},{65,33},{96,0},{97,65},{2,34}... | collective-permute-start | bytes 1769480 | tf_op jit(solution)/shard_map/ppermute | solution.py:259
  78.3 1.0 copy-start.2
  79.3 4.7 %copy-start = (bf16[2,3,128,768]{3,2,1,0:T(8,128)(2,1)}, bf16[2,3,128,768]{3,2,1,0:T(8,128)(2,1)S(1)}, u32[]{:S(2)}) copy-start(bf16[2,3,128,768]{3,2,1,0:T(8,128)(2,1)S(1)} %get-tuple-element.49) | copy-start | bytes 3538948
  79.5 11.8 %collective-permute-start.18 = (bf16[3,128,768]{2,1,0:T(8,128)(2,1)S(1)}, bf16[3,128,768]{2,1,0:T(8,128)(2,1)}, u32[]{:S(2)}, u32[]{:S(2)}) collective-permute-start(bf16[3,128,768]{2,1,0:T(8,128)(2,1)S(1)} %fusion), channel_id=1, source_target_pairs={{0,32},{1,97},{32,64},{33,1},{64,96},{65,33},{96,0},{97,65},{2,34}... | collective-permute-start | bytes 1769480 | tf_op jit(solution)/shard_map/ppermute | solution.py:259
  86.0 2.8 %copy-start.1 = (bf16[2,3,128,768]{3,2,1,0:T(8,128)(2,1)S(1)}, bf16[2,3,128,768]{3,2,1,0:T(8,128)(2,1)}, u32[]{:S(2)}) copy-start(bf16[2,3,128,768]{3,2,1,0:T(8,128)(2,1)} %copy-done) | copy-start | bytes 3538948
  86.3 1.0 copy-start.4
  87.3 4.0 %copy-start.3 = (bf16[2,3,128,768]{3,2,1,0:T(8,128)(2,1)S(1)}, bf16[2,3,128,768]{3,2,1,0:T(8,128)(2,1)}, u32[]{:S(2)}) copy-start(bf16[2,3,128,768]{3,2,1,0:T(8,128)(2,1)} %copy-done.2) | copy-start | bytes 3538948
  88.1 4.4 %collective-permute-start.14 = (bf16[128,2176]{1,0:T(8,128)(2,1)}, bf16[128,2176]{1,0:T(8,128)(2,1)}, u32[]{:S(2)}, u32[]{:S(2)}) collective-permute-start(bf16[128,2176]{1,0:T(8,128)(2,1)} %slice.54), channel_id=1, source_target_pairs={{0,1},{1,0},{2,3},{3,2},{4,5},{5,4},{6,7},{7,6},{8,9},{9,8},{10,11... | collective-permute-start | bytes 1671176 | tf_op jit(solution)/shard_map/ppermute | solution.py:286
  88.8 3.7 %copy-start.5 = (bf16[256,2176]{1,0:T(8,128)(2,1)S(1)}, bf16[256,2176]{1,0:T(8,128)(2,1)}, u32[]{:S(2)}) copy-start(bf16[256,2176]{1,0:T(8,128)(2,1)} %copy-done.4) | copy-start | bytes 3342340
  88.8 10.0 %collective-permute-start.20 = (bf16[3,128,768]{2,1,0:T(8,128)(2,1)S(1)}, bf16[3,128,768]{2,1,0:T(8,128)(2,1)S(1)}, u32[]{:S(2)}, u32[]{:S(2)}) collective-permute-start(bf16[3,128,768]{2,1,0:T(8,128)(2,1)S(1)} %slice_bitcast_fusion), channel_id=1, source_target_pairs={{0,8},{1,25},{8,0},{9,17},{16,24},{17,9},{24,16},{25,1},{2,10},{3,... | collective-permute-start | bytes 1769480 | tf_op jit(solution)/shard_map/ppermute | solution.py:294
  89.5 16.2 %collective-permute-start.21 = (bf16[3,128,768]{2,1,0:T(8,128)(2,1)}, bf16[3,128,768]{2,1,0:T(8,128)(2,1)S(1)}, u32[]{:S(2)}, u32[]{:S(2)}) collective-permute-start(bf16[3,128,768]{2,1,0:T(8,128)(2,1)} %fusion.3), channel_id=1, source_target_pairs={{0,40},{1,121},{8,32},{9,113},{16,56},{17,105},{24,48},{25,97},{32... | collective-permute-start | bytes 1769480 | tf_op jit(solution)/shard_map/ppermute | solution.py:295
  92.5 17.5 %collective-permute-start.19 = (bf16[3,128,768]{2,1,0:T(8,128)(2,1)S(1)}, bf16[3,128,768]{2,1,0:T(8,128)(2,1)S(1)}, u32[]{:S(2)}, u32[]{:S(2)}) collective-permute-start(bf16[3,128,768]{2,1,0:T(8,128)(2,1)S(1)} %fusion.1), channel_id=1, source_target_pairs={{0,32},{1,97},{32,64},{33,1},{64,96},{65,33},{96,0},{97,65},{2,34}... | collective-permute-start | bytes 1769480 | tf_op jit(solution)/shard_map/ppermute | solution.py:259
  93.8 18.9 %collective-permute-start.17 = (bf16[32,2176]{1,0:T(8,128)(2,1)S(1)}, bf16[32,2176]{1,0:T(8,128)(2,1)S(1)}, u32[]{:S(2)}, u32[]{:S(2)}) collective-permute-start(bf16[32,2176]{1,0:T(8,128)(2,1)S(1)} %get-tuple-element.66), channel_id=1, source_target_pairs={{0,4},{2,6},{4,0},{6,2},{1,5},{3,7},{5,1},{7,3},{8,12},{10,14},{12... | collective-permute-start | bytes 417800 | tf_op jit(solution)/shard_map/ppermute | solution.py:290
  97.0 15.7 %collective-permute-start.16 = (bf16[32,2176]{1,0:T(8,128)(2,1)S(1)}, bf16[32,2176]{1,0:T(8,128)(2,1)S(1)}, u32[]{:S(2)}, u32[]{:S(2)}) collective-permute-start(bf16[32,2176]{1,0:T(8,128)(2,1)S(1)} %get-tuple-element.67), channel_id=1, source_target_pairs={{0,6},{2,4},{4,2},{6,0},{1,7},{3,5},{5,3},{7,1},{8,14},{10,12},{12... | collective-permute-start | bytes 417800 | tf_op jit(solution)/shard_map/ppermute | solution.py:290
  98.8 13.9 %collective-permute-start.15 = (bf16[32,2176]{1,0:T(8,128)(2,1)S(1)}, bf16[32,2176]{1,0:T(8,128)(2,1)S(1)}, u32[]{:S(2)}, u32[]{:S(2)}) collective-permute-start(bf16[32,2176]{1,0:T(8,128)(2,1)S(1)} %get-tuple-element.65), channel_id=1, source_target_pairs={{0,2},{2,0},{4,6},{6,4},{1,3},{3,1},{5,7},{7,5},{8,10},{10,8},{12,... | collective-permute-start | bytes 417800 | tf_op jit(solution)/shard_map/ppermute | solution.py:290
  110.5 3.0 %copy-start.8 = (s32[32,8]{0,1:T(8,128)S(1)}, s32[32,8]{0,1:T(8,128)}, u32[]{:S(2)}) copy-start(s32[32,8]{0,1:T(8,128)} %param.8) | copy-start | bytes 3076
